TPU v7x, 256 devices: a whole 4x4x8 slice. The times are simulated.
256 devices in a mesh: dp: 4 (over y_hi, core), mp: 64 (over y_lo, x, z).
Axes of the slice: x: 4, y: 4 (y_hi: 2, y_lo: 2; y = y_hi * 2 + y_lo), z: 8, core: 2. Of those that a mesh axis runs over, the one named last changes fastest.
Arguments:
- patches: bfloat16 [1024, 6144], P('dp', 'mp'), may hold values from -110 to 110, as said below
- proj_in: bfloat16 [6144, 24576], P(None, 'mp'), may hold values from -0.21875 to 0.21875
- proj_out: bfloat16 [24576, 6144], P('mp'), may hold values from -0.109375 to 0.109375
- cotangent: bfloat16 [1024, 6144], P('dp', 'mp'), may hold values from -6 to 6
Outputs:
- mlp_out: bfloat16 [1024, 6144], P('dp', 'mp')
- patch_grad: bfloat16 [1024, 6144], P('dp', 'mp')
- grad_in: bfloat16 [6144, 24576], P('dp', 'mp')
- grad_out: bfloat16 [24576, 6144], P('mp', 'dp')
Inputs may be any that keep to these rules, and one draw needn't show every extreme that they name: `patches`: Real-valued activations whose rows and features have differing scales.
All inputs are finite; a program needn't handle non-finite values.
Results may differ from a plain program's by a relative error of at most 0.012.
Values may be sent and summed in bfloat16 or wider, within the bound.
No kernel may reach another device: no remote copies, remote signals or barrier semaphores. Data moves between devices by JAX's collectives and lax.ppermute only.
A program may use at most 192 MiB of HBM per device.

v0:
```python
import jax
import jax.numpy as jnp
from jax import lax
from jax.sharding import PartitionSpec as P

eps = 1e-06


def gelu_back(hidden_pre, grad_act):
    return jax.vjp(lambda values: jax.nn.gelu(values, approximate=True), hidden_pre)[1](grad_act)[0]


def rounded(values):
    low = lax.optimization_barrier(values.astype(jnp.bfloat16))
    return low.astype(jnp.float32)


def row_sums(first, second):
    return lax.psum((first, second), "mp")


def fold_rows(local, contract):
    piece = lax.all_gather(local, "mp", axis=1, tiled=True)
    return (contract(piece, jnp.int32(0)), piece)


def scatter_cols(term_fn, rows):
    return lax.psum_scatter(
        term_fn(jnp.int32(0), lax.axis_size("mp") * rows), "mp", scatter_dimension=0, tiled=True
    )


def per_device(patches, proj_in, proj_out, cotangent):
    own_cols = patches.shape[1]
    width = own_cols * lax.axis_size("mp")

    def contract_in(piece, start):
        return jnp.dot(piece, proj_in, preferred_element_type=jnp.float32)

    wide_x = patches.astype(jnp.float32)
    sum_first, sum_second = row_sums(jnp.sum(wide_x, axis=1), jnp.sum(wide_x * wide_x, axis=1))
    row_mean = (sum_first / width)[:, None]
    row_var = (sum_second / width)[:, None] - row_mean * row_mean
    row_rstd = lax.rsqrt(row_var + eps)
    normed = (wide_x - row_mean) * row_rstd
    hidden_pre, normed_full = fold_rows(normed.astype(jnp.bfloat16), contract_in)
    activated = jax.nn.gelu(hidden_pre, approximate=True).astype(jnp.bfloat16)

    def out_term(start, count):
        return lax.dot_general(
            proj_out, activated, (((0,), (1,)), ((), ())), preferred_element_type=jnp.float32
        )

    def contract_back(piece, start):
        return lax.dot_general(
            piece, proj_out, (((1,), (1,)), ((), ())), preferred_element_type=jnp.float32
        )

    mlp_out = scatter_cols(out_term, own_cols).T.astype(jnp.bfloat16)
    grad_act, cot_full = fold_rows(cotangent, contract_back)
    grad_pre = gelu_back(hidden_pre, grad_act).astype(jnp.bfloat16)

    def norm_term(start, count):
        return lax.dot_general(
            proj_in, grad_pre, (((1,), (1,)), ((), ())), preferred_element_type=jnp.float32
        )

    grad_norm = scatter_cols(norm_term, own_cols).T
    sum_grad, sum_cross = row_sums(jnp.sum(grad_norm, axis=1), jnp.sum(grad_norm * normed, axis=1))
    mean_grad = (sum_grad / width)[:, None]
    mean_cross = (sum_cross / width)[:, None]
    patch_grad = (row_rstd * (grad_norm - mean_grad - normed * mean_cross)).astype(jnp.bfloat16)
    part_in = rounded(
        lax.dot_general(
            normed_full, grad_pre, (((0,), (0,)), ((), ())), preferred_element_type=jnp.float32
        )
    )
    part_out = rounded(
        lax.dot_general(
            activated, cot_full, (((0,), (0,)), ((), ())), preferred_element_type=jnp.float32
        )
    )
    total_in, total_out = (
        lax.psum_scatter(
            part_in.astype(jnp.bfloat16), "dp", scatter_dimension=0, tiled=True
        ).astype(jnp.float32),
        lax.psum_scatter(
            part_out.astype(jnp.bfloat16), "dp", scatter_dimension=1, tiled=True
        ).astype(jnp.float32),
    )
    return (mlp_out, patch_grad, total_in.astype(jnp.bfloat16), total_out.astype(jnp.bfloat16))


def solution(mesh):
    in_specs = (P("dp", "mp"), P(None, "mp"), P("mp", None), P("dp", "mp"))
    out_specs = (P("dp", "mp"), P("dp", "mp"), P("dp", "mp"), P("mp", "dp"))
    return jax.shard_map(
        per_device, mesh=mesh, in_specs=in_specs, out_specs=out_specs, check_vma=False
    )
```

profile of v0, /device:TPU:24, one launch (start us, length us, event | category | flops | bytes accessed | tf_op | source)
XLA Modules:
  0.0 1448.9 jit_solution(2879326693230728401)
XLA Ops:
  7.2 0.0 all-gather.5.cloned.1.call-start
  7.2 0.7 all-gather.5.cloned.1.call-update
  7.9 0.0 all-gather.3.cloned.1.call-start
  7.9 0.8 convert_reduce_fusion
  8.8 160.6 %all-reduce.1 = (f32[256]{0:T(256)S(1)}, f32[256]{0:T(256)S(1)}) all-reduce(f32[256]{0:T(256)S(1)} %get-tuple-element.13, f32[256]{0:T(256)S(1)} %get-tuple-element.12), channel_id=1, replica_groups=mesh['dp'=4,'mp'=64] {'mp'}, use_global_device_ids=true, to_apply=%region_3.0 | all-reduce | flops 512 | bytes 4096 | tf_op jit(solution)/shard_map/psum | solution.py:19
  169.4 1.4 fusion.10
  170.9 0.0 all-gather.3.cloned.1.call-update
  170.9 0.0 reduce-scatter.13.cloned.1.call-start
  170.9 143.3 %all-gather.5.cloned.1.call-done = bf16[256,6144]{0,1:T(8,128)(2,1)} async-done(((bf16[256,96]{0,1:T(8,128)(2,1)}), bf16[256,6144]{0,1:T(8,128)(2,1)}) %all-gather.5.cloned.1.call-update) | async-done | bytes 3145744 | tf_op jit(solution)/shard_map/all_gather | solution.py:23
  314.2 5.1 fusion.16
  319.4 297.0 %all-gather.3.cloned.1.call-done = bf16[256,6144]{0,1:T(8,128)(2,1)} async-done(((bf16[256,96]{0,1:T(8,128)(2,1)}), bf16[256,6144]{0,1:T(8,128)(2,1)}) %all-gather.3.cloned.1.call-update) | async-done | bytes 3145744 | tf_op jit(solution)/shard_map/all_gather | solution.py:23
  616.4 5.3 fusion.6
  621.7 0.0 copy-start.2
  621.7 6.9 convolution_bitcast_fusion.1
  628.6 6.6 copy.13
  635.2 0.0 reduce-scatter.13.cloned.1.call-update
  635.3 0.0 reduce-scatter.15.cloned.1.call-start
  635.3 0.0 copy-done.2
  635.3 6.8 convolution_bitcast_fusion
  642.1 6.5 copy.15
  648.6 0.0 copy-start
  648.6 0.0 reduce-scatter.15.cloned.1.call-update
  648.7 0.0 reduce-scatter.9.cloned.1.call-start
  648.7 1.8 copy-done
  650.5 4.8 convolution_convert_fusion.1
  655.4 0.0 copy-start.1
  655.4 0.0 reduce-scatter.9.cloned.1.call-update
  655.4 0.0 reduce-scatter.11.cloned.1.call-start
  655.4 1.8 copy-done.1
  657.3 3.6 convolution_convert_fusion
  660.9 0.0 copy-start.3
  660.9 0.0 reduce-scatter.11.cloned.1.call-update
  660.9 299.3 %reduce-scatter.13.cloned.1.call-done = f32[96,256]{1,0:T(8,128)} async-done(((f32[6144,256]{1,0:T(8,128)}), f32[96,256]{1,0:T(8,128)}) %reduce-scatter.13.cloned.1.call-update) | async-done | bytes 98320
  960.3 1.0 copy.14
  961.3 0.7 copy.12
  962.0 321.5 %reduce-scatter.15.cloned.1.call-done = f32[96,256]{1,0:T(8,128)} async-done(((f32[6144,256]{1,0:T(8,128)}), f32[96,256]{1,0:T(8,128)}) %reduce-scatter.15.cloned.1.call-update) | async-done | bytes 98320 | tf_op jit(solution)/shard_map/reduce_scatter | solution.py:28
  1283.4 0.9 reduce_sum.38
  1284.4 0.0 copy-done.3
  1284.4 0.9 fusion.11
  1285.3 155.2 %all-reduce = (f32[256]{0:T(256)S(1)}, f32[256]{0:T(256)S(1)}) all-reduce(f32[256]{0:T(256)S(1)} %fusion.11, f32[256]{0:T(256)S(1)} %reduce_sum.38), channel_id=1, replica_groups=mesh['dp'=4,'mp'=64] {'mp'}, use_global_device_ids=true, to_apply=%region_9.0 | all-reduce | flops 512 | bytes 4096 | tf_op jit(solution)/shard_map/psum | solution.py:19
  1440.5 1.5 fusion.14
  1442.0 0.0 reduce-scatter.9.cloned.1.call-done
  1442.0 0.0 reduce-scatter.11.cloned.1.call-done
  (2 shorter events, 0.0 us)
Async XLA Ops:
  7.2 307.1 %all-gather.5.cloned.1.call-start = ((), (), s32[]{:S(2)}) async-start(), calls=%async_computation.5 | async-start | bytes 3194880 | tf_op jit(solution)/shard_map/all_gather | solution.py:23
  7.9 608.5 %all-gather.3.cloned.1.call-start = ((), (), s32[]{:S(2)}) async-start(), calls=%async_computation.4 | async-start | bytes 3194880 | tf_op jit(solution)/shard_map/all_gather | solution.py:23
  170.9 789.4 %reduce-scatter.13.cloned.1.call-start = ((), (), s32[]{:S(2)}) async-start(), calls=%async_computation.8 | async-start | bytes 6389760
  621.7 13.6 copy-start.2
  635.3 648.2 %reduce-scatter.15.cloned.1.call-start = ((), (), s32[]{:S(2)}) async-start(), calls=%async_computation.9 | async-start | bytes 6389760 | tf_op jit(solution)/shard_map/reduce_scatter | solution.py:28
  648.6 1.9 copy-start
  648.7 793.4 %reduce-scatter.9.cloned.1.call-start = ((), (), s32[]{:S(2)}) async-start(), calls=%async_computation.6 | async-start | bytes 5898240 | tf_op jit(solution)/shard_map/reduce_scatter | solution.py:84
  655.4 1.9 copy-start.1
  655.4 786.7 %reduce-scatter.11.cloned.1.call-start = ((), (), s32[]{:S(2)}) async-start(), calls=%async_computation.7 | async-start | bytes 5898240 | tf_op jit(solution)/shard_map/reduce_scatter | solution.py:87
  660.9 623.5 %copy-start.3 = (bf16[256,96]{0,1:T(8,128)(2,1)S(1)}, bf16[256,96]{0,1:T(8,128)(2,1)}, u32[]{:S(2)}) copy-start(bf16[256,96]{0,1:T(8,128)(2,1)} %param.4) | copy-start | bytes 147460
Sparse Core Ops, SparseCore 0:
  9.8 304.4 all-gather.4
  316.6 299.7 all-gather.2
  635.4 324.8 reduce-scatter.12
  962.8 320.5 reduce-scatter.14
  1286.7 53.5 reduce-scatter.8
  1343.7 58.9 reduce-scatter.10
where the time goes:
time: 1450 us
  waiting for transfers between devices  1060 us (73%)
  blocking collectives  316 us (22%)
  matrix products  32.6 us (2%)
  local copies, waits for them, and re-layouts  18.5 us (1%)
    all_gather x2, waiting for transfers between devices, fold_rows(): piece = lax.all_gather(local, 'mp', axis=1, tiled=True)  440 us
    reduce_scatter x1, waiting for transfers between devices, scatter_cols(): lax.psum_scatter(term_fn(jnp.int32(0), lax.axis_size('mp') * rows), 'mp',...  321 us
    psum x2, blocking collectives, row_sums(): return lax.psum((first, second), 'mp')  316 us
    unnamed x7, waiting for transfers between devices  300 us
  transfers between devices with their start and end apart: 6, of which 4 were waited for; matrix products, arithmetic and copies ran while one was open for 2% of the time, Pallas kernels for 0%

commit v1 on v0

v1 whole, which is shorter than its diff:
```python
import math

import jax
import jax.numpy as jnp
import numpy as np
from jax import lax
from jax.experimental import pallas as pl
from jax.experimental.pallas import tpu as pltpu
from jax.sharding import Mesh, PartitionSpec as P

eps = 1e-06
AXES = ("yh", "core", "yl", "x", "z")
SIZE = {"yh": 2, "core": 2, "yl": 2, "x": 4, "z": 8}
low = jnp.bfloat16
wide = jnp.float32
TOK, OWN, HID, WIDTH = 256, 96, 384, 6144
HALF, BLOCK, QUARTER = WIDTH // 2, WIDTH // 8, WIDTH // 4
root = math.sqrt(2.0 / math.pi)
work = 2 * TOK * WIDTH * HID


def shift(values, axis, step):
    count = SIZE[axis]
    return lax.ppermute(values, axis, [(i, (i + step) % count) for i in range(count)])


def dot(first, second, one, two):
    return lax.dot_general(first, second, (((one,), (two,)), ((), ())), preferred_element_type=wide)


def whole(shape):
    return pl.BlockSpec(shape, lambda t, me: (0,) * len(shape))


def call(body, steps, scalars, ins, outs, scratch=(), after=(), flops=work):
    count = 1 + len(ins)

    def run(*refs):
        body(*refs[:count], *refs[count + len(after) :])

    shapes = [jax.ShapeDtypeStruct(shape, kind) for shape, kind, _ in outs]
    moved = sum(math.prod(v.shape) * v.dtype.itemsize for v in [*(a for a, _ in ins), *shapes])
    return pl.pallas_call(
        run,
        out_shape=shapes,
        grid_spec=pltpu.PrefetchScalarGridSpec(
            num_scalar_prefetch=1,
            grid=(steps,),
            in_specs=[spec for _, spec in ins] + [pl.BlockSpec(memory_space=pl.ANY) for _ in after],
            out_specs=[spec for _, _, spec in outs],
            scratch_shapes=list(scratch),
        ),
        compiler_params=pltpu.CompilerParams(vmem_limit_bytes=24 << 20),
        cost_estimate=pl.CostEstimate(flops=flops, bytes_accessed=moved, transcendentals=0),
    )(scalars, *(a for a, _ in ins), *after)


def block_at(me, k, yl):
    return yl * 4 + ((me[0] - k) & 3)


def rows_of(block):
    return pl.ds(pl.multiple_of(block * BLOCK, BLOCK), BLOCK)


def gelu_parts(hidden):
    square = hidden * hidden
    tanh = jnp.tanh(root * (hidden + 0.044715 * hidden * square))
    half = 0.5 * (1.0 + tanh)
    slope = half + 0.5 * hidden * (1.0 - tanh * tanh) * (root * (1.0 + 3 * 0.044715 * square))
    return hidden * half, slope


def main_body(me, p0, p1, p2, p3, mean, rstd, col_sum, w_in, w_out, part, *refs):
    mlp_outs, (patch, mine, other, away_mine, away_other) = refs[:4], refs[4:9]
    p_near, in_near, out_near, cot, norm, mlp_stage, patch_stage, grad_stage, acc, grad_acc = refs[9:19]
    p_sem, in_sem, out_sem, cot_sem, mlp_sem, patch_sem, grad_sem = refs[19:]

    def p_copy(t, piece, yl):
        return pltpu.make_async_copy(piece.at[yl], p_near.at[t], p_sem.at[t])

    def in_copy(t):
        return pltpu.make_async_copy(w_in.at[rows_of(block_at(me, t // 2, t % 2))], in_near.at[t], in_sem.at[t])

    def out_copy(j):
        return pltpu.make_async_copy(w_out.at[:, rows_of(j)], out_near.at[j], out_sem.at[j])

    def cot_copy(j):
        return pltpu.make_async_copy(part.at[:, (me[0] - (j % 4)) & 3, j // 4], cot.at[j], cot_sem.at[j])

    for t in range(8):
        p_copy(t, (p0, p1, p2, p3)[t // 2], t % 2).start()
        in_copy(t).start()
    for j in range(8):
        out_copy(j).start()
        cot_copy(j).start()
    acc[...] = jnp.zeros_like(acc)
    grad_acc[...] = jnp.zeros_like(grad_acc)

    def hidden_step(t, _):
        p_copy(t, p0, 0).wait()
        value = ((p_near[t].astype(wide) - mean[...]) * rstd[...]).astype(low)
        norm[block_at(me, t // 2, t % 2)] = value
        in_copy(t).wait()
        acc[...] += dot(value, in_near[t], 0, 0)
        return 0

    lax.fori_loop(0, 8, hidden_step, 0)

    def grad_step(j, _):
        out_copy(j).wait()
        cot_copy(j).wait()
        grad_acc[...] += dot(out_near[j], cot[j].reshape(BLOCK, TOK), 1, 0)
        return 0

    lax.fori_loop(0, 8, grad_step, 0)

    hidden = acc[...].T
    act_wide, slope = gelu_parts(hidden)
    act_t = act_wide.astype(low)
    act = act_wide.T.astype(low)
    grad_wide = slope * grad_acc[...]
    grad_t = grad_wide.astype(low)
    grad = grad_wide.T.astype(low)
    rounded = grad_t.astype(wide)
    first = jnp.sum(rounded * col_sum[...].T, axis=0, keepdims=True) / WIDTH
    second = jnp.sum(rounded * hidden, axis=0, keepdims=True) / WIDTH

    grad_to = (away_other, away_mine, other, mine)

    def grad_copy(q):
        return pltpu.make_async_copy(grad_stage.at[q], grad_to[q], grad_sem.at[q])

    for q in range(4):
        yh = me[3] if q in (1, 3) else 1 - me[3]
        core = 1 - me[4] if q < 2 else me[4]
        blocks = pl.ds((yh * 2 + core) * 2, 2)
        grad_stage[q, :QUARTER] = dot(norm[blocks].reshape(QUARTER, TOK), grad, 1, 0).astype(low)
        value = dot(act_t, cot[blocks].reshape(QUARTER, TOK), 1, 1).astype(low)
        for i in range(4):
            grad_stage[q, QUARTER + i * HID : QUARTER + (i + 1) * HID] = value[:, i * HID : (i + 1) * HID]
        grad_copy(q).start()

    def patch_copy(t):
        to = patch.at[:, t % 2, (me[0] - t // 2) & 3]
        return pltpu.make_async_copy(patch_stage.at[t], to, patch_sem.at[t])

    def patch_step(t, _):
        share = dot(in_near[t], grad_t, 1, 0)
        normed = (p_near[t].astype(wide) - mean[...]) * rstd[...]
        share = rstd[...] * (share - first - normed * second)
        patch_stage[t] = share.astype(low).reshape(8, OWN, TOK)
        patch_copy(t).start()
        return 0

    lax.fori_loop(0, 8, patch_step, 0)

    def mlp_copy(t):
        return pltpu.make_async_copy(mlp_stage.at[t], mlp_outs[t // 2].at[t % 2], mlp_sem.at[t])

    for t in range(8):
        mlp_stage[t] = dot(act, out_near[(t % 2) * 4 + ((me[0] + t // 2) & 3)], 1, 0).astype(low)
        mlp_copy(t).start()
    for t in range(8):
        patch_copy(t).wait()
        mlp_copy(t).wait()
    for q in range(4):
        grad_copy(q).wait()


def send_body(me, other, got, out):
    out[...] = (other[...].astype(wide) + got[...].astype(wide)).astype(low)


def final_body(me, mine, got, back, out):
    out[...] = (mine[...].astype(wide) + got[...].astype(wide) + back[...].astype(wide)).astype(low)


def sum_body(me, r0, r1, r2, r3, keep, away, total):
    value = r0[0].astype(wide) + r1[0].astype(wide) + r2[0].astype(wide) + r3[0].astype(wide)
    total[...] = value.T
    for d in range(4):
        pair = ((me[1] // 2 + d) & 3) * 2
        same = pl.ds(pl.multiple_of((pair + (me[1] & 1)) * OWN, 8), OWN)
        flip = pl.ds(pl.multiple_of((pair + 1 - (me[1] & 1)) * OWN, 8), OWN)
        keep[d, 0] = total[same, :]
        away[d, 0] = total[flip, :].astype(low)


def ring_z(block, near, me):
    up, down = near
    parts = {0: block, 1: up, 7: down}
    for step in (2, 3):
        up, down = shift(up, "z", 1), shift(down, "z", -1)
        parts[step], parts[8 - step] = up, down
    half = OWN // 2
    parts[4] = jnp.concatenate([shift(up[:, :half], "z", 1), shift(down[:, half:], "z", -1)], axis=1)
    buffer = jnp.zeros((2, 8, OWN, TOK), low)
    for k, part in parts.items():
        buffer = lax.dynamic_update_slice_in_dim(buffer, part[:, None], (me - k) & 7, 1)
    return buffer.reshape(2, BLOCK, TOK)


def last_step(total, my_yl):
    mine = jnp.where(my_yl == 0, total[0], total[1])
    other = jnp.where(my_yl == 0, total[1], total[0])
    return (mine + shift(other.astype(low), "yl", 1).astype(wide)).astype(low).T


def per_device(patches, proj_in, proj_out, cotangent):
    me = {axis: lax.axis_index(axis) for axis in AXES}
    scalars = jnp.stack([me["x"], me["z"], me["yl"], me["yh"], me["core"]]).astype(jnp.int32)

    both = jnp.concatenate([patches.T, cotangent.T], axis=0)
    near = shift(both, "yl", 1)
    pair = jnp.where(me["yl"] == 0, jnp.stack([both, near]), jnp.stack([near, both]))
    x_pair, c_pair = pair[:, :OWN], pair[:, OWN:]

    z_near = [shift(x_pair, "z", 1), shift(x_pair, "z", -1)]
    c_pair = jnp.where(me["z"] > 7, z_near[0], c_pair)
    c_parts = [c_pair] + [shift(c_pair, "x", k) for k in range(1, 4)]
    c_x = jnp.concatenate(c_parts, axis=0)
    c_all = lax.all_gather(c_x.reshape(8 * OWN, TOK), "z", axis=0, tiled=True).reshape(8, 4, 2, OWN, TOK)
    x_z = ring_z(x_pair, z_near, me["z"])
    x_all = [x_z] + [shift(x_z, "x", k) for k in range(1, 4)]

    total = sum(jnp.sum(part.astype(wide), axis=(0, 1)) for part in x_all)
    squares = sum(jnp.sum(part.astype(wide) * part.astype(wide), axis=(0, 1)) for part in x_all)
    mean = (total / WIDTH)[None]
    rstd = lax.rsqrt((squares / WIDTH)[None] - mean * mean + eps)
    col_sum = jnp.sum(proj_in.astype(wide), axis=0, keepdims=True)

    dma = pltpu.SemaphoreType.DMA
    near, far = pl.BlockSpec(memory_space=pltpu.VMEM), pl.BlockSpec(memory_space=pl.ANY)
    both_rows = 2 * QUARTER
    shapes = [(2, TOK, BLOCK)] * 4 + [(8, 2, 4, OWN, TOK), *[(both_rows, HID)] * 4]
    *mlp_parts, patch_parts, mine, other, away_mine, away_other = pl.pallas_call(
        main_body,
        out_shape=[jax.ShapeDtypeStruct(shape, low) for shape in shapes],
        in_specs=[pl.BlockSpec(memory_space=pltpu.SMEM)] + [far] * 4 + [near] * 3 + [far] * 3,
        out_specs=[far] * len(shapes),
        scratch_shapes=[
            pltpu.VMEM((8, BLOCK, TOK), low),
            pltpu.VMEM((8, BLOCK, HID), low),
            pltpu.VMEM((8, HID, BLOCK), low),
            pltpu.VMEM((8, 8, OWN, TOK), low),
            pltpu.VMEM((8, BLOCK, TOK), low),
            pltpu.VMEM((8, TOK, BLOCK), low),
            pltpu.VMEM((8, 8, OWN, TOK), low),
            pltpu.VMEM((4, both_rows, HID), low),
            pltpu.VMEM((TOK, HID), wide),
            pltpu.VMEM((HID, TOK), wide),
        ]
        + [dma((8,))] * 6
        + [dma((4,))],
        compiler_params=pltpu.CompilerParams(vmem_limit_bytes=60 << 20),
        cost_estimate=pl.CostEstimate(flops=6 * work, bytes_accessed=31 << 20, transcendentals=0),
    )(scalars, *x_all, mean, rstd, col_sum, proj_in, proj_out, c_all)

    got_other = shift(away_other, "core", 1)
    got_mine = shift(away_mine, "core", 1)
    backs, halves = [], []
    for half in range(2):
        rows = pl.BlockSpec((HID, HID), lambda t, me, half=half: (4 * half + t, 0))
        (send,) = call(
            send_body,
            4,
            scalars,
            [(other, rows), (got_other, rows)],
            [((QUARTER, HID), low, pl.BlockSpec((HID, HID), lambda t, me: (t, 0)))],
        )
        backs.append(shift(send, "yh", 1))
        halves.append(rows)

    mlp_got = [mlp_parts[0]] + [shift(mlp_parts[k], "x", k) for k in range(1, 4)]
    keep, flip = call(
        sum_body,
        2,
        scalars,
        [(part, pl.BlockSpec((1, TOK, BLOCK), lambda t, me: (t, 0, 0))) for part in mlp_got],
        [((4, 2, OWN, TOK), kind, pl.BlockSpec((4, 1, OWN, TOK), lambda t, me: (0, t, 0, 0))) for kind in (wide, low)],
        [pltpu.VMEM((BLOCK, TOK), wide)],
        after=[backs[0]],
    )
    keep = keep + lax.ppermute(flip, "z", [(i, i ^ 1) for i in range(8)]).astype(wide)
    total = keep[0]
    for d in range(1, 4):
        total = total + shift(keep[d].astype(low), "z", 2 * d).astype(wide)
    mlp_out = last_step(total, me["yl"])

    part = lax.psum_scatter(patch_parts.reshape(WIDTH, TOK), "z", scatter_dimension=0, tiled=True)
    part = part.reshape(2, 4, OWN, TOK)
    total = lax.dynamic_index_in_dim(part, me["x"], 1, keepdims=False).astype(wide)
    for k in range(1, 4):
        away = lax.dynamic_index_in_dim(part, (me["x"] + k) & 3, 1, keepdims=False)
        total = total + shift(away, "x", k).astype(wide)
    patch_grad = last_step(total, me["yl"])

    own_rows = pl.BlockSpec((HID, HID), lambda t, me: (t, 0))
    own_cols = pl.BlockSpec((HID, HID), lambda t, me: (0, t))
    grad_in, grad_out = (
        call(
            final_body,
            4,
            scalars,
            [(mine, rows), (got_mine, rows), (back, own_rows)],
            [(shape, low, to)],
        )[0]
        for rows, back, shape, to in (
            (halves[0], backs[0], (QUARTER, HID), own_rows),
            (halves[1], backs[1], (HID, QUARTER), own_cols),
        )
    )
    return mlp_out, patch_grad, grad_in, grad_out


def solution(mesh):
    devices = np.asarray(mesh.devices).reshape([SIZE[axis] for axis in AXES])
    fine = Mesh(devices, AXES)
    dp, mp = ("yh", "core"), ("yl", "x", "z")
    in_specs = (P(dp, mp), P(None, mp), P(mp, None), P(dp, mp))
    out_specs = (P(dp, mp), P(dp, mp), P(dp, mp), P(mp, dp))
    return jax.shard_map(per_device, mesh=fine, in_specs=in_specs, out_specs=out_specs, check_vma=False)
```

time: 1450 us -> 207 us (0.14)
  waiting for transfers between devices: 1060 us -> 96.4 us
  blocking collectives: 316 us -> 0 us
  starting transfers between devices: 0.24 us -> 48.2 us
  matrix products: 32.6 us -> 0 us
  Pallas kernels: 0 us -> 32.2 us
    all_gather x2 -> x1, waiting for transfers between devices: 440 us -> 0.01 us  [per_device(): lax.all_gather(c_x.reshape(8 * OWN, TOK), 'z', axis=0, tiled=True)]
    reduce_scatter x3 -> x1, waiting for transfers between devices: 321 us -> 0.02 us  [per_device(): lax.psum_scatter(patch_parts.reshape(WIDTH, TOK), 'z', scatter_dimension=...]
    psum x2 -> x0, blocking collectives: 316 us -> none  [row_sums(): return lax.psum((first, second), 'mp')]
    unnamed x7 -> x2, waiting for transfers between devices: 300 us -> 0.03 us
    ppermute x0 -> x31, waiting for transfers between devices: none -> 96.3 us  [the longest x30 91.4 us: shift(): lax.ppermute(values, axis, [(i, (i + step) % count) for i in range(count)])]
    ppermute x0 -> x31, starting transfers between devices: none -> 48.1 us  [the longest x30 48.1 us: shift(): lax.ppermute(values, axis, [(i, (i + step) % count) for i in range(count)])]
    dot_general x6 -> x0, matrix products: 32.6 us -> none  [the longest x1 6.9 us: out_term(): lax.dot_general(proj_out, activated, (((0,), (1,)), ((), ())), preferred_...]
    pallas_call x0 -> x6, Pallas kernels: none -> 32.2 us  [the longest x1 18.7 us: per_device(): pl.pallas_call(main_body, out_shape=[jax.ShapeDtypeStruct(shape, low) for...]
  transfers between devices with their start and end apart: 6 -> 33, of which waited for: 4 -> 23; matrix products, arithmetic and copies ran while one was open for 2% -> 4% of each run, Pallas kernels for 0% -> 7%
where the time goes in v1:
time: 207 us; the launch traced here: 206 us
  waiting for transfers between devices  96.4 us (47%)
  starting transfers between devices  48.2 us (23%)
  Pallas kernels  32.2 us (16%)
  between operations  14.4 us (7%)
  other arithmetic  9.91 us (5%)
  local copies, waits for them, and re-layouts  4.69 us (2%)
    ppermute x30, waiting for transfers between devices, shift(): lax.ppermute(values, axis, [(i, (i + step) % count) for i in range(count)])  91.4 us
    ppermute x30, starting transfers between devices, shift(): lax.ppermute(values, axis, [(i, (i + step) % count) for i in range(count)])  48.1 us
    pallas_call x1, Pallas kernels, per_device(): pl.pallas_call(main_body, out_shape=[jax.ShapeDtypeStruct(shape, low) for...  18.7 us
    pallas_call x5, Pallas kernels, call(): pl.pallas_call(run, out_shape=shapes, grid_spec=pltpu.PrefetchScalarGridS...  13.5 us
    ppermute x1, waiting for transfers between devices, per_device(): lax.ppermute(flip, 'z', [(i, i ^ 1) for i in range(8)]).astype(wide)  4.89 us
  transfers between devices with their start and end apart: 33, of which 23 were waited for; matrix products, arithmetic and copies ran while one was open for 4% of the time, Pallas kernels for 7%

profile of v1, /device:TPU:24, one launch (start us, length us, event | category | flops | bytes accessed | tf_op | source)
XLA Modules:
  0.0 205.7 jit_solution(11639993933554240531)
XLA Ops:
  7.2 0.8 fusion.16
  8.1 0.8 collective-permute-start
  8.9 3.9 %collective-permute-done = bf16[192,256]{1,0:T(8,128)(2,1)S(1)} collective-permute-done((bf16[192,256]{1,0:T(8,128)(2,1)S(1)}, bf16[192,256]{1,0:T(8,128)(2,1)S(1)}, u32[]{:S(2)}, u32[]{:S(2)}) %collective-permute-start) | collective-permute-done | bytes 98336 | tf_op jit(solution)/shard_map/ppermute | solution.py:24
  12.8 2.0 collective-permute-start.1
  14.8 6.5 %collective-permute-done.1 = bf16[2,96,256]{2,1,0:T(8,128)(2,1)S(1)} collective-permute-done((bf16[2,96,256]{2,1,0:T(8,128)(2,1)S(1)}, bf16[2,96,256]{2,1,0:T(8,128)(2,1)S(1)}, u32[]{:S(2)}, u32[]{:S(2)}) %collective-permute-start.1) | collective-permute-done | bytes 98336 | tf_op jit(solution)/shard_map/ppermute | solution.py:24
  21.3 1.6 collective-permute-start.12
  22.9 2.7 %collective-permute-start.13 = (bf16[2,96,256]{2,1,0:T(8,128)(2,1)S(1)}, bf16[2,96,256]{2,1,0:T(8,128)(2,1)S(1)}, u32[]{:S(2)}, u32[]{:S(2)}) collective-permute-start(bf16[2,96,256]{2,1,0:T(8,128)(2,1)S(1)} %slice_select_fusion), channel_id=1, source_target_pairs={{0,16},{8,24},{16,0},{24,8},{1,17},{9,25},{17,1},{25,9},{2,18},{10... | collective-permute-start | bytes 294920 | tf_op jit(solution)/shard_map/ppermute | solution.py:24
  25.6 1.4 collective-permute-start.14
  27.2 2.0 collective-permute-done.13
  29.3 1.0 collective-permute-done.14
  30.3 0.8 pad_maximum_fusion
  31.1 2.1 %collective-permute-start.2 = (bf16[2,96,256]{2,1,0:T(8,128)(2,1)S(1)}, bf16[2,96,256]{2,1,0:T(8,128)(2,1)S(1)}, u32[]{:S(2)}, u32[]{:S(2)}) collective-permute-start(bf16[2,96,256]{2,1,0:T(8,128)(2,1)S(1)} %slice.55), channel_id=1, source_target_pairs={{0,7},{1,0},{2,1},{3,2},{4,3},{5,4},{6,5},{7,6},{8,15},{9,8},{10,9... | collective-permute-start | bytes 294920 | tf_op jit(solution)/shard_map/ppermute | solution.py:24
  33.4 2.8 %collective-permute-done.2 = bf16[2,96,256]{2,1,0:T(8,128)(2,1)S(1)} collective-permute-done((bf16[2,96,256]{2,1,0:T(8,128)(2,1)S(1)}, bf16[2,96,256]{2,1,0:T(8,128)(2,1)S(1)}, u32[]{:S(2)}, u32[]{:S(2)}) %collective-permute-start.2) | collective-permute-done | bytes 98336 | tf_op jit(solution)/shard_map/ppermute | solution.py:24
  36.3 3.7 %collective-permute-start.4 = (bf16[2,96,256]{2,1,0:T(8,128)(2,1)S(1)}, bf16[2,96,256]{2,1,0:T(8,128)(2,1)S(1)}, u32[]{:S(2)}, u32[]{:S(2)}) collective-permute-start(bf16[2,96,256]{2,1,0:T(8,128)(2,1)S(1)} %collective-permute-done.2), channel_id=1, source_target_pairs={{0,7},{1,0},{2,1},{3,2},{4,3},{5,4},{6,5},{7,6},{8,15},{9,8},{10,9... | collective-permute-start | bytes 294920 | tf_op jit(solution)/shard_map/ppermute | solution.py:24
  40.1 2.1 %collective-permute-done.4 = bf16[2,96,256]{2,1,0:T(8,128)(2,1)S(1)} collective-permute-done((bf16[2,96,256]{2,1,0:T(8,128)(2,1)S(1)}, bf16[2,96,256]{2,1,0:T(8,128)(2,1)S(1)}, u32[]{:S(2)}, u32[]{:S(2)}) %collective-permute-start.4) | collective-permute-done | bytes 98336 | tf_op jit(solution)/shard_map/ppermute | solution.py:24
  42.2 3.7 %collective-permute-start.6 = (bf16[2,96,256]{2,1,0:T(8,128)(2,1)S(1)}, bf16[2,96,256]{2,1,0:T(8,128)(2,1)S(1)}, u32[]{:S(2)}, u32[]{:S(2)}) collective-permute-start(bf16[2,96,256]{2,1,0:T(8,128)(2,1)S(1)} %collective-permute-done.4), channel_id=1, source_target_pairs={{0,7},{1,0},{2,1},{3,2},{4,3},{5,4},{6,5},{7,6},{8,15},{9,8},{10,9... | collective-permute-start | bytes 294920 | tf_op jit(solution)/shard_map/ppermute | solution.py:24
  46.0 2.7 %collective-permute-done.6 = bf16[2,96,256]{2,1,0:T(8,128)(2,1)S(1)} collective-permute-done((bf16[2,96,256]{2,1,0:T(8,128)(2,1)S(1)}, bf16[2,96,256]{2,1,0:T(8,128)(2,1)S(1)}, u32[]{:S(2)}, u32[]{:S(2)}) %collective-permute-start.6) | collective-permute-done | bytes 98336 | tf_op jit(solution)/shard_map/ppermute | solution.py:24
  48.8 3.2 %collective-permute-start.8 = (bf16[2,48,256]{2,1,0:T(8,128)(2,1)S(1)}, bf16[2,48,256]{2,1,0:T(8,128)(2,1)S(1)}, u32[]{:S(2)}, u32[]{:S(2)}) collective-permute-start(bf16[2,48,256]{2,1,0:T(8,128)(2,1)S(1)} %slice.57), channel_id=1, source_target_pairs={{0,7},{1,0},{2,1},{3,2},{4,3},{5,4},{6,5},{7,6},{8,15},{9,8},{10,9... | collective-permute-start | bytes 147464 | tf_op jit(solution)/shard_map/ppermute | solution.py:24
  52.1 2.5 %collective-permute-done.8 = bf16[2,48,256]{2,1,0:T(8,128)(2,1)S(1)} collective-permute-done((bf16[2,48,256]{2,1,0:T(8,128)(2,1)S(1)}, bf16[2,48,256]{2,1,0:T(8,128)(2,1)S(1)}, u32[]{:S(2)}, u32[]{:S(2)}) %collective-permute-start.8) | collective-permute-done | bytes 49184 | tf_op jit(solution)/shard_map/ppermute | solution.py:24
  54.5 0.9 collective-permute-start.9
  55.4 2.7 %collective-permute-start.10 = (bf16[2,768,256]{2,1,0:T(8,128)(2,1)S(1)}, bf16[2,768,256]{2,1,0:T(8,128)(2,1)S(1)}, u32[]{:S(2)}, u32[]{:S(2)}) collective-permute-start(bf16[2,768,256]{2,1,0:T(8,128)(2,1)S(1)} %bitcast.98), channel_id=1, source_target_pairs={{0,16},{8,24},{16,0},{24,8},{1,17},{9,25},{17,1},{25,9},{2,18},{10... | collective-permute-start | bytes 2359304 | tf_op jit(solution)/shard_map/ppermute | solution.py:24
  58.1 1.4 collective-permute-start.11
  59.5 3.2 %convert_reduce_fusion = f32[384]{0:T(512)S(1)} fusion(bf16[6144,384]{1,0:T(8,128)(2,1)} %w_in.1), kind=kLoop, calls=%fused_computation | loop fusion | flops 4718208 | bytes 4720128 | tf_op jit(solution)/shard_map/reduce_sum | solution.py:231
  62.7 0.6 broadcast_in_dim.41.col_sum
  63.3 0.7 stack.37.me.refs_0_
  64.0 0.3 fusion
  64.2 11.7 %collective-permute-done.9.p1 = bf16[2,768,256]{2,1,0:T(8,128)(2,1)S(1)} collective-permute-done((bf16[2,768,256]{2,1,0:T(8,128)(2,1)S(1)}, bf16[2,768,256]{2,1,0:T(8,128)(2,1)S(1)}, u32[]{:S(2)}, u32[]{:S(2)}) %collective-permute-start.9) | collective-permute-done | bytes 786464 | tf_op jit(solution)/shard_map/ppermute | solution.py:24
  76.1 8.2 %collective-permute-done.10.p2 = bf16[2,768,256]{2,1,0:T(8,128)(2,1)S(1)} collective-permute-done((bf16[2,768,256]{2,1,0:T(8,128)(2,1)S(1)}, bf16[2,768,256]{2,1,0:T(8,128)(2,1)S(1)}, u32[]{:S(2)}, u32[]{:S(2)}) %collective-permute-start.10) | collective-permute-done | bytes 786464 | tf_op jit(solution)/shard_map/ppermute | solution.py:24
  84.6 0.3 collective-permute-done.11.p3
  85.2 0.6 add_rsqrt_fusion.rstd
  85.8 18.7 %shard_map.75 = (bf16[2,256,768]{2,1,0:T(8,128)(2,1)}, bf16[2,256,768]{2,1,0:T(8,128)(2,1)}, bf16[2,256,768]{2,1,0:T(8,128)(2,1)}, bf16[2,256,768]{2,1,0:T(8,128...) custom-call(s32[5]{0:T(128)} %stack.37.me.refs_0_, ...), custom_call_target="tpu_custom_call" | custom-call | flops 7247757312 | bytes 32505856 | tf_op jit(solution)/shard_map/pallas_call | solution.py:237
  104.7 0.5 collective-permute-start.29
  105.2 6.6 %collective-permute-done.18.refs_2_ = bf16[3072,384]{1,0:T(8,128)(2,1)S(1)} collective-permute-done((bf16[3072,384]{1,0:T(8,128)(2,1)}, bf16[3072,384]{1,0:T(8,128)(2,1)S(1)}, u32[]{:S(2)}, u32[]{:S(2)}) %collective-permute-start.18) | collective-permute-done | bytes 2359328 | tf_op jit(solution)/shard_map/ppermute | solution.py:24
  111.8 0.9 shard_map.76
  112.7 1.3 collective-permute-start.19
  114.0 1.7 collective-permute-start.15
  115.7 2.4 %collective-permute-start.16 = (bf16[2,256,768]{2,1,0:T(8,128)(2,1)S(1)}, bf16[2,256,768]{2,1,0:T(8,128)(2,1)S(1)}, u32[]{:S(2)}, u32[]{:S(2)}) collective-permute-start(bf16[2,256,768]{2,1,0:T(8,128)(2,1)S(1)} %copy-done.14), channel_id=1, source_target_pairs={{0,16},{8,24},{16,0},{24,8},{1,17},{9,25},{17,1},{25,9},{2,18},{10... | collective-permute-start | bytes 2359304 | tf_op jit(solution)/shard_map/ppermute | solution.py:24
  118.1 1.0 collective-permute-start.17
  119.1 2.3 %shard_map.79 = bf16[1536,384]{1,0:T(8,128)(2,1)} custom-call(s32[5]{0:T(128)S(1)} %copy-done.6, bf16[3072,384]{1,0:T(8,128)(2,1)S(1)} %copy-done.1, bf16[3072,384]{1,0:T(8,128)(2,1)S(1)} %collective-permute-done.18.refs_2_), custom_call_target="tpu_custom_call" | custom-call | flops 1207959552 | bytes 5898240 | tf_op jit(solution)/shard_map/pallas_call | solution.py:43
  121.4 13.4 %collective-permute-done.15.refs_2_ = bf16[2,256,768]{2,1,0:T(8,128)(2,1)S(1)} collective-permute-done((bf16[2,256,768]{2,1,0:T(8,128)(2,1)S(1)}, bf16[2,256,768]{2,1,0:T(8,128)(2,1)S(1)}, u32[]{:S(2)}, u32[]{:S(2)}) %collective-permute-start.15) | collective-permute-done | bytes 786464 | tf_op jit(solution)/shard_map/ppermute | solution.py:24
  134.8 2.3 %collective-permute-start.30 = (bf16[1536,384]{1,0:T(8,128)(2,1)}, bf16[1536,384]{1,0:T(8,128)(2,1)S(1)}, u32[]{:S(2)}, u32[]{:S(2)}) collective-permute-start(bf16[1536,384]{1,0:T(8,128)(2,1)} %shard_map.79), channel_id=1, source_target_pairs={{0,128},{128,0},{1,129},{129,1},{2,130},{130,2},{3,131},{131,3},{4... | collective-permute-start | bytes 3538952 | tf_op jit(solution)/shard_map/ppermute | solution.py:24
  137.1 15.2 %collective-permute-done.16.refs_3_ = bf16[2,256,768]{2,1,0:T(8,128)(2,1)S(1)} collective-permute-done((bf16[2,256,768]{2,1,0:T(8,128)(2,1)S(1)}, bf16[2,256,768]{2,1,0:T(8,128)(2,1)S(1)}, u32[]{:S(2)}, u32[]{:S(2)}) %collective-permute-start.16) | collective-permute-done | bytes 786464 | tf_op jit(solution)/shard_map/ppermute | solution.py:24
  152.3 2.0 shard_map.77
  154.3 0.9 copy-done.4
  155.2 1.3 copy-done.3
  156.5 4.1 %shard_map.78 = bf16[1536,384]{1,0:T(8,128)(2,1)} custom-call(s32[5]{0:T(128)S(1)} %copy-done.6, bf16[3072,384]{1,0:T(8,128)(2,1)S(1)} %copy-done, bf16[3072,384]{1,0:T(8,128)(2,1)} %collective-permute-done.29.refs_2_, bf16[1536,384]{1,0:T(8,128)(2,1)S(1)} %copy-done.3), custom_call_target="tpu_custom_call" | custom-call | flops 1207959552 | bytes 7077888 | tf_op jit(solution)/shard_map/pallas_call | solution.py:43
  160.7 4.9 %collective-permute-done.20 = bf16[4,2,96,256]{3,2,1,0:T(8,128)(2,1)} collective-permute-done((bf16[4,2,96,256]{3,2,1,0:T(8,128)(2,1)}, bf16[4,2,96,256]{3,2,1,0:T(8,128)(2,1)}, u32[]{:S(2)}, u32[]{:S(2)}) %collective-permute-start.20) | collective-permute-done | bytes 393248 | tf_op jit(solution)/shard_map/ppermute | solution.py:285
  165.6 1.1 fusion.17
  166.7 2.7 %collective-permute-start.21 = (bf16[2,96,256]{2,1,0:T(8,128)(2,1)S(1)}, bf16[2,96,256]{2,1,0:T(8,128)(2,1)S(1)}, u32[]{:S(2)}, u32[]{:S(2)}) collective-permute-start(bf16[2,96,256]{2,1,0:T(8,128)(2,1)S(1)} %get-tuple-element.39), channel_id=1, source_target_pairs={{0,2},{1,3},{2,4},{3,5},{4,6},{5,7},{6,0},{7,1},{8,10},{9,11},{10,... | collective-permute-start | bytes 294920 | tf_op jit(solution)/shard_map/ppermute | solution.py:24
  169.4 3.2 %collective-permute-start.22 = (bf16[2,96,256]{2,1,0:T(8,128)(2,1)S(1)}, bf16[2,96,256]{2,1,0:T(8,128)(2,1)S(1)}, u32[]{:S(2)}, u32[]{:S(2)}) collective-permute-start(bf16[2,96,256]{2,1,0:T(8,128)(2,1)S(1)} %get-tuple-element.41), channel_id=1, source_target_pairs={{0,4},{1,5},{2,6},{3,7},{4,0},{5,1},{6,2},{7,3},{8,12},{9,13},{10,... | collective-permute-start | bytes 294920 | tf_op jit(solution)/shard_map/ppermute | solution.py:24
  172.6 1.0 collective-permute-start.23
  173.6 4.1 %shard_map.80 = bf16[384,1536]{1,0:T(8,128)(2,1)} custom-call(s32[5]{0:T(128)S(1)} %copy-done.6, bf16[3072,384]{1,0:T(8,128)(2,1)S(1)} %copy-done, bf16[3072,384]{1,0:T(8,128)(2,1)} %collective-permute-done.29.refs_2_, bf16[1536,384]{1,0:T(8,128)(2,1)S(1)} %collective-permute-done.30.refs_3_), custom_call_target="tpu_custom_call" | custom-call | flops 1207959552 | bytes 7077888 | tf_op jit(solution)/shard_map/pallas_call | solution.py:43
  177.8 2.0 collective-permute-done.22
  179.8 2.4 %collective-permute-done.23 = bf16[2,96,256]{2,1,0:T(8,128)(2,1)S(1)} collective-permute-done((bf16[2,96,256]{2,1,0:T(8,128)(2,1)S(1)}, bf16[2,96,256]{2,1,0:T(8,128)(2,1)S(1)}, u32[]{:S(2)}, u32[]{:S(2)}) %collective-permute-start.23) | collective-permute-done | bytes 98336 | tf_op jit(solution)/shard_map/ppermute | solution.py:24
  182.2 1.0 dynamic-slice_bitcast_fusion.2
  183.2 1.3 collective-permute-start.25
  184.5 4.0 %collective-permute-start.26 = (bf16[2,96,256]{2,1,0:T(8,128)(2,1)S(1)}, bf16[2,96,256]{2,1,0:T(8,128)(2,1)S(1)}, u32[]{:S(2)}, u32[]{:S(2)}) collective-permute-start(bf16[2,96,256]{2,1,0:T(8,128)(2,1)S(1)} %get-tuple-element.38), channel_id=1, source_target_pairs={{0,16},{8,24},{16,0},{24,8},{1,17},{9,25},{17,1},{25,9},{2,18},{10... | collective-permute-start | bytes 294920 | tf_op jit(solution)/shard_map/ppermute | solution.py:24
  188.6 1.0 collective-permute-done.25
  189.6 3.2 %collective-permute-done.26 = bf16[2,96,256]{2,1,0:T(8,128)(2,1)S(1)} collective-permute-done((bf16[2,96,256]{2,1,0:T(8,128)(2,1)S(1)}, bf16[2,96,256]{2,1,0:T(8,128)(2,1)S(1)}, u32[]{:S(2)}, u32[]{:S(2)}) %collective-permute-start.26) | collective-permute-done | bytes 98336 | tf_op jit(solution)/shard_map/ppermute | solution.py:24
  192.8 0.3 collective-permute-done.27
  193.1 0.9 fusion.8
  194.2 0.6 fusion.14
  194.8 3.4 %collective-permute-done.28 = bf16[96,256]{1,0:T(8,128)(2,1)S(1)} collective-permute-done((bf16[96,256]{1,0:T(8,128)(2,1)S(1)}, bf16[96,256]{1,0:T(8,128)(2,1)S(1)}, u32[]{:S(2)}, u32[]{:S(2)}) %collective-permute-start.28) | collective-permute-done | bytes 49184 | tf_op jit(solution)/shard_map/ppermute | solution.py:24
  198.3 0.6 fusion.15
  (77 shorter events, 2.0 us)
Async XLA Ops:
  7.2 78.6 %all-gather.2.cloned.1.call-start = ((), (), s32[]{:S(2)}) async-start(), calls=%async_computation.1 | async-start | bytes 3538944 | tf_op jit(solution)/shard_map/all_gather | solution.py:223
  8.1 4.7 %collective-permute-start = (bf16[192,256]{1,0:T(8,128)(2,1)S(1)}, bf16[192,256]{1,0:T(8,128)(2,1)S(1)}, u32[]{:S(2)}, u32[]{:S(2)}) collective-permute-start(bf16[192,256]{1,0:T(8,128)(2,1)S(1)} %get-tuple-element.43), channel_id=1, source_target_pairs={{0,32},{32,0},{1,33},{33,1},{2,34},{34,2},{3,35},{35,3},{4,36},{36... | collective-permute-start | bytes 294920 | tf_op jit(solution)/shard_map/ppermute | solution.py:24
  12.8 8.5 %collective-permute-start.1 = (bf16[2,96,256]{2,1,0:T(8,128)(2,1)S(1)}, bf16[2,96,256]{2,1,0:T(8,128)(2,1)S(1)}, u32[]{:S(2)}, u32[]{:S(2)}) collective-permute-start(bf16[2,96,256]{2,1,0:T(8,128)(2,1)S(1)} %slice.55), channel_id=1, source_target_pairs={{0,1},{1,2},{2,3},{3,4},{4,5},{5,6},{6,7},{7,0},{8,9},{9,10},{10,1... | collective-permute-start | bytes 294920 | tf_op jit(solution)/shard_map/ppermute | solution.py:24
  21.3 5.9 %collective-permute-start.12 = (bf16[2,96,256]{2,1,0:T(8,128)(2,1)S(1)}, bf16[2,96,256]{2,1,0:T(8,128)(2,1)S(1)}, u32[]{:S(2)}, u32[]{:S(2)}) collective-permute-start(bf16[2,96,256]{2,1,0:T(8,128)(2,1)S(1)} %slice_select_fusion), channel_id=1, source_target_pairs={{0,8},{8,16},{16,24},{24,0},{1,9},{9,17},{17,25},{25,1},{2,10},{10... | collective-permute-start | bytes 294920 | tf_op jit(solution)/shard_map/ppermute | solution.py:24
  22.9 6.4 %collective-permute-start.13 = (bf16[2,96,256]{2,1,0:T(8,128)(2,1)S(1)}, bf16[2,96,256]{2,1,0:T(8,128)(2,1)S(1)}, u32[]{:S(2)}, u32[]{:S(2)}) collective-permute-start(bf16[2,96,256]{2,1,0:T(8,128)(2,1)S(1)} %slice_select_fusion), channel_id=1, source_target_pairs={{0,16},{8,24},{16,0},{24,8},{1,17},{9,25},{17,1},{25,9},{2,18},{10... | collective-permute-start | bytes 294920 | tf_op jit(solution)/shard_map/ppermute | solution.py:24
  25.6 4.6 %collective-permute-start.14 = (bf16[2,96,256]{2,1,0:T(8,128)(2,1)S(1)}, bf16[2,96,256]{2,1,0:T(8,128)(2,1)S(1)}, u32[]{:S(2)}, u32[]{:S(2)}) collective-permute-start(bf16[2,96,256]{2,1,0:T(8,128)(2,1)S(1)} %slice_select_fusion), channel_id=1, source_target_pairs={{0,24},{8,0},{16,8},{24,16},{1,25},{9,1},{17,9},{25,17},{2,26},{10... | collective-permute-start | bytes 294920 | tf_op jit(solution)/shard_map/ppermute | solution.py:24
  31.1 151.1 %reduce-scatter.2.cloned.1.call-start = ((), (), s32[]{:S(2)}) async-start(), calls=%async_computation.2 | async-start | bytes 3538944 | tf_op jit(solution)/shard_map/reduce_scatter | solution.py:291
  31.1 5.1 %collective-permute-start.2 = (bf16[2,96,256]{2,1,0:T(8,128)(2,1)S(1)}, bf16[2,96,256]{2,1,0:T(8,128)(2,1)S(1)}, u32[]{:S(2)}, u32[]{:S(2)}) collective-permute-start(bf16[2,96,256]{2,1,0:T(8,128)(2,1)S(1)} %slice.55), channel_id=1, source_target_pairs={{0,7},{1,0},{2,1},{3,2},{4,3},{5,4},{6,5},{7,6},{8,15},{9,8},{10,9... | collective-permute-start | bytes 294920 | tf_op jit(solution)/shard_map/ppermute | solution.py:24
  33.3 6.6 %collective-permute-start.3 = (bf16[2,96,256]{2,1,0:T(8,128)(2,1)S(1)}, bf16[2,96,256]{2,1,0:T(8,128)(2,1)S(1)}, u32[]{:S(2)}, u32[]{:S(2)}) collective-permute-start(bf16[2,96,256]{2,1,0:T(8,128)(2,1)S(1)} %collective-permute-done.1), channel_id=1, source_target_pairs={{0,1},{1,2},{2,3},{3,4},{4,5},{5,6},{6,7},{7,0},{8,9},{9,10},{10,1... | collective-permute-start | bytes 294920 | tf_op jit(solution)/shard_map/ppermute | solution.py:24
  36.3 5.9 %collective-permute-start.4 = (bf16[2,96,256]{2,1,0:T(8,128)(2,1)S(1)}, bf16[2,96,256]{2,1,0:T(8,128)(2,1)S(1)}, u32[]{:S(2)}, u32[]{:S(2)}) collective-permute-start(bf16[2,96,256]{2,1,0:T(8,128)(2,1)S(1)} %collective-permute-done.2), channel_id=1, source_target_pairs={{0,7},{1,0},{2,1},{3,2},{4,3},{5,4},{6,5},{7,6},{8,15},{9,8},{10,9... | collective-permute-start | bytes 294920 | tf_op jit(solution)/shard_map/ppermute | solution.py:24
  40.0 6.0 %collective-permute-start.5 = (bf16[2,96,256]{2,1,0:T(8,128)(2,1)S(1)}, bf16[2,96,256]{2,1,0:T(8,128)(2,1)S(1)}, u32[]{:S(2)}, u32[]{:S(2)}) collective-permute-start(bf16[2,96,256]{2,1,0:T(8,128)(2,1)S(1)} %collective-permute-done.3), channel_id=1, source_target_pairs={{0,1},{1,2},{2,3},{3,4},{4,5},{5,6},{6,7},{7,0},{8,9},{9,10},{10,1... | collective-permute-start | bytes 294920 | tf_op jit(solution)/shard_map/ppermute | solution.py:24
  42.2 6.6 %collective-permute-start.6 = (bf16[2,96,256]{2,1,0:T(8,128)(2,1)S(1)}, bf16[2,96,256]{2,1,0:T(8,128)(2,1)S(1)}, u32[]{:S(2)}, u32[]{:S(2)}) collective-permute-start(bf16[2,96,256]{2,1,0:T(8,128)(2,1)S(1)} %collective-permute-done.4), channel_id=1, source_target_pairs={{0,7},{1,0},{2,1},{3,2},{4,3},{5,4},{6,5},{7,6},{8,15},{9,8},{10,9... | collective-permute-start | bytes 294920 | tf_op jit(solution)/shard_map/ppermute | solution.py:24
  46.0 6.0 %collective-permute-start.7 = (bf16[2,48,256]{2,1,0:T(8,128)(2,1)S(1)}, bf16[2,48,256]{2,1,0:T(8,128)(2,1)S(1)}, u32[]{:S(2)}, u32[]{:S(2)}) collective-permute-start(bf16[2,48,256]{2,1,0:T(8,128)(2,1)S(1)} %slice.56), channel_id=1, source_target_pairs={{0,1},{1,2},{2,3},{3,4},{4,5},{5,6},{6,7},{7,0},{8,9},{9,10},{10,1... | collective-permute-start | bytes 147464 | tf_op jit(solution)/shard_map/ppermute | solution.py:24
  48.8 5.8 %collective-permute-start.8 = (bf16[2,48,256]{2,1,0:T(8,128)(2,1)S(1)}, bf16[2,48,256]{2,1,0:T(8,128)(2,1)S(1)}, u32[]{:S(2)}, u32[]{:S(2)}) collective-permute-start(bf16[2,48,256]{2,1,0:T(8,128)(2,1)S(1)} %slice.57), channel_id=1, source_target_pairs={{0,7},{1,0},{2,1},{3,2},{4,3},{5,4},{6,5},{7,6},{8,15},{9,8},{10,9... | collective-permute-start | bytes 147464 | tf_op jit(solution)/shard_map/ppermute | solution.py:24
  54.5 9.5 %copy-start.8 = (bf16[2,8,96,256]{3,2,1,0:T(8,128)(2,1)}, bf16[2,8,96,256]{3,2,1,0:T(8,128)(2,1)S(1)}, u32[]{:S(2)}) copy-start(bf16[2,8,96,256]{3,2,1,0:T(8,128)(2,1)S(1)} %fusion.9) | copy-start | bytes 2359300
  54.5 21.4 %collective-permute-start.9 = (bf16[2,768,256]{2,1,0:T(8,128)(2,1)S(1)}, bf16[2,768,256]{2,1,0:T(8,128)(2,1)S(1)}, u32[]{:S(2)}, u32[]{:S(2)}) collective-permute-start(bf16[2,768,256]{2,1,0:T(8,128)(2,1)S(1)} %bitcast.97), channel_id=1, source_target_pairs={{0,8},{8,16},{16,24},{24,0},{1,9},{9,17},{17,25},{25,1},{2,10},{10... | collective-permute-start | bytes 2359304 | tf_op jit(solution)/shard_map/ppermute | solution.py:24
  55.4 28.9 %collective-permute-start.10 = (bf16[2,768,256]{2,1,0:T(8,128)(2,1)S(1)}, bf16[2,768,256]{2,1,0:T(8,128)(2,1)S(1)}, u32[]{:S(2)}, u32[]{:S(2)}) collective-permute-start(bf16[2,768,256]{2,1,0:T(8,128)(2,1)S(1)} %bitcast.98), channel_id=1, source_target_pairs={{0,16},{8,24},{16,0},{24,8},{1,17},{9,25},{17,1},{25,9},{2,18},{10... | collective-permute-start | bytes 2359304 | tf_op jit(solution)/shard_map/ppermute | solution.py:24
  58.1 26.8 %collective-permute-start.11 = (bf16[2,768,256]{2,1,0:T(8,128)(2,1)S(1)}, bf16[2,768,256]{2,1,0:T(8,128)(2,1)S(1)}, u32[]{:S(2)}, u32[]{:S(2)}) collective-permute-start(bf16[2,768,256]{2,1,0:T(8,128)(2,1)S(1)} %bitcast.99), channel_id=1, source_target_pairs={{0,24},{8,0},{16,8},{24,16},{1,25},{9,1},{17,9},{25,17},{2,26},{10... | collective-permute-start | bytes 2359304 | tf_op jit(solution)/shard_map/ppermute | solution.py:24
  75.9 9.9 %copy-start.9 = (bf16[2,768,256]{2,1,0:T(8,128)(2,1)}, bf16[2,768,256]{2,1,0:T(8,128)(2,1)S(1)}, u32[]{:S(2)}) copy-start(bf16[2,768,256]{2,1,0:T(8,128)(2,1)S(1)} %collective-permute-done.9.p1) | copy-start | bytes 2359300
  84.3 1.5 copy-start.10
  84.9 0.9 copy-start.11
  85.2 0.6 copy-start.12
  104.5 7.3 %copy-start.1 = (bf16[3072,384]{1,0:T(8,128)(2,1)S(1)}, bf16[3072,384]{1,0:T(8,128)(2,1)}, u32[]{:S(2)}) copy-start(bf16[3072,384]{1,0:T(8,128)(2,1)} %get-tuple-element.19.refs_1_) | copy-start | bytes 7077892
  104.5 7.2 %copy-start.6 = (s32[5]{0:T(128)S(1)}, s32[5]{0:T(128)}, u32[]{:S(2)}) copy-start(s32[5]{0:T(128)} %stack.37.me.refs_0_) | copy-start | bytes 64
  104.6 7.2 %collective-permute-start.18 = (bf16[3072,384]{1,0:T(8,128)(2,1)}, bf16[3072,384]{1,0:T(8,128)(2,1)S(1)}, u32[]{:S(2)}, u32[]{:S(2)}) collective-permute-start(bf16[3072,384]{1,0:T(8,128)(2,1)} %get-tuple-element.20), channel_id=1, source_target_pairs={{0,64},{64,0},{1,65},{65,1},{2,66},{66,2},{3,67},{67,3},{4,68},{68... | collective-permute-start | bytes 7077896 | tf_op jit(solution)/shard_map/ppermute | solution.py:24
  104.7 50.6 %collective-permute-start.29 = (bf16[3072,384]{1,0:T(8,128)(2,1)}, bf16[3072,384]{1,0:T(8,128)(2,1)}, u32[]{:S(2)}, u32[]{:S(2)}) collective-permute-start(bf16[3072,384]{1,0:T(8,128)(2,1)} %get-tuple-element.25), channel_id=1, source_target_pairs={{0,64},{64,0},{1,65},{65,1},{2,66},{66,2},{3,67},{67,3},{4,68},{68... | collective-permute-start | bytes 7077896 | tf_op jit(solution)/shard_map/ppermute | solution.py:24
  111.8 2.3 %copy-start.15 = (bf16[2,256,768]{2,1,0:T(8,128)(2,1)S(1)}, bf16[2,256,768]{2,1,0:T(8,128)(2,1)}, u32[]{:S(2)}) copy-start(bf16[2,256,768]{2,1,0:T(8,128)(2,1)} %get-tuple-element.16) | copy-start | bytes 2359300
  111.8 4.0 %copy-start.14 = (bf16[2,256,768]{2,1,0:T(8,128)(2,1)S(1)}, bf16[2,256,768]{2,1,0:T(8,128)(2,1)}, u32[]{:S(2)}) copy-start(bf16[2,256,768]{2,1,0:T(8,128)(2,1)} %get-tuple-element.17) | copy-start | bytes 2359300
  111.8 6.4 %copy-start.13 = (bf16[2,256,768]{2,1,0:T(8,128)(2,1)S(1)}, bf16[2,256,768]{2,1,0:T(8,128)(2,1)}, u32[]{:S(2)}) copy-start(bf16[2,256,768]{2,1,0:T(8,128)(2,1)} %get-tuple-element.18) | copy-start | bytes 2359300
  112.7 39.6 %collective-permute-start.19 = (bf16[1536,384]{1,0:T(8,128)(2,1)S(1)}, bf16[1536,384]{1,0:T(8,128)(2,1)S(1)}, u32[]{:S(2)}, u32[]{:S(2)}) collective-permute-start(bf16[1536,384]{1,0:T(8,128)(2,1)S(1)} %shard_map.76), channel_id=1, source_target_pairs={{0,128},{128,0},{1,129},{129,1},{2,130},{130,2},{3,131},{131,3},{4... | collective-permute-start | bytes 3538952 | tf_op jit(solution)/shard_map/ppermute | solution.py:24
  114.0 20.8 %collective-permute-start.15 = (bf16[2,256,768]{2,1,0:T(8,128)(2,1)S(1)}, bf16[2,256,768]{2,1,0:T(8,128)(2,1)S(1)}, u32[]{:S(2)}, u32[]{:S(2)}) collective-permute-start(bf16[2,256,768]{2,1,0:T(8,128)(2,1)S(1)} %copy-done.15), channel_id=1, source_target_pairs={{0,8},{8,16},{16,24},{24,0},{1,9},{9,17},{17,25},{25,1},{2,10},{10... | collective-permute-start | bytes 2359304 | tf_op jit(solution)/shard_map/ppermute | solution.py:24
  115.7 36.5 %collective-permute-start.16 = (bf16[2,256,768]{2,1,0:T(8,128)(2,1)S(1)}, bf16[2,256,768]{2,1,0:T(8,128)(2,1)S(1)}, u32[]{:S(2)}, u32[]{:S(2)}) collective-permute-start(bf16[2,256,768]{2,1,0:T(8,128)(2,1)S(1)} %copy-done.14), channel_id=1, source_target_pairs={{0,16},{8,24},{16,0},{24,8},{1,17},{9,25},{17,1},{25,9},{2,18},{10... | collective-permute-start | bytes 2359304 | tf_op jit(solution)/shard_map/ppermute | solution.py:24
  118.1 34.1 %copy-start.7 = (bf16[2,256,768]{2,1,0:T(8,128)(2,1)S(1)}, bf16[2,256,768]{2,1,0:T(8,128)(2,1)}, u32[]{:S(2)}) copy-start(bf16[2,256,768]{2,1,0:T(8,128)(2,1)} %get-tuple-element.15.refs_1_) | copy-start | bytes 2359300
  118.1 34.1 %collective-permute-start.17 = (bf16[2,256,768]{2,1,0:T(8,128)(2,1)S(1)}, bf16[2,256,768]{2,1,0:T(8,128)(2,1)S(1)}, u32[]{:S(2)}, u32[]{:S(2)}) collective-permute-start(bf16[2,256,768]{2,1,0:T(8,128)(2,1)S(1)} %copy-done.13), channel_id=1, source_target_pairs={{0,24},{8,0},{16,8},{24,16},{1,25},{9,1},{17,9},{25,17},{2,26},{10... | collective-permute-start | bytes 2359304 | tf_op jit(solution)/shard_map/ppermute | solution.py:24
  134.8 38.8 %collective-permute-start.30 = (bf16[1536,384]{1,0:T(8,128)(2,1)}, bf16[1536,384]{1,0:T(8,128)(2,1)S(1)}, u32[]{:S(2)}, u32[]{:S(2)}) collective-permute-start(bf16[1536,384]{1,0:T(8,128)(2,1)} %shard_map.79), channel_id=1, source_target_pairs={{0,128},{128,0},{1,129},{129,1},{2,130},{130,2},{3,131},{131,3},{4... | collective-permute-start | bytes 3538952 | tf_op jit(solution)/shard_map/ppermute | solution.py:24
  152.3 2.0 copy-start.2
  152.3 2.9 %copy-start = (bf16[3072,384]{1,0:T(8,128)(2,1)S(1)}, bf16[3072,384]{1,0:T(8,128)(2,1)}, u32[]{:S(2)}) copy-start(bf16[3072,384]{1,0:T(8,128)(2,1)} %get-tuple-element.24.refs_1_) | copy-start | bytes 7077892
  154.3 0.9 copy-start.4
  155.2 10.3 %collective-permute-start.20 = (bf16[4,2,96,256]{3,2,1,0:T(8,128)(2,1)}, bf16[4,2,96,256]{3,2,1,0:T(8,128)(2,1)}, u32[]{:S(2)}, u32[]{:S(2)}) collective-permute-start(bf16[4,2,96,256]{3,2,1,0:T(8,128)(2,1)} %get-tuple-element.22), channel_id=1, source_target_pairs={{0,1},{1,0},{2,3},{3,2},{4,5},{5,4},{6,7},{7,6},{8,9},{9,8},{10,11... | collective-permute-start | bytes 1179656 | tf_op jit(solution)/shard_map/ppermute | solution.py:285
  155.2 1.3 copy-start.3
  156.5 9.0 %copy-start.5 = (f32[4,2,96,256]{3,2,1,0:T(8,128)S(1)}, f32[4,2,96,256]{3,2,1,0:T(8,128)}, u32[]{:S(2)}) copy-start(f32[4,2,96,256]{3,2,1,0:T(8,128)} %copy-done.4) | copy-start | bytes 2359300
  166.7 11.1 %collective-permute-start.21 = (bf16[2,96,256]{2,1,0:T(8,128)(2,1)S(1)}, bf16[2,96,256]{2,1,0:T(8,128)(2,1)S(1)}, u32[]{:S(2)}, u32[]{:S(2)}) collective-permute-start(bf16[2,96,256]{2,1,0:T(8,128)(2,1)S(1)} %get-tuple-element.39), channel_id=1, source_target_pairs={{0,2},{1,3},{2,4},{3,5},{4,6},{5,7},{6,0},{7,1},{8,10},{9,11},{10,... | collective-permute-start | bytes 294920 | tf_op jit(solution)/shard_map/ppermute | solution.py:24
  169.4 10.3 %collective-permute-start.22 = (bf16[2,96,256]{2,1,0:T(8,128)(2,1)S(1)}, bf16[2,96,256]{2,1,0:T(8,128)(2,1)S(1)}, u32[]{:S(2)}, u32[]{:S(2)}) collective-permute-start(bf16[2,96,256]{2,1,0:T(8,128)(2,1)S(1)} %get-tuple-element.41), channel_id=1, source_target_pairs={{0,4},{1,5},{2,6},{3,7},{4,0},{5,1},{6,2},{7,3},{8,12},{9,13},{10,... | collective-permute-start | bytes 294920 | tf_op jit(solution)/shard_map/ppermute | solution.py:24
  172.6 9.5 %collective-permute-start.23 = (bf16[2,96,256]{2,1,0:T(8,128)(2,1)S(1)}, bf16[2,96,256]{2,1,0:T(8,128)(2,1)S(1)}, u32[]{:S(2)}, u32[]{:S(2)}) collective-permute-start(bf16[2,96,256]{2,1,0:T(8,128)(2,1)S(1)} %get-tuple-element.40), channel_id=1, source_target_pairs={{0,6},{1,7},{2,0},{3,1},{4,2},{5,3},{6,4},{7,5},{8,14},{9,15},{10,... | collective-permute-start | bytes 294920 | tf_op jit(solution)/shard_map/ppermute | solution.py:24
  183.2 6.4 %collective-permute-start.25 = (bf16[2,96,256]{2,1,0:T(8,128)(2,1)S(1)}, bf16[2,96,256]{2,1,0:T(8,128)(2,1)S(1)}, u32[]{:S(2)}, u32[]{:S(2)}) collective-permute-start(bf16[2,96,256]{2,1,0:T(8,128)(2,1)S(1)} %get-tuple-element.36), channel_id=1, source_target_pairs={{0,8},{8,16},{16,24},{24,0},{1,9},{9,17},{17,25},{25,1},{2,10},{10... | collective-permute-start | bytes 294920 | tf_op jit(solution)/shard_map/ppermute | solution.py:24
  184.5 8.3 %collective-permute-start.26 = (bf16[2,96,256]{2,1,0:T(8,128)(2,1)S(1)}, bf16[2,96,256]{2,1,0:T(8,128)(2,1)S(1)}, u32[]{:S(2)}, u32[]{:S(2)}) collective-permute-start(bf16[2,96,256]{2,1,0:T(8,128)(2,1)S(1)} %get-tuple-element.38), channel_id=1, source_target_pairs={{0,16},{8,24},{16,0},{24,8},{1,17},{9,25},{17,1},{25,9},{2,18},{10... | collective-permute-start | bytes 294920 | tf_op jit(solution)/shard_map/ppermute | solution.py:24
  188.5 4.6 %collective-permute-start.27 = (bf16[2,96,256]{2,1,0:T(8,128)(2,1)S(1)}, bf16[2,96,256]{2,1,0:T(8,128)(2,1)S(1)}, u32[]{:S(2)}, u32[]{:S(2)}) collective-permute-start(bf16[2,96,256]{2,1,0:T(8,128)(2,1)S(1)} %get-tuple-element.37), channel_id=1, source_target_pairs={{0,24},{8,0},{16,8},{24,16},{1,25},{9,1},{17,9},{25,17},{2,26},{10... | collective-permute-start | bytes 294920 | tf_op jit(solution)/shard_map/ppermute | solution.py:24
  188.5 5.7 %collective-permute-start.24 = (bf16[96,256]{1,0:T(8,128)(2,1)S(1)}, bf16[96,256]{1,0:T(8,128)(2,1)S(1)}, u32[]{:S(2)}, u32[]{:S(2)}) collective-permute-start(bf16[96,256]{1,0:T(8,128)(2,1)S(1)} %fusion.12), channel_id=1, source_target_pairs={{0,32},{32,0},{1,33},{33,1},{2,34},{34,2},{3,35},{35,3},{4,36},{36... | collective-permute-start | bytes 147464 | tf_op jit(solution)/shard_map/ppermute | solution.py:24
  194.1 4.2 %collective-permute-start.28 = (bf16[96,256]{1,0:T(8,128)(2,1)S(1)}, bf16[96,256]{1,0:T(8,128)(2,1)S(1)}, u32[]{:S(2)}, u32[]{:S(2)}) collective-permute-start(bf16[96,256]{1,0:T(8,128)(2,1)S(1)} %fusion.13), channel_id=1, source_target_pairs={{0,32},{32,0},{1,33},{33,1},{2,34},{34,2},{3,35},{35,3},{4,36},{36... | collective-permute-start | bytes 147464 | tf_op jit(solution)/shard_map/ppermute | solution.py:24
Sparse Core Ops, SparseCore 0:
  31.2 46.0 all-gather.1
  104.7 45.7 reduce-scatter.1

commit v2 on v1

v2 whole, which is shorter than its diff:
```python
import functools
import math

import jax
import jax.numpy as jnp
import numpy as np
from jax import lax
from jax.experimental import pallas as pl
from jax.experimental.pallas import tpu as pltpu
from jax.sharding import Mesh, PartitionSpec as P

eps = 1e-06
AXES = ("yh", "core", "yl", "x", "z")
SIZE = {"yh": 2, "core": 2, "yl": 2, "x": 4, "z": 8}
low = jnp.bfloat16
wide = jnp.float32
TOK, OWN, HID, WIDTH = 256, 96, 384, 6144
HALF, BLOCK, QUARTER = WIDTH // 2, WIDTH // 8, WIDTH // 4
NEAR = 80
REST = OWN - NEAR
FAR = OWN + REST
root = math.sqrt(2.0 / math.pi)
work = 2 * TOK * WIDTH * HID


def shift(values, axis, step):
    count = SIZE[axis]
    return lax.ppermute(values, axis, [(i, (i + step) % count) for i in range(count)])


def dot(first, second, one, two):
    return lax.dot_general(first, second, (((one,), (two,)), ((), ())), preferred_element_type=wide)


def whole(shape):
    return pl.BlockSpec(shape, lambda t, me: (0,) * len(shape))


def call(body, steps, scalars, ins, outs, scratch=(), after=(), flops=work):
    count = 1 + len(ins)

    def run(*refs):
        body(*refs[:count], *refs[count + len(after) :])

    shapes = [jax.ShapeDtypeStruct(shape, kind) for shape, kind, _ in outs]
    moved = sum(math.prod(v.shape) * v.dtype.itemsize for v in [*(a for a, _ in ins), *shapes])
    return pl.pallas_call(
        run,
        out_shape=shapes,
        grid_spec=pltpu.PrefetchScalarGridSpec(
            num_scalar_prefetch=1,
            grid=(steps,),
            in_specs=[spec for _, spec in ins] + [pl.BlockSpec(memory_space=pl.ANY) for _ in after],
            out_specs=[spec for _, _, spec in outs],
            scratch_shapes=list(scratch),
        ),
        compiler_params=pltpu.CompilerParams(vmem_limit_bytes=24 << 20),
        cost_estimate=pl.CostEstimate(flops=flops, bytes_accessed=moved, transcendentals=0),
    )(scalars, *(a for a, _ in ins), *after)


def block_at(me, k, yl):
    return yl * 4 + ((me[0] - k) & 3)


def rows_of(block):
    return pl.ds(pl.multiple_of(block * BLOCK, BLOCK), BLOCK)


def gelu_parts(hidden):
    square = hidden * hidden
    tanh = jnp.tanh(root * (hidden + 0.044715 * hidden * square))
    half = 0.5 * (1.0 + tanh)
    slope = half + 0.5 * hidden * (1.0 - tanh * tanh) * (root * (1.0 + 3 * 0.044715 * square))
    return hidden * half, slope


def main_body(me, p0, p1, p2, p3, col_sum, w_in, w_out, part, *refs):
    mlp_outs, (patch, mine, other, away_mine, away_other) = refs[:4], refs[4:9]
    p_near, in_near, out_near, cot, norm, mlp_stage, rest_stage, patch_stage, grad_stage, acc, grad_acc = refs[9:20]
    p_sem, rest_sem, in_sem, out_sem, cot_sem, mlp_sem, mlp_rest_sem, patch_sem, grad_sem = refs[20:]
    first_rows, rest_rows, far_rows = pl.ds(0, NEAR), pl.ds(NEAR, REST), pl.ds(OWN, REST)

    def p_copy(t, piece, yl):
        return pltpu.make_async_copy(piece.at[yl], p_near.at[t, :, first_rows], p_sem.at[t])

    def rest_copy(t):
        source = part.at[:, t // 2, t % 2, far_rows]
        return pltpu.make_async_copy(source, p_near.at[t, :, rest_rows], rest_sem.at[t])

    def in_copy(t):
        return pltpu.make_async_copy(w_in.at[rows_of(block_at(me, t // 2, t % 2))], in_near.at[t], in_sem.at[t])

    def out_copy(j):
        return pltpu.make_async_copy(w_out.at[:, rows_of(j)], out_near.at[j], out_sem.at[j])

    def cot_copy(j):
        source = part.at[:, (me[0] - (j % 4)) & 3, j // 4, pl.ds(0, OWN)]
        return pltpu.make_async_copy(source, cot.at[j], cot_sem.at[j])

    for t in range(8):
        p_copy(t, (p0, p1, p2, p3)[t // 2], t % 2).start()
        rest_copy(t).start()
    for t in range(8):
        in_copy(t).start()
    for j in range(8):
        out_copy(j).start()
        cot_copy(j).start()
    acc[...] = jnp.zeros_like(acc)
    grad_acc[...] = jnp.zeros_like(grad_acc)

    def sums_step(t, sums):
        p_copy(t, p0, 0).wait()
        rest_copy(t).wait()
        value = p_near[t].reshape(BLOCK, TOK).astype(wide)
        return sums[0] + jnp.sum(value, axis=0, keepdims=True), sums[1] + jnp.sum(value * value, axis=0, keepdims=True)

    zero = jnp.zeros((1, TOK), wide)
    sums = lax.fori_loop(0, 8, sums_step, (zero, zero))
    mean = sums[0] / WIDTH
    rstd = lax.rsqrt(sums[1] / WIDTH - mean * mean + eps)

    def hidden_step(t, _):
        value = ((p_near[t].reshape(BLOCK, TOK).astype(wide) - mean) * rstd).astype(low)
        norm[block_at(me, t // 2, t % 2)] = value
        in_copy(t).wait()
        acc[...] += dot(value, in_near[t], 0, 0)
        return 0

    lax.fori_loop(0, 8, hidden_step, 0)

    def grad_step(j, _):
        out_copy(j).wait()
        cot_copy(j).wait()
        grad_acc[...] += dot(out_near[j], cot[j].reshape(BLOCK, TOK), 1, 0)
        return 0

    lax.fori_loop(0, 8, grad_step, 0)

    hidden = acc[...].T
    act_wide, slope = gelu_parts(hidden)
    act_t = act_wide.astype(low)
    act = act_wide.T.astype(low)
    grad_wide = slope * grad_acc[...]
    grad_t = grad_wide.astype(low)
    grad = grad_wide.T.astype(low)
    rounded = grad_t.astype(wide)
    first = jnp.sum(rounded * col_sum[...].T, axis=0, keepdims=True) / WIDTH
    second = jnp.sum(rounded * hidden, axis=0, keepdims=True) / WIDTH

    grad_to = (away_other, away_mine, other, mine)

    def grad_copy(q):
        return pltpu.make_async_copy(grad_stage.at[q], grad_to[q], grad_sem.at[q])

    for q in range(4):
        yh = me[3] if q in (1, 3) else 1 - me[3]
        core = 1 - me[4] if q < 2 else me[4]
        blocks = pl.ds((yh * 2 + core) * 2, 2)
        grad_stage[q, :QUARTER] = dot(norm[blocks].reshape(QUARTER, TOK), grad, 1, 0).astype(low)
        value = dot(act_t, cot[blocks].reshape(QUARTER, TOK), 1, 1).astype(low)
        for i in range(4):
            grad_stage[q, QUARTER + i * HID : QUARTER + (i + 1) * HID] = value[:, i * HID : (i + 1) * HID]
        grad_copy(q).start()

    def patch_copy(t):
        to = patch.at[:, t % 2, (me[0] - t // 2) & 3, pl.ds(0, OWN)]
        return pltpu.make_async_copy(patch_stage.at[t], to, patch_sem.at[t])

    def patch_step(t, _):
        share = dot(in_near[t], grad_t, 1, 0)
        normed = (p_near[t].reshape(BLOCK, TOK).astype(wide) - mean) * rstd
        share = rstd * (share - first - normed * second)
        patch_stage[t] = share.astype(low).reshape(8, OWN, TOK)
        patch_copy(t).start()
        return 0

    lax.fori_loop(0, 8, patch_step, 0)

    def mlp_copy(t):
        return pltpu.make_async_copy(mlp_stage.at[t], mlp_outs[t // 2].at[t % 2], mlp_sem.at[t])

    def mlp_rest_copy(t):
        to = patch.at[:, t % 2, (me[0] + t // 2) & 3, far_rows]
        return pltpu.make_async_copy(rest_stage.at[t], to, mlp_rest_sem.at[t])

    for t in range(8):
        value = dot(act, out_near[(t % 2) * 4 + ((me[0] + t // 2) & 3)], 1, 0)
        value = value.T.astype(low).reshape(8, OWN, TOK)
        mlp_stage[t] = value[:, :NEAR]
        mlp_copy(t).start()
        rest_stage[t] = value[:, NEAR:]
        mlp_rest_copy(t).start()
    for t in range(8):
        patch_copy(t).wait()
        mlp_copy(t).wait()
        mlp_rest_copy(t).wait()
    for q in range(4):
        grad_copy(q).wait()


def add_body(count, plan, me, *refs):
    ins, rest = refs[:count], refs[count:]
    into, stage, in_sem, out_sem = rest[-4:]

    def fetch(i):
        return [
            pltpu.make_async_copy(ins[which].at[pl.ds(row, HID)], into.at[i, n], in_sem.at[i, n])
            for n, (which, row) in enumerate(plan[i][0])
        ]

    def store(i):
        which, at, across = plan[i][1]
        block = pl.ds(at, HID)
        return pltpu.make_async_copy(stage.at[i], rest[which].at[:, block] if across else rest[which].at[block], out_sem.at[i])

    for i in range(len(plan)):
        for copy in fetch(i):
            copy.start()
    for i in range(len(plan)):
        for copy in fetch(i):
            copy.wait()
        stage[i] = sum(into[i, n].astype(wide) for n in range(len(plan[i][0]))).astype(low)
        store(i).start()
    for i in range(len(plan)):
        store(i).wait()


def add_call(scalars, arrays, shapes, plan):
    far = pl.BlockSpec(memory_space=pl.ANY)
    blocks, terms = len(plan), len(plan[0][0])
    dma = pltpu.SemaphoreType.DMA
    return pl.pallas_call(
        functools.partial(add_body, len(arrays), plan),
        out_shape=[jax.ShapeDtypeStruct(shape, low) for shape in shapes],
        in_specs=[pl.BlockSpec(memory_space=pltpu.SMEM)] + [far] * len(arrays),
        out_specs=[far] * len(shapes),
        scratch_shapes=[
            pltpu.VMEM((blocks, terms, HID, HID), low),
            pltpu.VMEM((blocks, HID, HID), low),
            dma((blocks, terms)),
            dma((blocks,)),
        ],
        compiler_params=pltpu.CompilerParams(vmem_limit_bytes=60 << 20),
        cost_estimate=pl.CostEstimate(flops=0, bytes_accessed=0, transcendentals=0),
    )(scalars, *arrays)


def sum_body(me, r0, r1, r2, r3, keep, away, total):
    total[...] = r0[0].astype(wide) + r1[0].astype(wide) + r2[0].astype(wide) + r3[0].astype(wide)
    for d in range(4):
        pair = ((me[1] // 2 + d) & 3) * 2
        keep[d, 0] = total[pair + (me[1] & 1)]
        away[d, 0] = total[pair + 1 - (me[1] & 1)].astype(low)


def ring_z(block, me):
    up = down = block
    parts = {0: block}
    for step in (1, 2, 3):
        up, down = shift(up, "z", 1), shift(down, "z", -1)
        parts[step], parts[8 - step] = up, down
    half = NEAR // 2 // 16 * 16
    parts[4] = jnp.concatenate([shift(up[:, :half], "z", 1), shift(down[:, half:], "z", -1)], axis=1)
    buffer = jnp.zeros((2, 8, *block.shape[1:]), low)
    for k, part in parts.items():
        buffer = lax.dynamic_update_slice_in_dim(buffer, part[:, None], (me - k) & 7, 1)
    return buffer


def per_device(patches, proj_in, proj_out, cotangent):
    me = {axis: lax.axis_index(axis) for axis in AXES}
    scalars = jnp.stack([me["x"], me["z"], me["yl"], me["yh"], me["core"]]).astype(jnp.int32)

    both = jnp.concatenate([patches.T, cotangent.T], axis=0)
    near = shift(both, "yl", 1)
    pair = jnp.where(me["yl"] == 0, jnp.stack([both, near]), jnp.stack([near, both]))
    x_pair, c_pair = pair[:, :OWN], pair[:, OWN:]

    c_pair = jnp.concatenate([c_pair, x_pair[:, NEAR:]], axis=1)
    c_parts = [c_pair] + [shift(c_pair, "x", k) for k in range(1, 4)]
    c_x = jnp.concatenate(c_parts, axis=0)
    c_all = lax.all_gather(c_x.reshape(8 * FAR, TOK), "z", axis=0, tiled=True).reshape(8, 4, 2, FAR, TOK)
    x_z = ring_z(x_pair[:, :NEAR], me["z"])
    x_all = [x_z] + [shift(x_z, "x", k) for k in range(1, 4)]

    col_sum = jnp.sum(proj_in.astype(wide), axis=0, keepdims=True)

    dma = pltpu.SemaphoreType.DMA
    near, far = pl.BlockSpec(memory_space=pltpu.VMEM), pl.BlockSpec(memory_space=pl.ANY)
    both_rows = 2 * QUARTER
    shapes = [(2, 8, NEAR, TOK)] * 4 + [(8, 2, 4, FAR, TOK)] + [(both_rows, HID)] * 4
    params = pltpu.CompilerParams(vmem_limit_bytes=60 << 20)
    *mlp_parts, patch_parts, mine, other, away_mine, away_other = pl.pallas_call(
        main_body,
        out_shape=[jax.ShapeDtypeStruct(shape, low) for shape in shapes],
        in_specs=[pl.BlockSpec(memory_space=pltpu.SMEM)] + [far] * 4 + [near] + [far] * 3,
        out_specs=[far] * len(shapes),
        scratch_shapes=[
            pltpu.VMEM((8, 8, OWN, TOK), low),
            pltpu.VMEM((8, BLOCK, HID), low),
            pltpu.VMEM((8, HID, BLOCK), low),
            pltpu.VMEM((8, 8, OWN, TOK), low),
            pltpu.VMEM((8, BLOCK, TOK), low),
            pltpu.VMEM((8, 8, NEAR, TOK), low),
            pltpu.VMEM((8, 8, REST, TOK), low),
            pltpu.VMEM((8, 8, OWN, TOK), low),
            pltpu.VMEM((4, both_rows, HID), low),
            pltpu.VMEM((TOK, HID), wide),
            pltpu.VMEM((HID, TOK), wide),
        ]
        + [dma((8,))] * 8
        + [dma((4,))],
        compiler_params=params,
        cost_estimate=pl.CostEstimate(flops=6 * work, bytes_accessed=31 << 20, transcendentals=0),
    )(scalars, *x_all, col_sum, proj_in, proj_out, c_all)

    got_other = shift(away_other, "core", 1)
    got_mine = shift(away_mine, "core", 1)


    starts = range(0, both_rows, HID)
    backs = []
    for some in (starts[:2], starts[2:]):
        plan = [([(0, row), (1, row)], (0, row - some[0], False)) for row in some]
        (send,) = add_call(scalars, [other, got_other], [(len(some) * HID, HID)], plan)
        backs.append(shift(send, "yh", 1))

    mlp_got = [mlp_parts[0]] + [shift(mlp_parts[k], "x", k) for k in range(1, 4)]
    keep, flip = call(
        sum_body,
        2,
        scalars,
        [(part, pl.BlockSpec((1, 8, NEAR, TOK), lambda t, me: (t, 0, 0, 0))) for part in mlp_got],
        [((4, 2, NEAR, TOK), kind, pl.BlockSpec((4, 1, NEAR, TOK), lambda t, me: (0, t, 0, 0))) for kind in (wide, low)],
        [pltpu.VMEM((8, NEAR, TOK), wide)],
        after=[got_mine, backs[0]],
    )
    keep = keep + lax.ppermute(flip, "z", [(i, i ^ 1) for i in range(8)]).astype(wide)
    total = keep[0]
    for d in range(1, 4):
        total = total + shift(keep[d].astype(low), "z", 2 * d).astype(wide)

    rest = lax.psum_scatter(patch_parts.reshape(64 * FAR, TOK), "z", scatter_dimension=0, tiled=True)
    rest = rest.reshape(2, 4, FAR, TOK)
    rest_total = lax.dynamic_index_in_dim(rest, me["x"], 1, keepdims=False).astype(wide)
    for k in range(1, 4):
        block = lax.dynamic_index_in_dim(rest, (me["x"] + k) & 3, 1, keepdims=False)
        rest_total = rest_total + shift(block, "x", k).astype(wide)

    total = jnp.concatenate([rest_total, total], axis=1)
    mine_y = jnp.where(me["yl"] == 0, total[0], total[1])
    other_y = jnp.where(me["yl"] == 0, total[1], total[0])
    result = (mine_y + shift(other_y.astype(low), "yl", 1).astype(wide)).astype(low)
    patch_grad = result[:OWN].T
    mlp_out = jnp.concatenate([result[FAR:], result[OWN:FAR]], axis=0).T

    plan = []
    for i, row in enumerate(starts):
        back = (2, row) if i < 2 else (3, row - starts[2])
        plan.append(([(0, row), (1, row), back], (i // 4, i % 4 * HID, i > 3)))
    grad_in, grad_out = add_call(scalars, [mine, got_mine, *backs], [(QUARTER, HID), (HID, QUARTER)], plan)
    return mlp_out, patch_grad, grad_in, grad_out


def solution(mesh):
    devices = np.asarray(mesh.devices).reshape([SIZE[axis] for axis in AXES])
    fine = Mesh(devices, AXES)
    dp, mp = ("yh", "core"), ("yl", "x", "z")
    in_specs = (P(dp, mp), P(None, mp), P(mp, None), P(dp, mp))
    out_specs = (P(dp, mp), P(dp, mp), P(dp, mp), P(mp, dp))
    return jax.shard_map(per_device, mesh=fine, in_specs=in_specs, out_specs=out_specs, check_vma=False)
```

time: 207 us -> 192 us (0.928)
  waiting for transfers between devices: 96.4 us -> 76.8 us
  Pallas kernels: 32.2 us -> 36.8 us
  other arithmetic: 9.91 us -> 6.7 us
  local copies, waits for them, and re-layouts: 4.69 us -> 6.89 us
    ppermute x30 -> x29, waiting for transfers between devices: 91.4 us -> 62.6 us  [shift(): lax.ppermute(values, axis, [(i, (i + step) % count) for i in range(count)])]
    pallas_call x0 -> x3, Pallas kernels: none -> 11.6 us  [add_call(): pl.pallas_call(functools.partial(add_body, len(arrays), plan), out_shape=...]
    pallas_call x5 -> x1, Pallas kernels: 13.5 us -> 2.31 us  [call(): pl.pallas_call(run, out_shape=shapes, grid_spec=pltpu.PrefetchScalarGridS...]
    ppermute x1, waiting for transfers between devices: 4.89 us -> 14.2 us  [per_device(): lax.ppermute(flip, 'z', [(i, i ^ 1) for i in range(8)]).astype(wide)]
    pallas_call x1, Pallas kernels: 18.7 us -> 22.9 us  [per_device(): pl.pallas_call(main_body, out_shape=[jax.ShapeDtypeStruct(shape, low) for...]
    unnamed x32 -> x20, local copies, waits for them, and re-layouts: 2.24 us -> 4.54 us
    ppermute x30 -> x29, starting transfers between devices: 48.1 us -> 48.9 us  [shift(): lax.ppermute(values, axis, [(i, (i + step) % count) for i in range(count)])]
  transfers between devices with their start and end apart: 33 -> 32, of which waited for: 23 -> 18; matrix products, arithmetic and copies ran while one was open for 4% -> 4% of each run, Pallas kernels for 7% -> 7%
where the time goes in v2:
time: 192 us; the launch traced here: 191 us
  waiting for transfers between devices  76.8 us (40%)
  starting transfers between devices  49 us (26%)
  Pallas kernels  36.8 us (19%)
  between operations  14.4 us (8%)
  local copies, waits for them, and re-layouts  6.89 us (4%)
  other arithmetic  6.7 us (3%)
    ppermute x29, waiting for transfers between devices, shift(): lax.ppermute(values, axis, [(i, (i + step) % count) for i in range(count)])  62.6 us
    ppermute x29, starting transfers between devices, shift(): lax.ppermute(values, axis, [(i, (i + step) % count) for i in range(count)])  48.9 us
    pallas_call x1, Pallas kernels, per_device(): pl.pallas_call(main_body, out_shape=[jax.ShapeDtypeStruct(shape, low) for...  22.9 us
    ppermute x1, waiting for transfers between devices, per_device(): lax.ppermute(flip, 'z', [(i, i ^ 1) for i in range(8)]).astype(wide)  14.2 us
    pallas_call x3, Pallas kernels, add_call(): pl.pallas_call(functools.partial(add_body, len(arrays), plan), out_shape=...  11.6 us
    unnamed x20, local copies, waits for them, and re-layouts  4.54 us
  transfers between devices with their start and end apart: 32, of which 18 were waited for; matrix products, arithmetic and copies ran while one was open for 4% of the time, Pallas kernels for 7%

profile of v2, /device:TPU:24, one launch (start us, length us, event | category | flops | bytes accessed | tf_op | source)
XLA Modules:
  0.0 190.6 jit_solution(6757855046555963123)
XLA Ops:
  7.2 0.8 fusion.9
  8.1 0.8 collective-permute-start
  8.9 3.9 %collective-permute-done = bf16[192,256]{1,0:T(8,128)(2,1)S(1)} collective-permute-done((bf16[192,256]{1,0:T(8,128)(2,1)S(1)}, bf16[192,256]{1,0:T(8,128)(2,1)S(1)}, u32[]{:S(2)}, u32[]{:S(2)}) %collective-permute-start) | collective-permute-done | bytes 98336 | tf_op jit(solution)/shard_map/ppermute | solution.py:28
  12.8 1.6 collective-permute-start.12
  14.4 2.7 %collective-permute-start.13 = (bf16[2,112,256]{2,1,0:T(8,128)(2,1)S(1)}, bf16[2,112,256]{2,1,0:T(8,128)(2,1)S(1)}, u32[]{:S(2)}, u32[]{:S(2)}) collective-permute-start(bf16[2,112,256]{2,1,0:T(8,128)(2,1)S(1)} %pad_maximum_fusion.2), channel_id=1, source_target_pairs={{0,16},{8,24},{16,0},{24,8},{1,17},{9,25},{17,1},{25,9},{2,18},{10... | collective-permute-start | bytes 344072 | tf_op jit(solution)/shard_map/ppermute | solution.py:28
  17.1 1.4 collective-permute-start.14
  18.6 1.5 collective-permute-done.12
  20.1 1.2 collective-permute-done.13
  21.3 0.6 collective-permute-done.14
  21.9 0.8 pad_maximum_fusion
  22.7 0.0 reduce-scatter.2.cloned.1.call-start
  22.8 2.0 %collective-permute-start.1 = (bf16[2,80,256]{2,1,0:T(8,128)(2,1)S(1)}, bf16[2,80,256]{2,1,0:T(8,128)(2,1)S(1)}, u32[]{:S(2)}, u32[]{:S(2)}) collective-permute-start(bf16[2,80,256]{2,1,0:T(8,128)(2,1)S(1)} %slice.64), channel_id=1, source_target_pairs={{0,1},{1,2},{2,3},{3,4},{4,5},{5,6},{6,7},{7,0},{8,9},{9,10},{10,1... | collective-permute-start | bytes 245768 | tf_op jit(solution)/shard_map/ppermute | solution.py:28
  24.8 4.0 %collective-permute-start.2 = (bf16[2,80,256]{2,1,0:T(8,128)(2,1)S(1)}, bf16[2,80,256]{2,1,0:T(8,128)(2,1)S(1)}, u32[]{:S(2)}, u32[]{:S(2)}) collective-permute-start(bf16[2,80,256]{2,1,0:T(8,128)(2,1)S(1)} %slice.64), channel_id=1, source_target_pairs={{0,7},{1,0},{2,1},{3,2},{4,3},{5,4},{6,5},{7,6},{8,15},{9,8},{10,9... | collective-permute-start | bytes 245768 | tf_op jit(solution)/shard_map/ppermute | solution.py:28
  28.9 2.3 %collective-permute-done.1 = bf16[2,80,256]{2,1,0:T(8,128)(2,1)S(1)} collective-permute-done((bf16[2,80,256]{2,1,0:T(8,128)(2,1)S(1)}, bf16[2,80,256]{2,1,0:T(8,128)(2,1)S(1)}, u32[]{:S(2)}, u32[]{:S(2)}) %collective-permute-start.1) | collective-permute-done | bytes 81952 | tf_op jit(solution)/shard_map/ppermute | solution.py:28
  31.2 3.3 %collective-permute-start.4 = (bf16[2,80,256]{2,1,0:T(8,128)(2,1)S(1)}, bf16[2,80,256]{2,1,0:T(8,128)(2,1)S(1)}, u32[]{:S(2)}, u32[]{:S(2)}) collective-permute-start(bf16[2,80,256]{2,1,0:T(8,128)(2,1)S(1)} %collective-permute-done.2), channel_id=1, source_target_pairs={{0,7},{1,0},{2,1},{3,2},{4,3},{5,4},{6,5},{7,6},{8,15},{9,8},{10,9... | collective-permute-start | bytes 245768 | tf_op jit(solution)/shard_map/ppermute | solution.py:28
  34.5 2.7 %collective-permute-done.3 = bf16[2,80,256]{2,1,0:T(8,128)(2,1)S(1)} collective-permute-done((bf16[2,80,256]{2,1,0:T(8,128)(2,1)S(1)}, bf16[2,80,256]{2,1,0:T(8,128)(2,1)S(1)}, u32[]{:S(2)}, u32[]{:S(2)}) %collective-permute-start.3) | collective-permute-done | bytes 81952 | tf_op jit(solution)/shard_map/ppermute | solution.py:28
  37.3 0.7 collective-permute-done.4
  38.0 3.7 %collective-permute-start.6 = (bf16[2,80,256]{2,1,0:T(8,128)(2,1)S(1)}, bf16[2,80,256]{2,1,0:T(8,128)(2,1)S(1)}, u32[]{:S(2)}, u32[]{:S(2)}) collective-permute-start(bf16[2,80,256]{2,1,0:T(8,128)(2,1)S(1)} %collective-permute-done.4), channel_id=1, source_target_pairs={{0,7},{1,0},{2,1},{3,2},{4,3},{5,4},{6,5},{7,6},{8,15},{9,8},{10,9... | collective-permute-start | bytes 245768 | tf_op jit(solution)/shard_map/ppermute | solution.py:28
  41.7 4.2 %collective-permute-done.6 = bf16[2,80,256]{2,1,0:T(8,128)(2,1)S(1)} collective-permute-done((bf16[2,80,256]{2,1,0:T(8,128)(2,1)S(1)}, bf16[2,80,256]{2,1,0:T(8,128)(2,1)S(1)}, u32[]{:S(2)}, u32[]{:S(2)}) %collective-permute-start.6) | collective-permute-done | bytes 81952 | tf_op jit(solution)/shard_map/ppermute | solution.py:28
  45.9 3.7 %collective-permute-start.8 = (bf16[2,48,256]{2,1,0:T(8,128)(2,1)S(1)}, bf16[2,48,256]{2,1,0:T(8,128)(2,1)S(1)}, u32[]{:S(2)}, u32[]{:S(2)}) collective-permute-start(bf16[2,48,256]{2,1,0:T(8,128)(2,1)S(1)} %slice.66), channel_id=1, source_target_pairs={{0,7},{1,0},{2,1},{3,2},{4,3},{5,4},{6,5},{7,6},{8,15},{9,8},{10,9... | collective-permute-start | bytes 147464 | tf_op jit(solution)/shard_map/ppermute | solution.py:28
  49.6 5.7 %collective-permute-done.7 = bf16[2,32,256]{2,1,0:T(8,128)(2,1)S(1)} collective-permute-done((bf16[2,32,256]{2,1,0:T(8,128)(2,1)S(1)}, bf16[2,32,256]{2,1,0:T(8,128)(2,1)S(1)}, u32[]{:S(2)}, u32[]{:S(2)}) %collective-permute-start.7) | collective-permute-done | bytes 32800 | tf_op jit(solution)/shard_map/ppermute | solution.py:28
  55.4 0.8 collective-permute-start.10
  56.2 1.9 %collective-permute-start.11 = (bf16[2,8,80,256]{3,2,1,0:T(8,128)(2,1)S(1)}, bf16[2,8,80,256]{3,2,1,0:T(8,128)(2,1)S(1)}, u32[]{:S(2)}, u32[]{:S(2)}) collective-permute-start(bf16[2,8,80,256]{3,2,1,0:T(8,128)(2,1)S(1)} %fusion.8.p0), channel_id=1, source_target_pairs={{0,24},{8,0},{16,8},{24,16},{1,25},{9,1},{17,9},{25,17},{2,26},{10... | collective-permute-start | bytes 1966088 | tf_op jit(solution)/shard_map/ppermute | solution.py:28
  58.1 0.7 collective-permute-start.9
  58.9 3.2 %convert_reduce_fusion = f32[384]{0:T(512)S(1)} fusion(bf16[6144,384]{1,0:T(8,128)(2,1)} %w_in.1), kind=kLoop, calls=%fused_computation | loop fusion | flops 4718208 | bytes 4720128 | tf_op jit(solution)/shard_map/reduce_sum | solution.py:287
  62.1 0.6 broadcast_in_dim.39.col_sum
  62.6 0.6 stack.37.me.refs_0_
  63.2 9.6 %collective-permute-done.10.p2 = bf16[2,8,80,256]{3,2,1,0:T(8,128)(2,1)S(1)} collective-permute-done((bf16[2,8,80,256]{3,2,1,0:T(8,128)(2,1)S(1)}, bf16[2,8,80,256]{3,2,1,0:T(8,128)(2,1)S(1)}, u32[]{:S(2)}, u32[]{:S(2)}) %collective-permute-start.10) | collective-permute-done | bytes 655392 | tf_op jit(solution)/shard_map/ppermute | solution.py:28
  72.8 6.8 %collective-permute-done.11.p3 = bf16[2,8,80,256]{3,2,1,0:T(8,128)(2,1)S(1)} collective-permute-done((bf16[2,8,80,256]{3,2,1,0:T(8,128)(2,1)S(1)}, bf16[2,8,80,256]{3,2,1,0:T(8,128)(2,1)S(1)}, u32[]{:S(2)}, u32[]{:S(2)}) %collective-permute-start.11) | collective-permute-done | bytes 655392 | tf_op jit(solution)/shard_map/ppermute | solution.py:28
  79.7 0.8 copy-done.8
  80.5 0.2 copy-done.9
  80.7 22.9 %shard_map.75 = (bf16[2,8,80,256]{3,2,1,0:T(8,128)(2,1)}, bf16[2,8,80,256]{3,2,1,0:T(8,128)(2,1)}, bf16[2,8,80,256]{3,2,1,0:T(8,128)(2,1)}, bf16[2,8,80,256]{3,2...) custom-call(s32[5]{0:T(128)} %stack.37.me.refs_0_, ...), custom_call_target="tpu_custom_call" | custom-call | flops 7247757312 | bytes 32505856 | tf_op jit(solution)/shard_map/pallas_call | solution.py:294
  103.6 0.1 collective-permute-start.22
  103.7 0.5 collective-permute-start.21
  104.2 0.2 collective-permute-start.18
  104.4 3.6 %collective-permute-start.19 = (bf16[2,8,80,256]{3,2,1,0:T(8,128)(2,1)}, bf16[2,8,80,256]{3,2,1,0:T(8,128)(2,1)}, u32[]{:S(2)}, u32[]{:S(2)}) collective-permute-start(bf16[2,8,80,256]{3,2,1,0:T(8,128)(2,1)} %get-tuple-element.20), channel_id=1, source_target_pairs={{0,16},{8,24},{16,0},{24,8},{1,17},{9,25},{17,1},{25,9},{2,18},{10... | collective-permute-start | bytes 1966088 | tf_op jit(solution)/shard_map/ppermute | solution.py:28
  108.0 2.9 %collective-permute-done.22.refs_1_ = bf16[3072,384]{1,0:T(8,128)(2,1)} collective-permute-done((bf16[3072,384]{1,0:T(8,128)(2,1)}, bf16[3072,384]{1,0:T(8,128)(2,1)}, u32[]{:S(2)}, u32[]{:S(2)}) %collective-permute-start.22) | collective-permute-done | bytes 2359328 | tf_op jit(solution)/shard_map/ppermute | solution.py:28
  110.9 2.7 %shard_map.76 = bf16[768,384]{1,0:T(8,128)(2,1)} custom-call(s32[5]{0:T(128)} %stack.37.me.refs_0_, bf16[3072,384]{1,0:T(8,128)(2,1)} %get-tuple-element.23.refs_0_, bf16[3072,384]{1,0:T(8,128)(2,1)} %collective-permute-done.22.refs_1_), custom_call_target="tpu_custom_call" | custom-call | tf_op jit(solution)/shard_map/pallas_call | solution.py:233
  113.7 1.1 collective-permute-start.23
  114.8 3.6 %shard_map.78 = bf16[2304,384]{1,0:T(8,128)(2,1)} custom-call(s32[5]{0:T(128)} %stack.37.me.refs_0_, bf16[3072,384]{1,0:T(8,128)(2,1)} %get-tuple-element.23.refs_0_, bf16[3072,384]{1,0:T(8,128)(2,1)} %collective-permute-done.22.refs_1_), custom_call_target="tpu_custom_call" | custom-call | tf_op jit(solution)/shard_map/pallas_call | solution.py:233
  118.3 4.2 %collective-permute-done.18.refs_2_ = bf16[2,8,80,256]{3,2,1,0:T(8,128)(2,1)S(1)} collective-permute-done((bf16[2,8,80,256]{3,2,1,0:T(8,128)(2,1)}, bf16[2,8,80,256]{3,2,1,0:T(8,128)(2,1)S(1)}, u32[]{:S(2)}, u32[]{:S(2)}) %collective-permute-start.18) | collective-permute-done | bytes 655392 | tf_op jit(solution)/shard_map/ppermute | solution.py:28
  122.6 0.8 copy-done.3
  123.4 1.0 collective-permute-start.29
  124.4 12.7 %collective-permute-done.19.refs_3_ = bf16[2,8,80,256]{3,2,1,0:T(8,128)(2,1)} collective-permute-done((bf16[2,8,80,256]{3,2,1,0:T(8,128)(2,1)}, bf16[2,8,80,256]{3,2,1,0:T(8,128)(2,1)}, u32[]{:S(2)}, u32[]{:S(2)}) %collective-permute-start.19) | collective-permute-done | bytes 655392 | tf_op jit(solution)/shard_map/ppermute | solution.py:28
  137.2 1.6 copy-done.2
  138.7 1.1 copy-done.4
  139.8 2.3 %shard_map.77 = (f32[4,2,80,256]{3,2,1,0:T(8,128)S(1)}, bf16[4,2,80,256]{3,2,1,0:T(8,128)(2,1)S(1)}) custom-call(s32[5]{0:T(128)S(1)} %copy-done.5, bf16[2,8,80,256]{3,2,1,0:T(8,128)(2,1)S(1)} %copy-done.2, bf16[2,8,80,256]{3,2,1,0:T(8,128)(2,1)S(1)} %copy-done.4, bf16[2,8,80,256]{3,2,1,0:T(8,128)(2,1)} %collective-permute-done.19.refs_3_, ...), custom_call_target="tpu_custom_call" | custom-call | flops 1207959552 | bytes 3604480 | tf_op jit(solution)/shard_map/pallas_call | solution.py:47
  142.2 0.1 collective-permute-start.24
  142.3 14.2 %collective-permute-done.24 = bf16[4,2,80,256]{3,2,1,0:T(8,128)(2,1)S(1)} collective-permute-done((bf16[4,2,80,256]{3,2,1,0:T(8,128)(2,1)S(1)}, bf16[4,2,80,256]{3,2,1,0:T(8,128)(2,1)S(1)}, u32[]{:S(2)}, u32[]{:S(2)}) %collective-permute-start.24) | collective-permute-done | bytes 327712 | tf_op jit(solution)/shard_map/ppermute | solution.py:339
  156.5 0.1 fusion.10
  156.6 2.7 %collective-permute-start.25 = (bf16[2,80,256]{2,1,0:T(8,128)(2,1)S(1)}, bf16[2,80,256]{2,1,0:T(8,128)(2,1)S(1)}, u32[]{:S(2)}, u32[]{:S(2)}) collective-permute-start(bf16[2,80,256]{2,1,0:T(8,128)(2,1)S(1)} %get-tuple-element.35), channel_id=1, source_target_pairs={{0,2},{1,3},{2,4},{3,5},{4,6},{5,7},{6,0},{7,1},{8,10},{9,11},{10,... | collective-permute-start | bytes 245768 | tf_op jit(solution)/shard_map/ppermute | solution.py:28
  159.4 2.9 %collective-permute-start.26 = (bf16[2,80,256]{2,1,0:T(8,128)(2,1)S(1)}, bf16[2,80,256]{2,1,0:T(8,128)(2,1)S(1)}, u32[]{:S(2)}, u32[]{:S(2)}) collective-permute-start(bf16[2,80,256]{2,1,0:T(8,128)(2,1)S(1)} %get-tuple-element.37), channel_id=1, source_target_pairs={{0,4},{1,5},{2,6},{3,7},{4,0},{5,1},{6,2},{7,3},{8,12},{9,13},{10,... | collective-permute-start | bytes 245768 | tf_op jit(solution)/shard_map/ppermute | solution.py:28
  162.3 3.4 %collective-permute-start.27 = (bf16[2,80,256]{2,1,0:T(8,128)(2,1)S(1)}, bf16[2,80,256]{2,1,0:T(8,128)(2,1)S(1)}, u32[]{:S(2)}, u32[]{:S(2)}) collective-permute-start(bf16[2,80,256]{2,1,0:T(8,128)(2,1)S(1)} %get-tuple-element.36), channel_id=1, source_target_pairs={{0,6},{1,7},{2,0},{3,1},{4,2},{5,3},{6,4},{7,5},{8,14},{9,15},{10,... | collective-permute-start | bytes 245768 | tf_op jit(solution)/shard_map/ppermute | solution.py:28
  165.7 1.0 dynamic-slice_bitcast_fusion.2
  166.7 1.5 collective-permute-start.15
  168.3 2.7 %collective-permute-start.16 = (bf16[2,112,256]{2,1,0:T(8,128)(2,1)S(1)}, bf16[2,112,256]{2,1,0:T(8,128)(2,1)S(1)}, u32[]{:S(2)}, u32[]{:S(2)}) collective-permute-start(bf16[2,112,256]{2,1,0:T(8,128)(2,1)S(1)} %get-tuple-element.34), channel_id=1, source_target_pairs={{0,16},{8,24},{16,0},{24,8},{1,17},{9,25},{17,1},{25,9},{2,18},{10... | collective-permute-start | bytes 344072 | tf_op jit(solution)/shard_map/ppermute | solution.py:28
  171.0 1.3 collective-permute-start.17
  172.3 1.7 collective-permute-done.15
  174.0 1.5 collective-permute-done.16
  175.6 0.2 collective-permute-done.17
  175.8 1.0 fusion.1
  176.8 0.9 collective-permute-start.28
  177.7 5.3 %shard_map.79 = (bf16[1536,384]{1,0:T(8,128)(2,1)}, bf16[384,1536]{1,0:T(8,128)(2,1)}) custom-call(s32[5]{0:T(128)} %stack.37.me.refs_0_, bf16[3072,384]{1,0:T(8,128)(2,1)} %get-tuple-element.27.refs_0_, bf16[3072,384]{1,0:T(8,128)(2,1)} %copy-done, bf16[768,384]{1,0:T(8,128)(2,1)} %copy-done.1, bf16[2304,384]{1,0:T(8,128)(2,1)} %collective-permute-done.29.refs_3_), custom_call_target="tpu_custom_call" | custom-call | tf_op jit(solution)/shard_map/pallas_call | solution.py:233
  183.1 0.6 slice_bitcast_fusion.4
  (58 shorter events, 0.5 us)
Async XLA Ops:
  7.2 72.5 %all-gather.2.cloned.1.call-start = ((), (), s32[]{:S(2)}) async-start(), calls=%async_computation.1 | async-start | bytes 4128768 | tf_op jit(solution)/shard_map/all_gather | solution.py:283
  8.1 4.7 %collective-permute-start = (bf16[192,256]{1,0:T(8,128)(2,1)S(1)}, bf16[192,256]{1,0:T(8,128)(2,1)S(1)}, u32[]{:S(2)}, u32[]{:S(2)}) collective-permute-start(bf16[192,256]{1,0:T(8,128)(2,1)S(1)} %get-tuple-element.39), channel_id=1, source_target_pairs={{0,32},{32,0},{1,33},{33,1},{2,34},{34,2},{3,35},{35,3},{4,36},{36... | collective-permute-start | bytes 294920 | tf_op jit(solution)/shard_map/ppermute | solution.py:28
  12.8 7.2 %collective-permute-start.12 = (bf16[2,112,256]{2,1,0:T(8,128)(2,1)S(1)}, bf16[2,112,256]{2,1,0:T(8,128)(2,1)S(1)}, u32[]{:S(2)}, u32[]{:S(2)}) collective-permute-start(bf16[2,112,256]{2,1,0:T(8,128)(2,1)S(1)} %pad_maximum_fusion.2), channel_id=1, source_target_pairs={{0,8},{8,16},{16,24},{24,0},{1,9},{9,17},{17,25},{25,1},{2,10},{10... | collective-permute-start | bytes 344072 | tf_op jit(solution)/shard_map/ppermute | solution.py:28
  14.4 6.9 %collective-permute-start.13 = (bf16[2,112,256]{2,1,0:T(8,128)(2,1)S(1)}, bf16[2,112,256]{2,1,0:T(8,128)(2,1)S(1)}, u32[]{:S(2)}, u32[]{:S(2)}) collective-permute-start(bf16[2,112,256]{2,1,0:T(8,128)(2,1)S(1)} %pad_maximum_fusion.2), channel_id=1, source_target_pairs={{0,16},{8,24},{16,0},{24,8},{1,17},{9,25},{17,1},{25,9},{2,18},{10... | collective-permute-start | bytes 344072 | tf_op jit(solution)/shard_map/ppermute | solution.py:28
  17.1 4.8 %collective-permute-start.14 = (bf16[2,112,256]{2,1,0:T(8,128)(2,1)S(1)}, bf16[2,112,256]{2,1,0:T(8,128)(2,1)S(1)}, u32[]{:S(2)}, u32[]{:S(2)}) collective-permute-start(bf16[2,112,256]{2,1,0:T(8,128)(2,1)S(1)} %pad_maximum_fusion.2), channel_id=1, source_target_pairs={{0,24},{8,0},{16,8},{24,16},{1,25},{9,1},{17,9},{25,17},{2,26},{10... | collective-permute-start | bytes 344072 | tf_op jit(solution)/shard_map/ppermute | solution.py:28
  22.7 142.9 %reduce-scatter.2.cloned.1.call-start = ((), (), s32[]{:S(2)}) async-start(), calls=%async_computation.2 | async-start | bytes 4128768 | tf_op jit(solution)/shard_map/reduce_scatter | solution.py:344
  22.8 8.4 %collective-permute-start.1 = (bf16[2,80,256]{2,1,0:T(8,128)(2,1)S(1)}, bf16[2,80,256]{2,1,0:T(8,128)(2,1)S(1)}, u32[]{:S(2)}, u32[]{:S(2)}) collective-permute-start(bf16[2,80,256]{2,1,0:T(8,128)(2,1)S(1)} %slice.64), channel_id=1, source_target_pairs={{0,1},{1,2},{2,3},{3,4},{4,5},{5,6},{6,7},{7,0},{8,9},{9,10},{10,1... | collective-permute-start | bytes 245768 | tf_op jit(solution)/shard_map/ppermute | solution.py:28
  24.8 6.4 %collective-permute-start.2 = (bf16[2,80,256]{2,1,0:T(8,128)(2,1)S(1)}, bf16[2,80,256]{2,1,0:T(8,128)(2,1)S(1)}, u32[]{:S(2)}, u32[]{:S(2)}) collective-permute-start(bf16[2,80,256]{2,1,0:T(8,128)(2,1)S(1)} %slice.64), channel_id=1, source_target_pairs={{0,7},{1,0},{2,1},{3,2},{4,3},{5,4},{6,5},{7,6},{8,15},{9,8},{10,9... | collective-permute-start | bytes 245768 | tf_op jit(solution)/shard_map/ppermute | solution.py:28
  31.2 6.1 %collective-permute-start.3 = (bf16[2,80,256]{2,1,0:T(8,128)(2,1)S(1)}, bf16[2,80,256]{2,1,0:T(8,128)(2,1)S(1)}, u32[]{:S(2)}, u32[]{:S(2)}) collective-permute-start(bf16[2,80,256]{2,1,0:T(8,128)(2,1)S(1)} %collective-permute-done.1), channel_id=1, source_target_pairs={{0,1},{1,2},{2,3},{3,4},{4,5},{5,6},{6,7},{7,0},{8,9},{9,10},{10,1... | collective-permute-start | bytes 245768 | tf_op jit(solution)/shard_map/ppermute | solution.py:28
  31.2 6.8 %collective-permute-start.4 = (bf16[2,80,256]{2,1,0:T(8,128)(2,1)S(1)}, bf16[2,80,256]{2,1,0:T(8,128)(2,1)S(1)}, u32[]{:S(2)}, u32[]{:S(2)}) collective-permute-start(bf16[2,80,256]{2,1,0:T(8,128)(2,1)S(1)} %collective-permute-done.2), channel_id=1, source_target_pairs={{0,7},{1,0},{2,1},{3,2},{4,3},{5,4},{6,5},{7,6},{8,15},{9,8},{10,9... | collective-permute-start | bytes 245768 | tf_op jit(solution)/shard_map/ppermute | solution.py:28
  37.3 12.3 %collective-permute-start.5 = (bf16[2,80,256]{2,1,0:T(8,128)(2,1)S(1)}, bf16[2,80,256]{2,1,0:T(8,128)(2,1)S(1)}, u32[]{:S(2)}, u32[]{:S(2)}) collective-permute-start(bf16[2,80,256]{2,1,0:T(8,128)(2,1)S(1)} %collective-permute-done.3), channel_id=1, source_target_pairs={{0,1},{1,2},{2,3},{3,4},{4,5},{5,6},{6,7},{7,0},{8,9},{9,10},{10,1... | collective-permute-start | bytes 245768 | tf_op jit(solution)/shard_map/ppermute | solution.py:28
  38.0 7.9 %collective-permute-start.6 = (bf16[2,80,256]{2,1,0:T(8,128)(2,1)S(1)}, bf16[2,80,256]{2,1,0:T(8,128)(2,1)S(1)}, u32[]{:S(2)}, u32[]{:S(2)}) collective-permute-start(bf16[2,80,256]{2,1,0:T(8,128)(2,1)S(1)} %collective-permute-done.4), channel_id=1, source_target_pairs={{0,7},{1,0},{2,1},{3,2},{4,3},{5,4},{6,5},{7,6},{8,15},{9,8},{10,9... | collective-permute-start | bytes 245768 | tf_op jit(solution)/shard_map/ppermute | solution.py:28
  45.9 9.5 %collective-permute-start.8 = (bf16[2,48,256]{2,1,0:T(8,128)(2,1)S(1)}, bf16[2,48,256]{2,1,0:T(8,128)(2,1)S(1)}, u32[]{:S(2)}, u32[]{:S(2)}) collective-permute-start(bf16[2,48,256]{2,1,0:T(8,128)(2,1)S(1)} %slice.66), channel_id=1, source_target_pairs={{0,7},{1,0},{2,1},{3,2},{4,3},{5,4},{6,5},{7,6},{8,15},{9,8},{10,9... | collective-permute-start | bytes 147464 | tf_op jit(solution)/shard_map/ppermute | solution.py:28
  49.6 5.8 %collective-permute-start.7 = (bf16[2,32,256]{2,1,0:T(8,128)(2,1)S(1)}, bf16[2,32,256]{2,1,0:T(8,128)(2,1)S(1)}, u32[]{:S(2)}, u32[]{:S(2)}) collective-permute-start(bf16[2,32,256]{2,1,0:T(8,128)(2,1)S(1)} %slice.65), channel_id=1, source_target_pairs={{0,1},{1,2},{2,3},{3,4},{4,5},{5,6},{6,7},{7,0},{8,9},{9,10},{10,1... | collective-permute-start | bytes 98312 | tf_op jit(solution)/shard_map/ppermute | solution.py:28
  55.4 6.7 %copy-start.6 = (bf16[2,8,80,256]{3,2,1,0:T(8,128)(2,1)}, bf16[2,8,80,256]{3,2,1,0:T(8,128)(2,1)S(1)}, u32[]{:S(2)}) copy-start(bf16[2,8,80,256]{3,2,1,0:T(8,128)(2,1)S(1)} %fusion.8.p0) | copy-start | bytes 1966084
  55.4 17.4 %collective-permute-start.10 = (bf16[2,8,80,256]{3,2,1,0:T(8,128)(2,1)S(1)}, bf16[2,8,80,256]{3,2,1,0:T(8,128)(2,1)S(1)}, u32[]{:S(2)}, u32[]{:S(2)}) collective-permute-start(bf16[2,8,80,256]{3,2,1,0:T(8,128)(2,1)S(1)} %fusion.8.p0), channel_id=1, source_target_pairs={{0,16},{8,24},{16,0},{24,8},{1,17},{9,25},{17,1},{25,9},{2,18},{10... | collective-permute-start | bytes 1966088 | tf_op jit(solution)/shard_map/ppermute | solution.py:28
  56.2 23.4 %collective-permute-start.11 = (bf16[2,8,80,256]{3,2,1,0:T(8,128)(2,1)S(1)}, bf16[2,8,80,256]{3,2,1,0:T(8,128)(2,1)S(1)}, u32[]{:S(2)}, u32[]{:S(2)}) collective-permute-start(bf16[2,8,80,256]{3,2,1,0:T(8,128)(2,1)S(1)} %fusion.8.p0), channel_id=1, source_target_pairs={{0,24},{8,0},{16,8},{24,16},{1,25},{9,1},{17,9},{25,17},{2,26},{10... | collective-permute-start | bytes 1966088 | tf_op jit(solution)/shard_map/ppermute | solution.py:28
  58.1 21.5 %collective-permute-start.9 = (bf16[2,8,80,256]{3,2,1,0:T(8,128)(2,1)S(1)}, bf16[2,8,80,256]{3,2,1,0:T(8,128)(2,1)S(1)}, u32[]{:S(2)}, u32[]{:S(2)}) collective-permute-start(bf16[2,8,80,256]{3,2,1,0:T(8,128)(2,1)S(1)} %fusion.8.p0), channel_id=1, source_target_pairs={{0,8},{8,16},{16,24},{24,0},{1,9},{9,17},{17,25},{25,1},{2,10},{10... | collective-permute-start | bytes 1966088 | tf_op jit(solution)/shard_map/ppermute | solution.py:28
  72.8 6.9 %copy-start.7 = (bf16[2,8,80,256]{3,2,1,0:T(8,128)(2,1)}, bf16[2,8,80,256]{3,2,1,0:T(8,128)(2,1)S(1)}, u32[]{:S(2)}) copy-start(bf16[2,8,80,256]{3,2,1,0:T(8,128)(2,1)S(1)} %collective-permute-done.10.p2) | copy-start | bytes 1966084
  79.6 0.8 copy-start.8
  79.7 1.0 copy-start.9
  103.6 7.3 %collective-permute-start.22 = (bf16[3072,384]{1,0:T(8,128)(2,1)}, bf16[3072,384]{1,0:T(8,128)(2,1)}, u32[]{:S(2)}, u32[]{:S(2)}) collective-permute-start(bf16[3072,384]{1,0:T(8,128)(2,1)} %get-tuple-element.24), channel_id=1, source_target_pairs={{0,64},{64,0},{1,65},{65,1},{2,66},{66,2},{3,67},{67,3},{4,68},{68... | collective-permute-start | bytes 7077896 | tf_op jit(solution)/shard_map/ppermute | solution.py:28
  103.7 33.4 %collective-permute-start.21 = (bf16[3072,384]{1,0:T(8,128)(2,1)}, bf16[3072,384]{1,0:T(8,128)(2,1)S(1)}, u32[]{:S(2)}, u32[]{:S(2)}) collective-permute-start(bf16[3072,384]{1,0:T(8,128)(2,1)} %get-tuple-element.22), channel_id=1, source_target_pairs={{0,64},{64,0},{1,65},{65,1},{2,66},{66,2},{3,67},{67,3},{4,68},{68... | collective-permute-start | bytes 7077896 | tf_op jit(solution)/shard_map/ppermute | solution.py:28
  104.2 18.4 %collective-permute-start.18 = (bf16[2,8,80,256]{3,2,1,0:T(8,128)(2,1)}, bf16[2,8,80,256]{3,2,1,0:T(8,128)(2,1)S(1)}, u32[]{:S(2)}, u32[]{:S(2)}) collective-permute-start(bf16[2,8,80,256]{3,2,1,0:T(8,128)(2,1)} %get-tuple-element.19), channel_id=1, source_target_pairs={{0,8},{8,16},{16,24},{24,0},{1,9},{9,17},{17,25},{25,1},{2,10},{10... | collective-permute-start | bytes 1966088 | tf_op jit(solution)/shard_map/ppermute | solution.py:28
  104.4 32.7 %collective-permute-start.19 = (bf16[2,8,80,256]{3,2,1,0:T(8,128)(2,1)}, bf16[2,8,80,256]{3,2,1,0:T(8,128)(2,1)}, u32[]{:S(2)}, u32[]{:S(2)}) collective-permute-start(bf16[2,8,80,256]{3,2,1,0:T(8,128)(2,1)} %get-tuple-element.20), channel_id=1, source_target_pairs={{0,16},{8,24},{16,0},{24,8},{1,17},{9,25},{17,1},{25,9},{2,18},{10... | collective-permute-start | bytes 1966088 | tf_op jit(solution)/shard_map/ppermute | solution.py:28
  108.0 29.1 %collective-permute-start.20 = (bf16[2,8,80,256]{3,2,1,0:T(8,128)(2,1)}, bf16[2,8,80,256]{3,2,1,0:T(8,128)(2,1)}, u32[]{:S(2)}, u32[]{:S(2)}) collective-permute-start(bf16[2,8,80,256]{3,2,1,0:T(8,128)(2,1)} %get-tuple-element.21), channel_id=1, source_target_pairs={{0,24},{8,0},{16,8},{24,16},{1,25},{9,1},{17,9},{25,17},{2,26},{10... | collective-permute-start | bytes 1966088 | tf_op jit(solution)/shard_map/ppermute | solution.py:28
  113.6 23.5 %copy-start.5 = (s32[5]{0:T(128)S(1)}, s32[5]{0:T(128)}, u32[]{:S(2)}) copy-start(s32[5]{0:T(128)} %stack.37.me.refs_0_) | copy-start | bytes 64
  113.7 23.5 %collective-permute-start.23 = (bf16[768,384]{1,0:T(8,128)(2,1)}, bf16[768,384]{1,0:T(8,128)(2,1)S(1)}, u32[]{:S(2)}, u32[]{:S(2)}) collective-permute-start(bf16[768,384]{1,0:T(8,128)(2,1)} %shard_map.76), channel_id=1, source_target_pairs={{0,128},{128,0},{1,129},{129,1},{2,130},{130,2},{3,131},{131,3},{4... | collective-permute-start | bytes 1769480 | tf_op jit(solution)/shard_map/ppermute | solution.py:28
  122.6 0.8 copy-start.3
  123.4 54.3 %collective-permute-start.29 = (bf16[2304,384]{1,0:T(8,128)(2,1)}, bf16[2304,384]{1,0:T(8,128)(2,1)}, u32[]{:S(2)}, u32[]{:S(2)}) collective-permute-start(bf16[2304,384]{1,0:T(8,128)(2,1)} %shard_map.78), channel_id=1, source_target_pairs={{0,128},{128,0},{1,129},{129,1},{2,130},{130,2},{3,131},{131,3},{4... | collective-permute-start | bytes 5308424 | tf_op jit(solution)/shard_map/ppermute | solution.py:28
  137.1 5.0 %copy-start = (bf16[3072,384]{1,0:T(8,128)(2,1)}, bf16[3072,384]{1,0:T(8,128)(2,1)S(1)}, u32[]{:S(2)}) copy-start(bf16[3072,384]{1,0:T(8,128)(2,1)S(1)} %collective-permute-done.21.refs_5_.refs_1_) | copy-start | bytes 7077892
  137.1 5.0 %copy-start.1 = (bf16[768,384]{1,0:T(8,128)(2,1)}, bf16[768,384]{1,0:T(8,128)(2,1)S(1)}, u32[]{:S(2)}) copy-start(bf16[768,384]{1,0:T(8,128)(2,1)S(1)} %collective-permute-done.23.refs_6_.refs_2_) | copy-start | bytes 1769476
  137.2 1.6 copy-start.2
  138.7 1.1 copy-start.4
  142.2 14.3 %collective-permute-start.24 = (bf16[4,2,80,256]{3,2,1,0:T(8,128)(2,1)S(1)}, bf16[4,2,80,256]{3,2,1,0:T(8,128)(2,1)S(1)}, u32[]{:S(2)}, u32[]{:S(2)}) collective-permute-start(bf16[4,2,80,256]{3,2,1,0:T(8,128)(2,1)S(1)} %get-tuple-element.26), channel_id=1, source_target_pairs={{0,1},{1,0},{2,3},{3,2},{4,5},{5,4},{6,7},{7,6},{8,9},{9,8},{10,11... | collective-permute-start | bytes 983048 | tf_op jit(solution)/shard_map/ppermute | solution.py:339
  156.6 11.6 %collective-permute-start.25 = (bf16[2,80,256]{2,1,0:T(8,128)(2,1)S(1)}, bf16[2,80,256]{2,1,0:T(8,128)(2,1)S(1)}, u32[]{:S(2)}, u32[]{:S(2)}) collective-permute-start(bf16[2,80,256]{2,1,0:T(8,128)(2,1)S(1)} %get-tuple-element.35), channel_id=1, source_target_pairs={{0,2},{1,3},{2,4},{3,5},{4,6},{5,7},{6,0},{7,1},{8,10},{9,11},{10,... | collective-permute-start | bytes 245768 | tf_op jit(solution)/shard_map/ppermute | solution.py:28
  159.4 11.6 %collective-permute-start.26 = (bf16[2,80,256]{2,1,0:T(8,128)(2,1)S(1)}, bf16[2,80,256]{2,1,0:T(8,128)(2,1)S(1)}, u32[]{:S(2)}, u32[]{:S(2)}) collective-permute-start(bf16[2,80,256]{2,1,0:T(8,128)(2,1)S(1)} %get-tuple-element.37), channel_id=1, source_target_pairs={{0,4},{1,5},{2,6},{3,7},{4,0},{5,1},{6,2},{7,3},{8,12},{9,13},{10,... | collective-permute-start | bytes 245768 | tf_op jit(solution)/shard_map/ppermute | solution.py:28
  162.3 10.0 %collective-permute-start.27 = (bf16[2,80,256]{2,1,0:T(8,128)(2,1)S(1)}, bf16[2,80,256]{2,1,0:T(8,128)(2,1)S(1)}, u32[]{:S(2)}, u32[]{:S(2)}) collective-permute-start(bf16[2,80,256]{2,1,0:T(8,128)(2,1)S(1)} %get-tuple-element.36), channel_id=1, source_target_pairs={{0,6},{1,7},{2,0},{3,1},{4,2},{5,3},{6,4},{7,5},{8,14},{9,15},{10,... | collective-permute-start | bytes 245768 | tf_op jit(solution)/shard_map/ppermute | solution.py:28
  166.7 7.3 %collective-permute-start.15 = (bf16[2,112,256]{2,1,0:T(8,128)(2,1)S(1)}, bf16[2,112,256]{2,1,0:T(8,128)(2,1)S(1)}, u32[]{:S(2)}, u32[]{:S(2)}) collective-permute-start(bf16[2,112,256]{2,1,0:T(8,128)(2,1)S(1)} %get-tuple-element.32), channel_id=1, source_target_pairs={{0,8},{8,16},{16,24},{24,0},{1,9},{9,17},{17,25},{25,1},{2,10},{10... | collective-permute-start | bytes 344072 | tf_op jit(solution)/shard_map/ppermute | solution.py:28
  168.3 7.3 %collective-permute-start.16 = (bf16[2,112,256]{2,1,0:T(8,128)(2,1)S(1)}, bf16[2,112,256]{2,1,0:T(8,128)(2,1)S(1)}, u32[]{:S(2)}, u32[]{:S(2)}) collective-permute-start(bf16[2,112,256]{2,1,0:T(8,128)(2,1)S(1)} %get-tuple-element.34), channel_id=1, source_target_pairs={{0,16},{8,24},{16,0},{24,8},{1,17},{9,25},{17,1},{25,9},{2,18},{10... | collective-permute-start | bytes 344072 | tf_op jit(solution)/shard_map/ppermute | solution.py:28
  171.0 4.8 %collective-permute-start.17 = (bf16[2,112,256]{2,1,0:T(8,128)(2,1)S(1)}, bf16[2,112,256]{2,1,0:T(8,128)(2,1)S(1)}, u32[]{:S(2)}, u32[]{:S(2)}) collective-permute-start(bf16[2,112,256]{2,1,0:T(8,128)(2,1)S(1)} %get-tuple-element.33), channel_id=1, source_target_pairs={{0,24},{8,0},{16,8},{24,16},{1,25},{9,1},{17,9},{25,17},{2,26},{10... | collective-permute-start | bytes 344072 | tf_op jit(solution)/shard_map/ppermute | solution.py:28
  176.8 6.2 %collective-permute-start.28 = (bf16[192,256]{1,0:T(8,128)(2,1)S(1)}, bf16[192,256]{1,0:T(8,128)(2,1)S(1)}, u32[]{:S(2)}, u32[]{:S(2)}) collective-permute-start(bf16[192,256]{1,0:T(8,128)(2,1)S(1)} %fusion.7), channel_id=1, source_target_pairs={{0,32},{32,0},{1,33},{33,1},{2,34},{34,2},{3,35},{35,3},{4,36},{36... | collective-permute-start | bytes 294920 | tf_op jit(solution)/shard_map/ppermute | solution.py:28
Sparse Core Ops, SparseCore 0:
  22.9 53.7 all-gather.1
  103.7 52.4 reduce-scatter.1

commit v3 on v2

--- a/solution.py
+++ b/solution.py
@@ -76,9 +76,9 @@
 
 
 def main_body(me, p0, p1, p2, p3, col_sum, w_in, w_out, part, *refs):
-    mlp_outs, (patch, mine, other, away_mine, away_other) = refs[:4], refs[4:9]
-    p_near, in_near, out_near, cot, norm, mlp_stage, rest_stage, patch_stage, grad_stage, acc, grad_acc = refs[9:20]
-    p_sem, rest_sem, in_sem, out_sem, cot_sem, mlp_sem, mlp_rest_sem, patch_sem, grad_sem = refs[20:]
+    mlp_outs, (patch, norm_out, act_out, grad_out) = refs[:4], refs[4:8]
+    p_near, in_near, out_near, cot, norm, mlp_stage, rest_stage, patch_stage, act_near, grad_near, acc, grad_acc = refs[8:20]
+    p_sem, rest_sem, in_sem, out_sem, cot_sem, mlp_sem, mlp_rest_sem, patch_sem, extra_sem = refs[20:]
     first_rows, rest_rows, far_rows = pl.ds(0, NEAR), pl.ds(NEAR, REST), pl.ds(OWN, REST)
 
     def p_copy(t, piece, yl):
@@ -148,20 +148,14 @@
     first = jnp.sum(rounded * col_sum[...].T, axis=0, keepdims=True) / WIDTH
     second = jnp.sum(rounded * hidden, axis=0, keepdims=True) / WIDTH
 
-    grad_to = (away_other, away_mine, other, mine)
-
-    def grad_copy(q):
-        return pltpu.make_async_copy(grad_stage.at[q], grad_to[q], grad_sem.at[q])
-
-    for q in range(4):
-        yh = me[3] if q in (1, 3) else 1 - me[3]
-        core = 1 - me[4] if q < 2 else me[4]
-        blocks = pl.ds((yh * 2 + core) * 2, 2)
-        grad_stage[q, :QUARTER] = dot(norm[blocks].reshape(QUARTER, TOK), grad, 1, 0).astype(low)
-        value = dot(act_t, cot[blocks].reshape(QUARTER, TOK), 1, 1).astype(low)
-        for i in range(4):
-            grad_stage[q, QUARTER + i * HID : QUARTER + (i + 1) * HID] = value[:, i * HID : (i + 1) * HID]
-        grad_copy(q).start()
+    act_near[...] = act_t
+    grad_near[...] = grad
+    extra = [
+        pltpu.make_async_copy(source, to, extra_sem.at[i])
+        for i, (source, to) in enumerate(((norm, norm_out), (act_near, act_out), (grad_near, grad_out)))
+    ]
+    for copy in extra:
+        copy.start()
 
     def patch_copy(t):
         to = patch.at[:, t % 2, (me[0] - t // 2) & 3, pl.ds(0, OWN)]
@@ -195,6 +189,53 @@
         patch_copy(t).wait()
         mlp_copy(t).wait()
         mlp_rest_copy(t).wait()
+    for copy in extra:
+        copy.wait()
+
+
+def weights_body(me, part, norm_in, act_in, grad_in, mine, other, away_mine, away_other, *refs):
+    cot, norm, act_near, grad_near, grad_stage, cot_sem, norm_sem, small_sem, grad_sem = refs
+
+    def spot(q):
+        yh = me[3] if q in (1, 3) else 1 - me[3]
+        return (yh * 2 + (1 - me[4] if q < 2 else me[4])) * 2
+
+    def cot_copy(q, i):
+        j = spot(q) + i
+        source = part.at[:, (me[0] - (j % 4)) & 3, j // 4, pl.ds(0, OWN)]
+        return pltpu.make_async_copy(source, cot.at[2 * q + i], cot_sem.at[2 * q + i])
+
+    def norm_copy(q):
+        return pltpu.make_async_copy(norm_in.at[pl.ds(spot(q), 2)], norm.at[q], norm_sem.at[q])
+
+    small = [
+        pltpu.make_async_copy(grad_in, grad_near, small_sem.at[0]),
+        pltpu.make_async_copy(act_in, act_near, small_sem.at[1]),
+    ]
+    for copy in small:
+        copy.start()
+    for q in range(4):
+        norm_copy(q).start()
+        cot_copy(q, 0).start()
+        cot_copy(q, 1).start()
+    for copy in small:
+        copy.wait()
+    grad, act_t = grad_near[...], act_near[...]
+
+    grad_to = (away_other, away_mine, other, mine)
+
+    def grad_copy(q):
+        return pltpu.make_async_copy(grad_stage.at[q], grad_to[q], grad_sem.at[q])
+
+    for q in range(4):
+        norm_copy(q).wait()
+        grad_stage[q, :QUARTER] = dot(norm[q].reshape(QUARTER, TOK), grad, 1, 0).astype(low)
+        cot_copy(q, 0).wait()
+        cot_copy(q, 1).wait()
+        value = dot(act_t, cot[2 * q : 2 * q + 2].reshape(QUARTER, TOK), 1, 1).astype(low)
+        for i in range(4):
+            grad_stage[q, QUARTER + i * HID : QUARTER + (i + 1) * HID] = value[:, i * HID : (i + 1) * HID]
+        grad_copy(q).start()
     for q in range(4):
         grad_copy(q).wait()
 
@@ -289,9 +330,9 @@
     dma = pltpu.SemaphoreType.DMA
     near, far = pl.BlockSpec(memory_space=pltpu.VMEM), pl.BlockSpec(memory_space=pl.ANY)
     both_rows = 2 * QUARTER
-    shapes = [(2, 8, NEAR, TOK)] * 4 + [(8, 2, 4, FAR, TOK)] + [(both_rows, HID)] * 4
+    shapes = [(2, 8, NEAR, TOK)] * 4 + [(8, 2, 4, FAR, TOK), (8, BLOCK, TOK), (HID, TOK), (TOK, HID)]
     params = pltpu.CompilerParams(vmem_limit_bytes=60 << 20)
-    *mlp_parts, patch_parts, mine, other, away_mine, away_other = pl.pallas_call(
+    *mlp_parts, patch_parts, norm, act_t, grad = pl.pallas_call(
         main_body,
         out_shape=[jax.ShapeDtypeStruct(shape, low) for shape in shapes],
         in_specs=[pl.BlockSpec(memory_space=pltpu.SMEM)] + [far] * 4 + [near] + [far] * 3,
@@ -305,26 +346,58 @@
             pltpu.VMEM((8, 8, NEAR, TOK), low),
             pltpu.VMEM((8, 8, REST, TOK), low),
             pltpu.VMEM((8, 8, OWN, TOK), low),
-            pltpu.VMEM((4, both_rows, HID), low),
+            pltpu.VMEM((HID, TOK), low),
+            pltpu.VMEM((TOK, HID), low),
             pltpu.VMEM((TOK, HID), wide),
             pltpu.VMEM((HID, TOK), wide),
         ]
         + [dma((8,))] * 8
-        + [dma((4,))],
+        + [dma((3,))],
         compiler_params=params,
         cost_estimate=pl.CostEstimate(flops=6 * work, bytes_accessed=31 << 20, transcendentals=0),
     )(scalars, *x_all, col_sum, proj_in, proj_out, c_all)
 
+    mine, other, away_mine, away_other = pl.pallas_call(
+        weights_body,
+        out_shape=[jax.ShapeDtypeStruct((both_rows, HID), low)] * 4,
+        in_specs=[pl.BlockSpec(memory_space=pltpu.SMEM)] + [far] * 4,
+        out_specs=[far] * 4,
+        scratch_shapes=[
+            pltpu.VMEM((8, 8, OWN, TOK), low),
+            pltpu.VMEM((4, 2, BLOCK, TOK), low),
+            pltpu.VMEM((HID, TOK), low),
+            pltpu.VMEM((TOK, HID), low),
+            pltpu.VMEM((4, both_rows, HID), low),
+            dma((8,)),
+            dma((4,)),
+            dma((2,)),
+            dma((4,)),
+        ],
+        compiler_params=params,
+        cost_estimate=pl.CostEstimate(flops=2 * work, bytes_accessed=16 << 20, transcendentals=0),
+    )(scalars, c_all, norm, act_t, grad)
+
     got_other = shift(away_other, "core", 1)
     got_mine = shift(away_mine, "core", 1)
 
 
     starts = range(0, both_rows, HID)
-    backs = []
-    for some in (starts[:2], starts[2:]):
-        plan = [([(0, row), (1, row)], (0, row - some[0], False)) for row in some]
-        (send,) = add_call(scalars, [other, got_other], [(len(some) * HID, HID)], plan)
-        backs.append(shift(send, "yh", 1))
+    head, tail = starts[:2], starts[2:]
+    (send,) = add_call(
+        scalars,
+        [other, got_other],
+        [(len(head) * HID, HID)],
+        [([(0, row), (1, row)], (0, row, False)) for row in head],
+    )
+    backs = [shift(send, "yh", 1)]
+    send, both_mine = add_call(
+        scalars,
+        [other, got_other, mine, got_mine],
+        [(len(tail) * HID, HID), (both_rows, HID)],
+        [([(0, row), (1, row)], (0, row - tail[0], False)) for row in tail]
+        + [([(2, row), (3, row)], (1, row, False)) for row in starts],
+    )
+    backs.append(shift(send, "yh", 1))
 
     mlp_got = [mlp_parts[0]] + [shift(mlp_parts[k], "x", k) for k in range(1, 4)]
     keep, flip = call(
@@ -334,7 +407,7 @@
         [(part, pl.BlockSpec((1, 8, NEAR, TOK), lambda t, me: (t, 0, 0, 0))) for part in mlp_got],
         [((4, 2, NEAR, TOK), kind, pl.BlockSpec((4, 1, NEAR, TOK), lambda t, me: (0, t, 0, 0))) for kind in (wide, low)],
         [pltpu.VMEM((8, NEAR, TOK), wide)],
-        after=[got_mine, backs[0]],
+        after=[both_mine[:16, :128], backs[0]],
     )
     keep = keep + lax.ppermute(flip, "z", [(i, i ^ 1) for i in range(8)]).astype(wide)
     total = keep[0]
@@ -357,9 +430,9 @@
 
     plan = []
     for i, row in enumerate(starts):
-        back = (2, row) if i < 2 else (3, row - starts[2])
-        plan.append(([(0, row), (1, row), back], (i // 4, i % 4 * HID, i > 3)))
-    grad_in, grad_out = add_call(scalars, [mine, got_mine, *backs], [(QUARTER, HID), (HID, QUARTER)], plan)
+        back = (1, row) if i < 2 else (2, row - tail[0])
+        plan.append(([(0, row), back], (i // 4, i % 4 * HID, i > 3)))
+    grad_in, grad_out = add_call(scalars, [both_mine, *backs], [(QUARTER, HID), (HID, QUARTER)], plan)
     return mlp_out, patch_grad, grad_in, grad_out
 
 

time: 192 us -> 188 us (0.979)
  waiting for transfers between devices: 76.8 us -> 68.7 us
  Pallas kernels: 36.8 us -> 44.1 us
  starting transfers between devices: 49 us -> 46.6 us
    pallas_call x0 -> x1, Pallas kernels: none -> 9.35 us  [per_device(): pl.pallas_call(weights_body, out_shape=[jax.ShapeDtypeStruct((both_rows,...]
    ppermute x1, waiting for transfers between devices: 14.2 us -> 8.53 us  [per_device(): lax.ppermute(flip, 'z', [(i, i ^ 1) for i in range(8)]).astype(wide)]
    pallas_call x1, Pallas kernels: 22.9 us -> 20.1 us  [per_device(): pl.pallas_call(main_body, out_shape=[jax.ShapeDtypeStruct(shape, low) for...]
    ppermute x29, starting transfers between devices: 48.9 us -> 46.2 us  [shift(): lax.ppermute(values, axis, [(i, (i + step) % count) for i in range(count)])]
    ppermute x29, waiting for transfers between devices: 62.6 us -> 60.2 us  [shift(): lax.ppermute(values, axis, [(i, (i + step) % count) for i in range(count)])]
    unnamed x20 -> x16, local copies, waits for them, and re-layouts: 4.54 us -> 2.15 us
  transfers between devices with their start and end apart: 32 -> 32, of which waited for: 18 -> 20; matrix products, arithmetic and copies ran while one was open for 4% -> 4% of each run, Pallas kernels for 7% -> 13%
where the time goes in v3:
time: 188 us; the launch traced here: 186 us
  waiting for transfers between devices  68.7 us (37%)
  starting transfers between devices  46.6 us (25%)
  Pallas kernels  44.1 us (23%)
  between operations  14.3 us (8%)
  other arithmetic  6.73 us (4%)
  local copies, waits for them, and re-layouts  5.24 us (3%)
    ppermute x29, waiting for transfers between devices, shift(): lax.ppermute(values, axis, [(i, (i + step) % count) for i in range(count)])  60.2 us
    ppermute x29, starting transfers between devices, shift(): lax.ppermute(values, axis, [(i, (i + step) % count) for i in range(count)])  46.2 us
    pallas_call x1, Pallas kernels, per_device(): pl.pallas_call(main_body, out_shape=[jax.ShapeDtypeStruct(shape, low) for...  20.1 us
    pallas_call x3, Pallas kernels, add_call(): pl.pallas_call(functools.partial(add_body, len(arrays), plan), out_shape=...  13.5 us
    pallas_call x1, Pallas kernels, per_device(): pl.pallas_call(weights_body, out_shape=[jax.ShapeDtypeStruct((both_rows,...  9.35 us
    ppermute x1, waiting for transfers between devices, per_device(): lax.ppermute(flip, 'z', [(i, i ^ 1) for i in range(8)]).astype(wide)  8.53 us
  transfers between devices with their start and end apart: 32, of which 20 were waited for; matrix products, arithmetic and copies ran while one was open for 4% of the time, Pallas kernels for 13%

profile of v3, /device:TPU:24, one launch (start us, length us, event | category | flops | bytes accessed | tf_op | source)
XLA Modules:
  0.0 185.8 jit_solution(11485503364674417003)
XLA Ops:
  7.2 0.8 fusion.9
  8.1 0.8 collective-permute-start
  8.9 3.9 %collective-permute-done = bf16[192,256]{1,0:T(8,128)(2,1)S(1)} collective-permute-done((bf16[192,256]{1,0:T(8,128)(2,1)S(1)}, bf16[192,256]{1,0:T(8,128)(2,1)S(1)}, u32[]{:S(2)}, u32[]{:S(2)}) %collective-permute-start) | collective-permute-done | bytes 98336 | tf_op jit(solution)/shard_map/ppermute | solution.py:28
  12.8 2.8 %collective-permute-start.14 = (bf16[2,112,256]{2,1,0:T(8,128)(2,1)S(1)}, bf16[2,112,256]{2,1,0:T(8,128)(2,1)S(1)}, u32[]{:S(2)}, u32[]{:S(2)}) collective-permute-start(bf16[2,112,256]{2,1,0:T(8,128)(2,1)S(1)} %pad_maximum_fusion.2), channel_id=1, source_target_pairs={{0,24},{8,0},{16,8},{24,16},{1,25},{9,1},{17,9},{25,17},{2,26},{10... | collective-permute-start | bytes 344072 | tf_op jit(solution)/shard_map/ppermute | solution.py:28
  15.7 0.8 collective-permute-start.13
  16.5 0.9 collective-permute-start.12
  17.3 2.3 %collective-permute-done.14 = bf16[2,112,256]{2,1,0:T(8,128)(2,1)S(1)} collective-permute-done((bf16[2,112,256]{2,1,0:T(8,128)(2,1)S(1)}, bf16[2,112,256]{2,1,0:T(8,128)(2,1)S(1)}, u32[]{:S(2)}, u32[]{:S(2)}) %collective-permute-start.14) | collective-permute-done | bytes 114720 | tf_op jit(solution)/shard_map/ppermute | solution.py:28
  19.7 2.4 %collective-permute-done.13 = bf16[2,112,256]{2,1,0:T(8,128)(2,1)S(1)} collective-permute-done((bf16[2,112,256]{2,1,0:T(8,128)(2,1)S(1)}, bf16[2,112,256]{2,1,0:T(8,128)(2,1)S(1)}, u32[]{:S(2)}, u32[]{:S(2)}) %collective-permute-start.13) | collective-permute-done | bytes 114720 | tf_op jit(solution)/shard_map/ppermute | solution.py:28
  22.0 1.2 collective-permute-done.12
  23.2 0.8 pad_maximum_fusion
  24.1 2.0 %collective-permute-start.1 = (bf16[2,80,256]{2,1,0:T(8,128)(2,1)S(1)}, bf16[2,80,256]{2,1,0:T(8,128)(2,1)S(1)}, u32[]{:S(2)}, u32[]{:S(2)}) collective-permute-start(bf16[2,80,256]{2,1,0:T(8,128)(2,1)S(1)} %slice.68), channel_id=1, source_target_pairs={{0,1},{1,2},{2,3},{3,4},{4,5},{5,6},{6,7},{7,0},{8,9},{9,10},{10,1... | collective-permute-start | bytes 245768 | tf_op jit(solution)/shard_map/ppermute | solution.py:28
  26.1 4.0 %collective-permute-start.2 = (bf16[2,80,256]{2,1,0:T(8,128)(2,1)S(1)}, bf16[2,80,256]{2,1,0:T(8,128)(2,1)S(1)}, u32[]{:S(2)}, u32[]{:S(2)}) collective-permute-start(bf16[2,80,256]{2,1,0:T(8,128)(2,1)S(1)} %slice.68), channel_id=1, source_target_pairs={{0,7},{1,0},{2,1},{3,2},{4,3},{5,4},{6,5},{7,6},{8,15},{9,8},{10,9... | collective-permute-start | bytes 245768 | tf_op jit(solution)/shard_map/ppermute | solution.py:28
  30.2 2.3 %collective-permute-done.1 = bf16[2,80,256]{2,1,0:T(8,128)(2,1)S(1)} collective-permute-done((bf16[2,80,256]{2,1,0:T(8,128)(2,1)S(1)}, bf16[2,80,256]{2,1,0:T(8,128)(2,1)S(1)}, u32[]{:S(2)}, u32[]{:S(2)}) %collective-permute-start.1) | collective-permute-done | bytes 81952 | tf_op jit(solution)/shard_map/ppermute | solution.py:28
  32.5 3.4 %collective-permute-start.4 = (bf16[2,80,256]{2,1,0:T(8,128)(2,1)S(1)}, bf16[2,80,256]{2,1,0:T(8,128)(2,1)S(1)}, u32[]{:S(2)}, u32[]{:S(2)}) collective-permute-start(bf16[2,80,256]{2,1,0:T(8,128)(2,1)S(1)} %collective-permute-done.2), channel_id=1, source_target_pairs={{0,7},{1,0},{2,1},{3,2},{4,3},{5,4},{6,5},{7,6},{8,15},{9,8},{10,9... | collective-permute-start | bytes 245768 | tf_op jit(solution)/shard_map/ppermute | solution.py:28
  36.0 3.0 %collective-permute-done.3 = bf16[2,80,256]{2,1,0:T(8,128)(2,1)S(1)} collective-permute-done((bf16[2,80,256]{2,1,0:T(8,128)(2,1)S(1)}, bf16[2,80,256]{2,1,0:T(8,128)(2,1)S(1)}, u32[]{:S(2)}, u32[]{:S(2)}) %collective-permute-start.3) | collective-permute-done | bytes 81952 | tf_op jit(solution)/shard_map/ppermute | solution.py:28
  38.9 1.1 collective-permute-done.4
  40.0 3.7 %collective-permute-start.6 = (bf16[2,80,256]{2,1,0:T(8,128)(2,1)S(1)}, bf16[2,80,256]{2,1,0:T(8,128)(2,1)S(1)}, u32[]{:S(2)}, u32[]{:S(2)}) collective-permute-start(bf16[2,80,256]{2,1,0:T(8,128)(2,1)S(1)} %collective-permute-done.4), channel_id=1, source_target_pairs={{0,7},{1,0},{2,1},{3,2},{4,3},{5,4},{6,5},{7,6},{8,15},{9,8},{10,9... | collective-permute-start | bytes 245768 | tf_op jit(solution)/shard_map/ppermute | solution.py:28
  43.7 2.6 %collective-permute-done.5 = bf16[2,80,256]{2,1,0:T(8,128)(2,1)S(1)} collective-permute-done((bf16[2,80,256]{2,1,0:T(8,128)(2,1)S(1)}, bf16[2,80,256]{2,1,0:T(8,128)(2,1)S(1)}, u32[]{:S(2)}, u32[]{:S(2)}) %collective-permute-start.5) | collective-permute-done | bytes 81952 | tf_op jit(solution)/shard_map/ppermute | solution.py:28
  46.4 1.2 collective-permute-done.6
  47.5 3.7 %collective-permute-start.8 = (bf16[2,48,256]{2,1,0:T(8,128)(2,1)S(1)}, bf16[2,48,256]{2,1,0:T(8,128)(2,1)S(1)}, u32[]{:S(2)}, u32[]{:S(2)}) collective-permute-start(bf16[2,48,256]{2,1,0:T(8,128)(2,1)S(1)} %slice.70), channel_id=1, source_target_pairs={{0,7},{1,0},{2,1},{3,2},{4,3},{5,4},{6,5},{7,6},{8,15},{9,8},{10,9... | collective-permute-start | bytes 147464 | tf_op jit(solution)/shard_map/ppermute | solution.py:28
  51.3 0.9 collective-permute-done.7
  52.1 1.7 collective-permute-done.8
  53.9 0.1 collective-permute-start.11
  54.0 0.1 collective-permute-start.10
  54.1 1.9 %collective-permute-start.9 = (bf16[2,8,80,256]{3,2,1,0:T(8,128)(2,1)S(1)}, bf16[2,8,80,256]{3,2,1,0:T(8,128)(2,1)S(1)}, u32[]{:S(2)}, u32[]{:S(2)}) collective-permute-start(bf16[2,8,80,256]{3,2,1,0:T(8,128)(2,1)S(1)} %fusion.8.p0), channel_id=1, source_target_pairs={{0,8},{8,16},{16,24},{24,0},{1,9},{9,17},{17,25},{25,1},{2,10},{10... | collective-permute-start | bytes 1966088 | tf_op jit(solution)/shard_map/ppermute | solution.py:28
  56.0 3.2 %convert_reduce_fusion = f32[384]{0:T(512)S(1)} fusion(bf16[6144,384]{1,0:T(8,128)(2,1)} %w_in.1), kind=kLoop, calls=%fused_computation | loop fusion | flops 4718208 | bytes 4720128 | tf_op jit(solution)/shard_map/reduce_sum | solution.py:328
  59.2 0.6 broadcast_in_dim.39.col_sum
  59.8 0.6 stack.37.me.refs_0_
  60.4 8.8 %collective-permute-done.11.p3 = bf16[2,8,80,256]{3,2,1,0:T(8,128)(2,1)S(1)} collective-permute-done((bf16[2,8,80,256]{3,2,1,0:T(8,128)(2,1)S(1)}, bf16[2,8,80,256]{3,2,1,0:T(8,128)(2,1)S(1)}, u32[]{:S(2)}, u32[]{:S(2)}) %collective-permute-start.11) | collective-permute-done | bytes 655392 | tf_op jit(solution)/shard_map/ppermute | solution.py:28
  69.3 1.7 collective-permute-done.10.p2
  71.0 6.9 %collective-permute-done.9.p1 = bf16[2,8,80,256]{3,2,1,0:T(8,128)(2,1)S(1)} collective-permute-done((bf16[2,8,80,256]{3,2,1,0:T(8,128)(2,1)S(1)}, bf16[2,8,80,256]{3,2,1,0:T(8,128)(2,1)S(1)}, u32[]{:S(2)}, u32[]{:S(2)}) %collective-permute-start.9) | collective-permute-done | bytes 655392 | tf_op jit(solution)/shard_map/ppermute | solution.py:28
  77.9 0.8 copy-done.7
  78.7 20.1 %shard_map.75 = (bf16[2,8,80,256]{3,2,1,0:T(8,128)(2,1)}, bf16[2,8,80,256]{3,2,1,0:T(8,128)(2,1)}, bf16[2,8,80,256]{3,2,1,0:T(8,128)(2,1)}, bf16[2,8,80,256]{3,2...) custom-call(s32[5]{0:T(128)} %stack.37.me.refs_0_, ...), custom_call_target="tpu_custom_call" | custom-call | flops 7247757312 | bytes 32505856 | tf_op jit(solution)/shard_map/pallas_call | solution.py:335
  98.8 9.4 %shard_map.76 = (bf16[3072,384]{1,0:T(8,128)(2,1)}, bf16[3072,384]{1,0:T(8,128)(2,1)}, bf16[3072,384]{1,0:T(8,128)(2,1)}, bf16[3072,384]{1,0:T(8,128)(2,1)}) custom-call(s32[5]{0:T(128)} %stack.37.me.refs_0_, bf16[8,4,2,112,256]{4,3,2,1,0:T(8,128)(2,1)} %bitcast.87, bf16[8,768,256]{2,1,0:T(8,128)(2,1)} %get-tuple-element.27.norm_in, ...), custom_call_target="tpu_custom_call" | custom-call | flops 2415919104 | bytes 16777216 | tf_op jit(solution)/shard_map/pallas_call | solution.py:360
  108.2 0.1 collective-permute-start.21
  108.3 0.5 collective-permute-start.22
  108.8 2.8 %collective-permute-start.19 = (bf16[2,8,80,256]{3,2,1,0:T(8,128)(2,1)}, bf16[2,8,80,256]{3,2,1,0:T(8,128)(2,1)S(1)}, u32[]{:S(2)}, u32[]{:S(2)}) collective-permute-start(bf16[2,8,80,256]{3,2,1,0:T(8,128)(2,1)} %get-tuple-element.25), channel_id=1, source_target_pairs={{0,16},{8,24},{16,0},{24,8},{1,17},{9,25},{17,1},{25,9},{2,18},{10... | collective-permute-start | bytes 1966088 | tf_op jit(solution)/shard_map/ppermute | solution.py:28
  111.5 0.5 collective-permute-start.20
  112.0 1.1 collective-permute-done.21.refs_1_
  113.1 2.7 %shard_map.78 = bf16[768,384]{1,0:T(8,128)(2,1)} custom-call(s32[5]{0:T(128)} %stack.37.me.refs_0_, bf16[3072,384]{1,0:T(8,128)(2,1)} %get-tuple-element.30.refs_0_, bf16[3072,384]{1,0:T(8,128)(2,1)} %collective-permute-done.21.refs_1_), custom_call_target="tpu_custom_call" | custom-call | tf_op jit(solution)/shard_map/pallas_call | solution.py:274
  115.9 1.5 collective-permute-start.23
  117.4 6.4 %shard_map.77 = (bf16[2304,384]{1,0:T(8,128)(2,1)}, bf16[3072,384]{1,0:T(8,128)(2,1)}) custom-call(s32[5]{0:T(128)} %stack.37.me.refs_0_, bf16[3072,384]{1,0:T(8,128)(2,1)} %get-tuple-element.30.refs_0_, bf16[3072,384]{1,0:T(8,128)(2,1)} %collective-permute-done.21.refs_1_, bf16[3072,384]{1,0:T(8,128)(2,1)} %get-tuple-element.32.refs_2_, ...), custom_call_target="tpu_custom_call" | custom-call | tf_op jit(solution)/shard_map/pallas_call | solution.py:274
  123.8 2.5 %collective-permute-start.29 = (bf16[2304,384]{1,0:T(8,128)(2,1)}, bf16[2304,384]{1,0:T(8,128)(2,1)}, u32[]{:S(2)}, u32[]{:S(2)}) collective-permute-start(bf16[2304,384]{1,0:T(8,128)(2,1)} %get-tuple-element.37), channel_id=1, source_target_pairs={{0,128},{128,0},{1,129},{129,1},{2,130},{130,2},{3,131},{131,3},{4... | collective-permute-start | bytes 5308424 | tf_op jit(solution)/shard_map/ppermute | solution.py:28
  126.3 0.7 slice.58.refs_5_
  126.9 14.0 %collective-permute-done.18.refs_2_ = bf16[2,8,80,256]{3,2,1,0:T(8,128)(2,1)S(1)} collective-permute-done((bf16[2,8,80,256]{3,2,1,0:T(8,128)(2,1)}, bf16[2,8,80,256]{3,2,1,0:T(8,128)(2,1)S(1)}, u32[]{:S(2)}, u32[]{:S(2)}) %collective-permute-start.18) | collective-permute-done | bytes 655392 | tf_op jit(solution)/shard_map/ppermute | solution.py:28
  141.0 0.6 collective-permute-done.20.refs_4_
  141.6 1.3 copy-done.2
  142.9 1.2 shard_map.79
  144.2 0.3 collective-permute-start.24
  144.4 8.5 %collective-permute-done.24 = bf16[4,2,80,256]{3,2,1,0:T(8,128)(2,1)S(1)} collective-permute-done((bf16[4,2,80,256]{3,2,1,0:T(8,128)(2,1)S(1)}, bf16[4,2,80,256]{3,2,1,0:T(8,128)(2,1)S(1)}, u32[]{:S(2)}, u32[]{:S(2)}) %collective-permute-start.24) | collective-permute-done | bytes 327712 | tf_op jit(solution)/shard_map/ppermute | solution.py:412
  153.0 0.1 fusion.10
  153.1 3.8 %collective-permute-start.25 = (bf16[2,80,256]{2,1,0:T(8,128)(2,1)S(1)}, bf16[2,80,256]{2,1,0:T(8,128)(2,1)S(1)}, u32[]{:S(2)}, u32[]{:S(2)}) collective-permute-start(bf16[2,80,256]{2,1,0:T(8,128)(2,1)S(1)} %get-tuple-element.45), channel_id=1, source_target_pairs={{0,2},{1,3},{2,4},{3,5},{4,6},{5,7},{6,0},{7,1},{8,10},{9,11},{10,... | collective-permute-start | bytes 245768 | tf_op jit(solution)/shard_map/ppermute | solution.py:28
  156.9 0.4 collective-permute-start.27
  157.3 3.9 %collective-permute-start.26 = (bf16[2,80,256]{2,1,0:T(8,128)(2,1)S(1)}, bf16[2,80,256]{2,1,0:T(8,128)(2,1)S(1)}, u32[]{:S(2)}, u32[]{:S(2)}) collective-permute-start(bf16[2,80,256]{2,1,0:T(8,128)(2,1)S(1)} %get-tuple-element.47), channel_id=1, source_target_pairs={{0,4},{1,5},{2,6},{3,7},{4,0},{5,1},{6,2},{7,3},{8,12},{9,13},{10,... | collective-permute-start | bytes 245768 | tf_op jit(solution)/shard_map/ppermute | solution.py:28
  161.2 1.0 dynamic-slice_bitcast_fusion.2
  162.3 1.5 collective-permute-start.15
  163.8 1.8 collective-permute-start.17
  165.6 1.8 collective-permute-start.16
  167.4 2.1 %collective-permute-done.15 = bf16[2,112,256]{2,1,0:T(8,128)(2,1)S(1)} collective-permute-done((bf16[2,112,256]{2,1,0:T(8,128)(2,1)S(1)}, bf16[2,112,256]{2,1,0:T(8,128)(2,1)S(1)}, u32[]{:S(2)}, u32[]{:S(2)}) %collective-permute-start.15) | collective-permute-done | bytes 114720 | tf_op jit(solution)/shard_map/ppermute | solution.py:28
  169.5 2.4 %collective-permute-done.16 = bf16[2,112,256]{2,1,0:T(8,128)(2,1)S(1)} collective-permute-done((bf16[2,112,256]{2,1,0:T(8,128)(2,1)S(1)}, bf16[2,112,256]{2,1,0:T(8,128)(2,1)S(1)}, u32[]{:S(2)}, u32[]{:S(2)}) %collective-permute-start.16) | collective-permute-done | bytes 114720 | tf_op jit(solution)/shard_map/ppermute | solution.py:28
  171.9 1.0 fusion.1
  172.9 0.9 collective-permute-start.28
  173.8 4.4 %shard_map.80 = (bf16[1536,384]{1,0:T(8,128)(2,1)}, bf16[384,1536]{1,0:T(8,128)(2,1)}) custom-call(s32[5]{0:T(128)} %stack.37.me.refs_0_, bf16[3072,384]{1,0:T(8,128)(2,1)} %get-tuple-element.34.refs_0_, bf16[768,384]{1,0:T(8,128)(2,1)} %copy-done, bf16[2304,384]{1,0:T(8,128)(2,1)} %collective-permute-done.29.refs_2_), custom_call_target="tpu_custom_call" | custom-call | tf_op jit(solution)/shard_map/pallas_call | solution.py:274
  178.3 0.6 slice_bitcast_fusion.4
  (56 shorter events, 0.5 us)
Async XLA Ops:
  7.2 70.7 %all-gather.2.cloned.1.call-start = ((), (), s32[]{:S(2)}) async-start(), calls=%async_computation.1 | async-start | bytes 4128768 | tf_op jit(solution)/shard_map/all_gather | solution.py:324
  8.1 4.7 %collective-permute-start = (bf16[192,256]{1,0:T(8,128)(2,1)S(1)}, bf16[192,256]{1,0:T(8,128)(2,1)S(1)}, u32[]{:S(2)}, u32[]{:S(2)}) collective-permute-start(bf16[192,256]{1,0:T(8,128)(2,1)S(1)} %get-tuple-element.49), channel_id=1, source_target_pairs={{0,32},{32,0},{1,33},{33,1},{2,34},{34,2},{3,35},{35,3},{4,36},{36... | collective-permute-start | bytes 294920 | tf_op jit(solution)/shard_map/ppermute | solution.py:28
  12.8 6.8 %collective-permute-start.14 = (bf16[2,112,256]{2,1,0:T(8,128)(2,1)S(1)}, bf16[2,112,256]{2,1,0:T(8,128)(2,1)S(1)}, u32[]{:S(2)}, u32[]{:S(2)}) collective-permute-start(bf16[2,112,256]{2,1,0:T(8,128)(2,1)S(1)} %pad_maximum_fusion.2), channel_id=1, source_target_pairs={{0,24},{8,0},{16,8},{24,16},{1,25},{9,1},{17,9},{25,17},{2,26},{10... | collective-permute-start | bytes 344072 | tf_op jit(solution)/shard_map/ppermute | solution.py:28
  15.7 6.4 %collective-permute-start.13 = (bf16[2,112,256]{2,1,0:T(8,128)(2,1)S(1)}, bf16[2,112,256]{2,1,0:T(8,128)(2,1)S(1)}, u32[]{:S(2)}, u32[]{:S(2)}) collective-permute-start(bf16[2,112,256]{2,1,0:T(8,128)(2,1)S(1)} %pad_maximum_fusion.2), channel_id=1, source_target_pairs={{0,16},{8,24},{16,0},{24,8},{1,17},{9,25},{17,1},{25,9},{2,18},{10... | collective-permute-start | bytes 344072 | tf_op jit(solution)/shard_map/ppermute | solution.py:28
  16.5 6.7 %collective-permute-start.12 = (bf16[2,112,256]{2,1,0:T(8,128)(2,1)S(1)}, bf16[2,112,256]{2,1,0:T(8,128)(2,1)S(1)}, u32[]{:S(2)}, u32[]{:S(2)}) collective-permute-start(bf16[2,112,256]{2,1,0:T(8,128)(2,1)S(1)} %pad_maximum_fusion.2), channel_id=1, source_target_pairs={{0,8},{8,16},{16,24},{24,0},{1,9},{9,17},{17,25},{25,1},{2,10},{10... | collective-permute-start | bytes 344072 | tf_op jit(solution)/shard_map/ppermute | solution.py:28
  24.1 137.2 %reduce-scatter.2.cloned.1.call-start = ((), (), s32[]{:S(2)}) async-start(), calls=%async_computation.2 | async-start | bytes 4128768 | tf_op jit(solution)/shard_map/reduce_scatter | solution.py:417
  24.1 8.4 %collective-permute-start.1 = (bf16[2,80,256]{2,1,0:T(8,128)(2,1)S(1)}, bf16[2,80,256]{2,1,0:T(8,128)(2,1)S(1)}, u32[]{:S(2)}, u32[]{:S(2)}) collective-permute-start(bf16[2,80,256]{2,1,0:T(8,128)(2,1)S(1)} %slice.68), channel_id=1, source_target_pairs={{0,1},{1,2},{2,3},{3,4},{4,5},{5,6},{6,7},{7,0},{8,9},{9,10},{10,1... | collective-permute-start | bytes 245768 | tf_op jit(solution)/shard_map/ppermute | solution.py:28
  26.1 6.4 %collective-permute-start.2 = (bf16[2,80,256]{2,1,0:T(8,128)(2,1)S(1)}, bf16[2,80,256]{2,1,0:T(8,128)(2,1)S(1)}, u32[]{:S(2)}, u32[]{:S(2)}) collective-permute-start(bf16[2,80,256]{2,1,0:T(8,128)(2,1)S(1)} %slice.68), channel_id=1, source_target_pairs={{0,7},{1,0},{2,1},{3,2},{4,3},{5,4},{6,5},{7,6},{8,15},{9,8},{10,9... | collective-permute-start | bytes 245768 | tf_op jit(solution)/shard_map/ppermute | solution.py:28
  32.5 6.4 %collective-permute-start.3 = (bf16[2,80,256]{2,1,0:T(8,128)(2,1)S(1)}, bf16[2,80,256]{2,1,0:T(8,128)(2,1)S(1)}, u32[]{:S(2)}, u32[]{:S(2)}) collective-permute-start(bf16[2,80,256]{2,1,0:T(8,128)(2,1)S(1)} %collective-permute-done.1), channel_id=1, source_target_pairs={{0,1},{1,2},{2,3},{3,4},{4,5},{5,6},{6,7},{7,0},{8,9},{9,10},{10,1... | collective-permute-start | bytes 245768 | tf_op jit(solution)/shard_map/ppermute | solution.py:28
  32.5 7.5 %collective-permute-start.4 = (bf16[2,80,256]{2,1,0:T(8,128)(2,1)S(1)}, bf16[2,80,256]{2,1,0:T(8,128)(2,1)S(1)}, u32[]{:S(2)}, u32[]{:S(2)}) collective-permute-start(bf16[2,80,256]{2,1,0:T(8,128)(2,1)S(1)} %collective-permute-done.2), channel_id=1, source_target_pairs={{0,7},{1,0},{2,1},{3,2},{4,3},{5,4},{6,5},{7,6},{8,15},{9,8},{10,9... | collective-permute-start | bytes 245768 | tf_op jit(solution)/shard_map/ppermute | solution.py:28
  38.9 7.4 %collective-permute-start.5 = (bf16[2,80,256]{2,1,0:T(8,128)(2,1)S(1)}, bf16[2,80,256]{2,1,0:T(8,128)(2,1)S(1)}, u32[]{:S(2)}, u32[]{:S(2)}) collective-permute-start(bf16[2,80,256]{2,1,0:T(8,128)(2,1)S(1)} %collective-permute-done.3), channel_id=1, source_target_pairs={{0,1},{1,2},{2,3},{3,4},{4,5},{5,6},{6,7},{7,0},{8,9},{9,10},{10,1... | collective-permute-start | bytes 245768 | tf_op jit(solution)/shard_map/ppermute | solution.py:28
  40.0 7.5 %collective-permute-start.6 = (bf16[2,80,256]{2,1,0:T(8,128)(2,1)S(1)}, bf16[2,80,256]{2,1,0:T(8,128)(2,1)S(1)}, u32[]{:S(2)}, u32[]{:S(2)}) collective-permute-start(bf16[2,80,256]{2,1,0:T(8,128)(2,1)S(1)} %collective-permute-done.4), channel_id=1, source_target_pairs={{0,7},{1,0},{2,1},{3,2},{4,3},{5,4},{6,5},{7,6},{8,15},{9,8},{10,9... | collective-permute-start | bytes 245768 | tf_op jit(solution)/shard_map/ppermute | solution.py:28
  46.4 5.8 %collective-permute-start.7 = (bf16[2,32,256]{2,1,0:T(8,128)(2,1)S(1)}, bf16[2,32,256]{2,1,0:T(8,128)(2,1)S(1)}, u32[]{:S(2)}, u32[]{:S(2)}) collective-permute-start(bf16[2,32,256]{2,1,0:T(8,128)(2,1)S(1)} %slice.69), channel_id=1, source_target_pairs={{0,1},{1,2},{2,3},{3,4},{4,5},{5,6},{6,7},{7,0},{8,9},{9,10},{10,1... | collective-permute-start | bytes 98312 | tf_op jit(solution)/shard_map/ppermute | solution.py:28
  47.5 6.3 %collective-permute-start.8 = (bf16[2,48,256]{2,1,0:T(8,128)(2,1)S(1)}, bf16[2,48,256]{2,1,0:T(8,128)(2,1)S(1)}, u32[]{:S(2)}, u32[]{:S(2)}) collective-permute-start(bf16[2,48,256]{2,1,0:T(8,128)(2,1)S(1)} %slice.70), channel_id=1, source_target_pairs={{0,7},{1,0},{2,1},{3,2},{4,3},{5,4},{6,5},{7,6},{8,15},{9,8},{10,9... | collective-permute-start | bytes 147464 | tf_op jit(solution)/shard_map/ppermute | solution.py:28
  53.9 5.3 %copy-start.3 = (bf16[2,8,80,256]{3,2,1,0:T(8,128)(2,1)}, bf16[2,8,80,256]{3,2,1,0:T(8,128)(2,1)S(1)}, u32[]{:S(2)}) copy-start(bf16[2,8,80,256]{3,2,1,0:T(8,128)(2,1)S(1)} %fusion.8.p0) | copy-start | bytes 1966084
  53.9 15.4 %collective-permute-start.11 = (bf16[2,8,80,256]{3,2,1,0:T(8,128)(2,1)S(1)}, bf16[2,8,80,256]{3,2,1,0:T(8,128)(2,1)S(1)}, u32[]{:S(2)}, u32[]{:S(2)}) collective-permute-start(bf16[2,8,80,256]{3,2,1,0:T(8,128)(2,1)S(1)} %fusion.8.p0), channel_id=1, source_target_pairs={{0,24},{8,0},{16,8},{24,16},{1,25},{9,1},{17,9},{25,17},{2,26},{10... | collective-permute-start | bytes 1966088 | tf_op jit(solution)/shard_map/ppermute | solution.py:28
  54.0 17.0 %collective-permute-start.10 = (bf16[2,8,80,256]{3,2,1,0:T(8,128)(2,1)S(1)}, bf16[2,8,80,256]{3,2,1,0:T(8,128)(2,1)S(1)}, u32[]{:S(2)}, u32[]{:S(2)}) collective-permute-start(bf16[2,8,80,256]{3,2,1,0:T(8,128)(2,1)S(1)} %fusion.8.p0), channel_id=1, source_target_pairs={{0,16},{8,24},{16,0},{24,8},{1,17},{9,25},{17,1},{25,9},{2,18},{10... | collective-permute-start | bytes 1966088 | tf_op jit(solution)/shard_map/ppermute | solution.py:28
  54.1 23.8 %collective-permute-start.9 = (bf16[2,8,80,256]{3,2,1,0:T(8,128)(2,1)S(1)}, bf16[2,8,80,256]{3,2,1,0:T(8,128)(2,1)S(1)}, u32[]{:S(2)}, u32[]{:S(2)}) collective-permute-start(bf16[2,8,80,256]{3,2,1,0:T(8,128)(2,1)S(1)} %fusion.8.p0), channel_id=1, source_target_pairs={{0,8},{8,16},{16,24},{24,0},{1,9},{9,17},{17,25},{25,1},{2,10},{10... | collective-permute-start | bytes 1966088 | tf_op jit(solution)/shard_map/ppermute | solution.py:28
  69.3 8.6 %copy-start.5 = (bf16[2,8,80,256]{3,2,1,0:T(8,128)(2,1)}, bf16[2,8,80,256]{3,2,1,0:T(8,128)(2,1)S(1)}, u32[]{:S(2)}) copy-start(bf16[2,8,80,256]{3,2,1,0:T(8,128)(2,1)S(1)} %collective-permute-done.11.p3) | copy-start | bytes 1966084
  71.0 6.9 %copy-start.6 = (bf16[2,8,80,256]{3,2,1,0:T(8,128)(2,1)}, bf16[2,8,80,256]{3,2,1,0:T(8,128)(2,1)S(1)}, u32[]{:S(2)}) copy-start(bf16[2,8,80,256]{3,2,1,0:T(8,128)(2,1)S(1)} %collective-permute-done.10.p2) | copy-start | bytes 1966084
  77.9 0.8 copy-start.7
  98.8 12.7 %copy-start.4 = (bf16[2,8,80,256]{3,2,1,0:T(8,128)(2,1)S(1)}, bf16[2,8,80,256]{3,2,1,0:T(8,128)(2,1)}, u32[]{:S(2)}) copy-start(bf16[2,8,80,256]{3,2,1,0:T(8,128)(2,1)} %get-tuple-element.26) | copy-start | bytes 1966084
  108.2 5.0 %collective-permute-start.21 = (bf16[3072,384]{1,0:T(8,128)(2,1)}, bf16[3072,384]{1,0:T(8,128)(2,1)}, u32[]{:S(2)}, u32[]{:S(2)}) collective-permute-start(bf16[3072,384]{1,0:T(8,128)(2,1)} %get-tuple-element.31), channel_id=1, source_target_pairs={{0,64},{64,0},{1,65},{65,1},{2,66},{66,2},{3,67},{67,3},{4,68},{68... | collective-permute-start | bytes 7077896 | tf_op jit(solution)/shard_map/ppermute | solution.py:28
  108.3 9.1 %collective-permute-start.22 = (bf16[3072,384]{1,0:T(8,128)(2,1)}, bf16[3072,384]{1,0:T(8,128)(2,1)}, u32[]{:S(2)}, u32[]{:S(2)}) collective-permute-start(bf16[3072,384]{1,0:T(8,128)(2,1)} %get-tuple-element.33), channel_id=1, source_target_pairs={{0,64},{64,0},{1,65},{65,1},{2,66},{66,2},{3,67},{67,3},{4,68},{68... | collective-permute-start | bytes 7077896 | tf_op jit(solution)/shard_map/ppermute | solution.py:28
  108.8 32.2 %collective-permute-start.18 = (bf16[2,8,80,256]{3,2,1,0:T(8,128)(2,1)}, bf16[2,8,80,256]{3,2,1,0:T(8,128)(2,1)S(1)}, u32[]{:S(2)}, u32[]{:S(2)}) collective-permute-start(bf16[2,8,80,256]{3,2,1,0:T(8,128)(2,1)} %get-tuple-element.24), channel_id=1, source_target_pairs={{0,8},{8,16},{16,24},{24,0},{1,9},{9,17},{17,25},{25,1},{2,10},{10... | collective-permute-start | bytes 1966088 | tf_op jit(solution)/shard_map/ppermute | solution.py:28
  108.8 32.2 %collective-permute-start.19 = (bf16[2,8,80,256]{3,2,1,0:T(8,128)(2,1)}, bf16[2,8,80,256]{3,2,1,0:T(8,128)(2,1)S(1)}, u32[]{:S(2)}, u32[]{:S(2)}) collective-permute-start(bf16[2,8,80,256]{3,2,1,0:T(8,128)(2,1)} %get-tuple-element.25), channel_id=1, source_target_pairs={{0,16},{8,24},{16,0},{24,8},{1,17},{9,25},{17,1},{25,9},{2,18},{10... | collective-permute-start | bytes 1966088 | tf_op jit(solution)/shard_map/ppermute | solution.py:28
  111.5 30.1 %collective-permute-start.20 = (bf16[2,8,80,256]{3,2,1,0:T(8,128)(2,1)S(1)}, bf16[2,8,80,256]{3,2,1,0:T(8,128)(2,1)S(1)}, u32[]{:S(2)}, u32[]{:S(2)}) collective-permute-start(bf16[2,8,80,256]{3,2,1,0:T(8,128)(2,1)S(1)} %copy-done.4), channel_id=1, source_target_pairs={{0,24},{8,0},{16,8},{24,16},{1,25},{9,1},{17,9},{25,17},{2,26},{10... | collective-permute-start | bytes 1966088 | tf_op jit(solution)/shard_map/ppermute | solution.py:28
  115.9 25.7 %collective-permute-start.23 = (bf16[768,384]{1,0:T(8,128)(2,1)}, bf16[768,384]{1,0:T(8,128)(2,1)S(1)}, u32[]{:S(2)}, u32[]{:S(2)}) collective-permute-start(bf16[768,384]{1,0:T(8,128)(2,1)} %shard_map.78), channel_id=1, source_target_pairs={{0,128},{128,0},{1,129},{129,1},{2,130},{130,2},{3,131},{131,3},{4... | collective-permute-start | bytes 1769480 | tf_op jit(solution)/shard_map/ppermute | solution.py:28
  117.4 24.2 %copy-start.1 = (s32[5]{0:T(128)S(1)}, s32[5]{0:T(128)}, u32[]{:S(2)}) copy-start(s32[5]{0:T(128)} %stack.37.me.refs_0_) | copy-start | bytes 64
  123.8 50.0 %collective-permute-start.29 = (bf16[2304,384]{1,0:T(8,128)(2,1)}, bf16[2304,384]{1,0:T(8,128)(2,1)}, u32[]{:S(2)}, u32[]{:S(2)}) collective-permute-start(bf16[2304,384]{1,0:T(8,128)(2,1)} %get-tuple-element.37), channel_id=1, source_target_pairs={{0,128},{128,0},{1,129},{129,1},{2,130},{130,2},{3,131},{131,3},{4... | collective-permute-start | bytes 5308424 | tf_op jit(solution)/shard_map/ppermute | solution.py:28
  141.6 11.5 %copy-start = (bf16[768,384]{1,0:T(8,128)(2,1)}, bf16[768,384]{1,0:T(8,128)(2,1)S(1)}, u32[]{:S(2)}) copy-start(bf16[768,384]{1,0:T(8,128)(2,1)S(1)} %collective-permute-done.23.refs_6_.refs_1_) | copy-start | bytes 1769476
  141.6 1.3 copy-start.2
  144.2 8.8 %collective-permute-start.24 = (bf16[4,2,80,256]{3,2,1,0:T(8,128)(2,1)S(1)}, bf16[4,2,80,256]{3,2,1,0:T(8,128)(2,1)S(1)}, u32[]{:S(2)}, u32[]{:S(2)}) collective-permute-start(bf16[4,2,80,256]{3,2,1,0:T(8,128)(2,1)S(1)} %get-tuple-element.36), channel_id=1, source_target_pairs={{0,1},{1,0},{2,3},{3,2},{4,5},{5,4},{6,7},{7,6},{8,9},{9,8},{10,11... | collective-permute-start | bytes 983048 | tf_op jit(solution)/shard_map/ppermute | solution.py:412
  153.1 10.7 %collective-permute-start.25 = (bf16[2,80,256]{2,1,0:T(8,128)(2,1)S(1)}, bf16[2,80,256]{2,1,0:T(8,128)(2,1)S(1)}, u32[]{:S(2)}, u32[]{:S(2)}) collective-permute-start(bf16[2,80,256]{2,1,0:T(8,128)(2,1)S(1)} %get-tuple-element.45), channel_id=1, source_target_pairs={{0,2},{1,3},{2,4},{3,5},{4,6},{5,7},{6,0},{7,1},{8,10},{9,11},{10,... | collective-permute-start | bytes 245768 | tf_op jit(solution)/shard_map/ppermute | solution.py:28
  156.9 8.7 %collective-permute-start.27 = (bf16[2,80,256]{2,1,0:T(8,128)(2,1)S(1)}, bf16[2,80,256]{2,1,0:T(8,128)(2,1)S(1)}, u32[]{:S(2)}, u32[]{:S(2)}) collective-permute-start(bf16[2,80,256]{2,1,0:T(8,128)(2,1)S(1)} %get-tuple-element.46), channel_id=1, source_target_pairs={{0,6},{1,7},{2,0},{3,1},{4,2},{5,3},{6,4},{7,5},{8,14},{9,15},{10,... | collective-permute-start | bytes 245768 | tf_op jit(solution)/shard_map/ppermute | solution.py:28
  157.3 10.0 %collective-permute-start.26 = (bf16[2,80,256]{2,1,0:T(8,128)(2,1)S(1)}, bf16[2,80,256]{2,1,0:T(8,128)(2,1)S(1)}, u32[]{:S(2)}, u32[]{:S(2)}) collective-permute-start(bf16[2,80,256]{2,1,0:T(8,128)(2,1)S(1)} %get-tuple-element.47), channel_id=1, source_target_pairs={{0,4},{1,5},{2,6},{3,7},{4,0},{5,1},{6,2},{7,3},{8,12},{9,13},{10,... | collective-permute-start | bytes 245768 | tf_op jit(solution)/shard_map/ppermute | solution.py:28
  162.3 7.3 %collective-permute-start.15 = (bf16[2,112,256]{2,1,0:T(8,128)(2,1)S(1)}, bf16[2,112,256]{2,1,0:T(8,128)(2,1)S(1)}, u32[]{:S(2)}, u32[]{:S(2)}) collective-permute-start(bf16[2,112,256]{2,1,0:T(8,128)(2,1)S(1)} %get-tuple-element.42), channel_id=1, source_target_pairs={{0,8},{8,16},{16,24},{24,0},{1,9},{9,17},{17,25},{25,1},{2,10},{10... | collective-permute-start | bytes 344072 | tf_op jit(solution)/shard_map/ppermute | solution.py:28
  163.8 5.7 %collective-permute-start.17 = (bf16[2,112,256]{2,1,0:T(8,128)(2,1)S(1)}, bf16[2,112,256]{2,1,0:T(8,128)(2,1)S(1)}, u32[]{:S(2)}, u32[]{:S(2)}) collective-permute-start(bf16[2,112,256]{2,1,0:T(8,128)(2,1)S(1)} %get-tuple-element.43), channel_id=1, source_target_pairs={{0,24},{8,0},{16,8},{24,16},{1,25},{9,1},{17,9},{25,17},{2,26},{10... | collective-permute-start | bytes 344072 | tf_op jit(solution)/shard_map/ppermute | solution.py:28
  165.6 6.3 %collective-permute-start.16 = (bf16[2,112,256]{2,1,0:T(8,128)(2,1)S(1)}, bf16[2,112,256]{2,1,0:T(8,128)(2,1)S(1)}, u32[]{:S(2)}, u32[]{:S(2)}) collective-permute-start(bf16[2,112,256]{2,1,0:T(8,128)(2,1)S(1)} %get-tuple-element.44), channel_id=1, source_target_pairs={{0,16},{8,24},{16,0},{24,8},{1,17},{9,25},{17,1},{25,9},{2,18},{10... | collective-permute-start | bytes 344072 | tf_op jit(solution)/shard_map/ppermute | solution.py:28
  172.9 5.3 %collective-permute-start.28 = (bf16[192,256]{1,0:T(8,128)(2,1)S(1)}, bf16[192,256]{1,0:T(8,128)(2,1)S(1)}, u32[]{:S(2)}, u32[]{:S(2)}) collective-permute-start(bf16[192,256]{1,0:T(8,128)(2,1)S(1)} %fusion.7), channel_id=1, source_target_pairs={{0,32},{32,0},{1,33},{33,1},{2,34},{34,2},{3,35},{35,3},{4,36},{36... | collective-permute-start | bytes 294920 | tf_op jit(solution)/shard_map/ppermute | solution.py:28
Sparse Core Ops, SparseCore 0:
  24.2 51.9 all-gather.1
  98.9 48.8 reduce-scatter.1

commit v4 on v3

--- a/solution.py
+++ b/solution.py
@@ -103,9 +103,6 @@
         rest_copy(t).start()
     for t in range(8):
         in_copy(t).start()
-    for j in range(8):
-        out_copy(j).start()
-        cot_copy(j).start()
     acc[...] = jnp.zeros_like(acc)
     grad_acc[...] = jnp.zeros_like(grad_acc)
 
@@ -117,6 +114,9 @@
 
     zero = jnp.zeros((1, TOK), wide)
     sums = lax.fori_loop(0, 8, sums_step, (zero, zero))
+    for j in range(8):
+        out_copy(j).start()
+        cot_copy(j).start()
     mean = sums[0] / WIDTH
     rstd = lax.rsqrt(sums[1] / WIDTH - mean * mean + eps)
 

time: 188 us -> 186 us (0.989)
  Pallas kernels: 44.1 us -> 42.2 us
    pallas_call x1, Pallas kernels: 20.1 us -> 18.1 us  [per_device(): pl.pallas_call(main_body, out_shape=[jax.ShapeDtypeStruct(shape, low) for...]
where the time goes in v4:
time: 186 us; the launch traced here: 184 us
  waiting for transfers between devices  68.7 us (37%)
  starting transfers between devices  46.6 us (25%)
  Pallas kernels  42.2 us (23%)
  between operations  14.3 us (8%)
  other arithmetic  6.73 us (4%)
  local copies, waits for them, and re-layouts  5.24 us (3%)
    ppermute x29, waiting for transfers between devices, shift(): lax.ppermute(values, axis, [(i, (i + step) % count) for i in range(count)])  60.2 us
    ppermute x29, starting transfers between devices, shift(): lax.ppermute(values, axis, [(i, (i + step) % count) for i in range(count)])  46.2 us
    pallas_call x1, Pallas kernels, per_device(): pl.pallas_call(main_body, out_shape=[jax.ShapeDtypeStruct(shape, low) for...  18.1 us
    pallas_call x3, Pallas kernels, add_call(): pl.pallas_call(functools.partial(add_body, len(arrays), plan), out_shape=...  13.5 us
    pallas_call x1, Pallas kernels, per_device(): pl.pallas_call(weights_body, out_shape=[jax.ShapeDtypeStruct((both_rows,...  9.35 us
    ppermute x1, waiting for transfers between devices, per_device(): lax.ppermute(flip, 'z', [(i, i ^ 1) for i in range(8)]).astype(wide)  8.53 us
  transfers between devices with their start and end apart: 32, of which 20 were waited for; matrix products, arithmetic and copies ran while one was open for 4% of the time, Pallas kernels for 13%

profile of v4, /device:TPU:24, one launch (start us, length us, event | category | flops | bytes accessed | tf_op | source)
XLA Modules:
  0.0 183.8 jit_solution(9237931823800539883)
XLA Ops:
  7.2 0.8 fusion.9
  8.1 0.8 collective-permute-start
  8.9 3.9 %collective-permute-done = bf16[192,256]{1,0:T(8,128)(2,1)S(1)} collective-permute-done((bf16[192,256]{1,0:T(8,128)(2,1)S(1)}, bf16[192,256]{1,0:T(8,128)(2,1)S(1)}, u32[]{:S(2)}, u32[]{:S(2)}) %collective-permute-start) | collective-permute-done | bytes 98336 | tf_op jit(solution)/shard_map/ppermute | solution.py:28
  12.8 2.8 %collective-permute-start.14 = (bf16[2,112,256]{2,1,0:T(8,128)(2,1)S(1)}, bf16[2,112,256]{2,1,0:T(8,128)(2,1)S(1)}, u32[]{:S(2)}, u32[]{:S(2)}) collective-permute-start(bf16[2,112,256]{2,1,0:T(8,128)(2,1)S(1)} %pad_maximum_fusion.2), channel_id=1, source_target_pairs={{0,24},{8,0},{16,8},{24,16},{1,25},{9,1},{17,9},{25,17},{2,26},{10... | collective-permute-start | bytes 344072 | tf_op jit(solution)/shard_map/ppermute | solution.py:28
  15.7 0.8 collective-permute-start.13
  16.5 0.9 collective-permute-start.12
  17.3 2.3 %collective-permute-done.14 = bf16[2,112,256]{2,1,0:T(8,128)(2,1)S(1)} collective-permute-done((bf16[2,112,256]{2,1,0:T(8,128)(2,1)S(1)}, bf16[2,112,256]{2,1,0:T(8,128)(2,1)S(1)}, u32[]{:S(2)}, u32[]{:S(2)}) %collective-permute-start.14) | collective-permute-done | bytes 114720 | tf_op jit(solution)/shard_map/ppermute | solution.py:28
  19.7 2.4 %collective-permute-done.13 = bf16[2,112,256]{2,1,0:T(8,128)(2,1)S(1)} collective-permute-done((bf16[2,112,256]{2,1,0:T(8,128)(2,1)S(1)}, bf16[2,112,256]{2,1,0:T(8,128)(2,1)S(1)}, u32[]{:S(2)}, u32[]{:S(2)}) %collective-permute-start.13) | collective-permute-done | bytes 114720 | tf_op jit(solution)/shard_map/ppermute | solution.py:28
  22.0 1.2 collective-permute-done.12
  23.2 0.8 pad_maximum_fusion
  24.1 2.0 %collective-permute-start.1 = (bf16[2,80,256]{2,1,0:T(8,128)(2,1)S(1)}, bf16[2,80,256]{2,1,0:T(8,128)(2,1)S(1)}, u32[]{:S(2)}, u32[]{:S(2)}) collective-permute-start(bf16[2,80,256]{2,1,0:T(8,128)(2,1)S(1)} %slice.68), channel_id=1, source_target_pairs={{0,1},{1,2},{2,3},{3,4},{4,5},{5,6},{6,7},{7,0},{8,9},{9,10},{10,1... | collective-permute-start | bytes 245768 | tf_op jit(solution)/shard_map/ppermute | solution.py:28
  26.1 4.0 %collective-permute-start.2 = (bf16[2,80,256]{2,1,0:T(8,128)(2,1)S(1)}, bf16[2,80,256]{2,1,0:T(8,128)(2,1)S(1)}, u32[]{:S(2)}, u32[]{:S(2)}) collective-permute-start(bf16[2,80,256]{2,1,0:T(8,128)(2,1)S(1)} %slice.68), channel_id=1, source_target_pairs={{0,7},{1,0},{2,1},{3,2},{4,3},{5,4},{6,5},{7,6},{8,15},{9,8},{10,9... | collective-permute-start | bytes 245768 | tf_op jit(solution)/shard_map/ppermute | solution.py:28
  30.2 2.3 %collective-permute-done.1 = bf16[2,80,256]{2,1,0:T(8,128)(2,1)S(1)} collective-permute-done((bf16[2,80,256]{2,1,0:T(8,128)(2,1)S(1)}, bf16[2,80,256]{2,1,0:T(8,128)(2,1)S(1)}, u32[]{:S(2)}, u32[]{:S(2)}) %collective-permute-start.1) | collective-permute-done | bytes 81952 | tf_op jit(solution)/shard_map/ppermute | solution.py:28
  32.5 3.4 %collective-permute-start.4 = (bf16[2,80,256]{2,1,0:T(8,128)(2,1)S(1)}, bf16[2,80,256]{2,1,0:T(8,128)(2,1)S(1)}, u32[]{:S(2)}, u32[]{:S(2)}) collective-permute-start(bf16[2,80,256]{2,1,0:T(8,128)(2,1)S(1)} %collective-permute-done.2), channel_id=1, source_target_pairs={{0,7},{1,0},{2,1},{3,2},{4,3},{5,4},{6,5},{7,6},{8,15},{9,8},{10,9... | collective-permute-start | bytes 245768 | tf_op jit(solution)/shard_map/ppermute | solution.py:28
  36.0 3.0 %collective-permute-done.3 = bf16[2,80,256]{2,1,0:T(8,128)(2,1)S(1)} collective-permute-done((bf16[2,80,256]{2,1,0:T(8,128)(2,1)S(1)}, bf16[2,80,256]{2,1,0:T(8,128)(2,1)S(1)}, u32[]{:S(2)}, u32[]{:S(2)}) %collective-permute-start.3) | collective-permute-done | bytes 81952 | tf_op jit(solution)/shard_map/ppermute | solution.py:28
  38.9 1.1 collective-permute-done.4
  40.0 3.7 %collective-permute-start.6 = (bf16[2,80,256]{2,1,0:T(8,128)(2,1)S(1)}, bf16[2,80,256]{2,1,0:T(8,128)(2,1)S(1)}, u32[]{:S(2)}, u32[]{:S(2)}) collective-permute-start(bf16[2,80,256]{2,1,0:T(8,128)(2,1)S(1)} %collective-permute-done.4), channel_id=1, source_target_pairs={{0,7},{1,0},{2,1},{3,2},{4,3},{5,4},{6,5},{7,6},{8,15},{9,8},{10,9... | collective-permute-start | bytes 245768 | tf_op jit(solution)/shard_map/ppermute | solution.py:28
  43.7 2.6 %collective-permute-done.5 = bf16[2,80,256]{2,1,0:T(8,128)(2,1)S(1)} collective-permute-done((bf16[2,80,256]{2,1,0:T(8,128)(2,1)S(1)}, bf16[2,80,256]{2,1,0:T(8,128)(2,1)S(1)}, u32[]{:S(2)}, u32[]{:S(2)}) %collective-permute-start.5) | collective-permute-done | bytes 81952 | tf_op jit(solution)/shard_map/ppermute | solution.py:28
  46.4 1.2 collective-permute-done.6
  47.5 3.7 %collective-permute-start.8 = (bf16[2,48,256]{2,1,0:T(8,128)(2,1)S(1)}, bf16[2,48,256]{2,1,0:T(8,128)(2,1)S(1)}, u32[]{:S(2)}, u32[]{:S(2)}) collective-permute-start(bf16[2,48,256]{2,1,0:T(8,128)(2,1)S(1)} %slice.70), channel_id=1, source_target_pairs={{0,7},{1,0},{2,1},{3,2},{4,3},{5,4},{6,5},{7,6},{8,15},{9,8},{10,9... | collective-permute-start | bytes 147464 | tf_op jit(solution)/shard_map/ppermute | solution.py:28
  51.3 0.9 collective-permute-done.7
  52.1 1.7 collective-permute-done.8
  53.9 0.1 collective-permute-start.11
  54.0 0.1 collective-permute-start.10
  54.1 1.9 %collective-permute-start.9 = (bf16[2,8,80,256]{3,2,1,0:T(8,128)(2,1)S(1)}, bf16[2,8,80,256]{3,2,1,0:T(8,128)(2,1)S(1)}, u32[]{:S(2)}, u32[]{:S(2)}) collective-permute-start(bf16[2,8,80,256]{3,2,1,0:T(8,128)(2,1)S(1)} %fusion.8.p0), channel_id=1, source_target_pairs={{0,8},{8,16},{16,24},{24,0},{1,9},{9,17},{17,25},{25,1},{2,10},{10... | collective-permute-start | bytes 1966088 | tf_op jit(solution)/shard_map/ppermute | solution.py:28
  56.0 3.2 %convert_reduce_fusion = f32[384]{0:T(512)S(1)} fusion(bf16[6144,384]{1,0:T(8,128)(2,1)} %w_in.1), kind=kLoop, calls=%fused_computation | loop fusion | flops 4718208 | bytes 4720128 | tf_op jit(solution)/shard_map/reduce_sum | solution.py:328
  59.2 0.6 broadcast_in_dim.39.col_sum
  59.8 0.6 stack.37.me.refs_0_
  60.4 8.8 %collective-permute-done.11.p3 = bf16[2,8,80,256]{3,2,1,0:T(8,128)(2,1)S(1)} collective-permute-done((bf16[2,8,80,256]{3,2,1,0:T(8,128)(2,1)S(1)}, bf16[2,8,80,256]{3,2,1,0:T(8,128)(2,1)S(1)}, u32[]{:S(2)}, u32[]{:S(2)}) %collective-permute-start.11) | collective-permute-done | bytes 655392 | tf_op jit(solution)/shard_map/ppermute | solution.py:28
  69.3 1.7 collective-permute-done.10.p2
  71.0 6.9 %collective-permute-done.9.p1 = bf16[2,8,80,256]{3,2,1,0:T(8,128)(2,1)S(1)} collective-permute-done((bf16[2,8,80,256]{3,2,1,0:T(8,128)(2,1)S(1)}, bf16[2,8,80,256]{3,2,1,0:T(8,128)(2,1)S(1)}, u32[]{:S(2)}, u32[]{:S(2)}) %collective-permute-start.9) | collective-permute-done | bytes 655392 | tf_op jit(solution)/shard_map/ppermute | solution.py:28
  77.9 0.8 copy-done.7
  78.7 18.1 %shard_map.75 = (bf16[2,8,80,256]{3,2,1,0:T(8,128)(2,1)}, bf16[2,8,80,256]{3,2,1,0:T(8,128)(2,1)}, bf16[2,8,80,256]{3,2,1,0:T(8,128)(2,1)}, bf16[2,8,80,256]{3,2...) custom-call(s32[5]{0:T(128)} %stack.37.me.refs_0_, ...), custom_call_target="tpu_custom_call" | custom-call | flops 7247757312 | bytes 32505856 | tf_op jit(solution)/shard_map/pallas_call | solution.py:335
  96.8 9.4 %shard_map.76 = (bf16[3072,384]{1,0:T(8,128)(2,1)}, bf16[3072,384]{1,0:T(8,128)(2,1)}, bf16[3072,384]{1,0:T(8,128)(2,1)}, bf16[3072,384]{1,0:T(8,128)(2,1)}) custom-call(s32[5]{0:T(128)} %stack.37.me.refs_0_, bf16[8,4,2,112,256]{4,3,2,1,0:T(8,128)(2,1)} %bitcast.87, bf16[8,768,256]{2,1,0:T(8,128)(2,1)} %get-tuple-element.27.norm_in, ...), custom_call_target="tpu_custom_call" | custom-call | flops 2415919104 | bytes 16777216 | tf_op jit(solution)/shard_map/pallas_call | solution.py:360
  106.2 0.1 collective-permute-start.21
  106.3 0.5 collective-permute-start.22
  106.8 2.8 %collective-permute-start.19 = (bf16[2,8,80,256]{3,2,1,0:T(8,128)(2,1)}, bf16[2,8,80,256]{3,2,1,0:T(8,128)(2,1)S(1)}, u32[]{:S(2)}, u32[]{:S(2)}) collective-permute-start(bf16[2,8,80,256]{3,2,1,0:T(8,128)(2,1)} %get-tuple-element.25), channel_id=1, source_target_pairs={{0,16},{8,24},{16,0},{24,8},{1,17},{9,25},{17,1},{25,9},{2,18},{10... | collective-permute-start | bytes 1966088 | tf_op jit(solution)/shard_map/ppermute | solution.py:28
  109.6 0.5 collective-permute-start.20
  110.0 1.1 collective-permute-done.21.refs_1_
  111.2 2.7 %shard_map.78 = bf16[768,384]{1,0:T(8,128)(2,1)} custom-call(s32[5]{0:T(128)} %stack.37.me.refs_0_, bf16[3072,384]{1,0:T(8,128)(2,1)} %get-tuple-element.30.refs_0_, bf16[3072,384]{1,0:T(8,128)(2,1)} %collective-permute-done.21.refs_1_), custom_call_target="tpu_custom_call" | custom-call | tf_op jit(solution)/shard_map/pallas_call | solution.py:274
  113.9 1.5 collective-permute-start.23
  115.4 6.4 %shard_map.77 = (bf16[2304,384]{1,0:T(8,128)(2,1)}, bf16[3072,384]{1,0:T(8,128)(2,1)}) custom-call(s32[5]{0:T(128)} %stack.37.me.refs_0_, bf16[3072,384]{1,0:T(8,128)(2,1)} %get-tuple-element.30.refs_0_, bf16[3072,384]{1,0:T(8,128)(2,1)} %collective-permute-done.21.refs_1_, bf16[3072,384]{1,0:T(8,128)(2,1)} %get-tuple-element.32.refs_2_, ...), custom_call_target="tpu_custom_call" | custom-call | tf_op jit(solution)/shard_map/pallas_call | solution.py:274
  121.8 2.5 %collective-permute-start.29 = (bf16[2304,384]{1,0:T(8,128)(2,1)}, bf16[2304,384]{1,0:T(8,128)(2,1)}, u32[]{:S(2)}, u32[]{:S(2)}) collective-permute-start(bf16[2304,384]{1,0:T(8,128)(2,1)} %get-tuple-element.37), channel_id=1, source_target_pairs={{0,128},{128,0},{1,129},{129,1},{2,130},{130,2},{3,131},{131,3},{4... | collective-permute-start | bytes 5308424 | tf_op jit(solution)/shard_map/ppermute | solution.py:28
  124.3 0.7 slice.58.refs_5_
  125.0 14.0 %collective-permute-done.18.refs_2_ = bf16[2,8,80,256]{3,2,1,0:T(8,128)(2,1)S(1)} collective-permute-done((bf16[2,8,80,256]{3,2,1,0:T(8,128)(2,1)}, bf16[2,8,80,256]{3,2,1,0:T(8,128)(2,1)S(1)}, u32[]{:S(2)}, u32[]{:S(2)}) %collective-permute-start.18) | collective-permute-done | bytes 655392 | tf_op jit(solution)/shard_map/ppermute | solution.py:28
  139.0 0.6 collective-permute-done.20.refs_4_
  139.6 1.3 copy-done.2
  140.9 1.2 shard_map.79
  142.2 0.3 collective-permute-start.24
  142.5 8.5 %collective-permute-done.24 = bf16[4,2,80,256]{3,2,1,0:T(8,128)(2,1)S(1)} collective-permute-done((bf16[4,2,80,256]{3,2,1,0:T(8,128)(2,1)S(1)}, bf16[4,2,80,256]{3,2,1,0:T(8,128)(2,1)S(1)}, u32[]{:S(2)}, u32[]{:S(2)}) %collective-permute-start.24) | collective-permute-done | bytes 327712 | tf_op jit(solution)/shard_map/ppermute | solution.py:412
  151.0 0.1 fusion.10
  151.1 3.8 %collective-permute-start.25 = (bf16[2,80,256]{2,1,0:T(8,128)(2,1)S(1)}, bf16[2,80,256]{2,1,0:T(8,128)(2,1)S(1)}, u32[]{:S(2)}, u32[]{:S(2)}) collective-permute-start(bf16[2,80,256]{2,1,0:T(8,128)(2,1)S(1)} %get-tuple-element.45), channel_id=1, source_target_pairs={{0,2},{1,3},{2,4},{3,5},{4,6},{5,7},{6,0},{7,1},{8,10},{9,11},{10,... | collective-permute-start | bytes 245768 | tf_op jit(solution)/shard_map/ppermute | solution.py:28
  154.9 0.4 collective-permute-start.27
  155.3 3.9 %collective-permute-start.26 = (bf16[2,80,256]{2,1,0:T(8,128)(2,1)S(1)}, bf16[2,80,256]{2,1,0:T(8,128)(2,1)S(1)}, u32[]{:S(2)}, u32[]{:S(2)}) collective-permute-start(bf16[2,80,256]{2,1,0:T(8,128)(2,1)S(1)} %get-tuple-element.47), channel_id=1, source_target_pairs={{0,4},{1,5},{2,6},{3,7},{4,0},{5,1},{6,2},{7,3},{8,12},{9,13},{10,... | collective-permute-start | bytes 245768 | tf_op jit(solution)/shard_map/ppermute | solution.py:28
  159.3 1.0 dynamic-slice_bitcast_fusion.2
  160.3 1.5 collective-permute-start.15
  161.9 1.8 collective-permute-start.17
  163.6 1.8 collective-permute-start.16
  165.4 2.1 %collective-permute-done.15 = bf16[2,112,256]{2,1,0:T(8,128)(2,1)S(1)} collective-permute-done((bf16[2,112,256]{2,1,0:T(8,128)(2,1)S(1)}, bf16[2,112,256]{2,1,0:T(8,128)(2,1)S(1)}, u32[]{:S(2)}, u32[]{:S(2)}) %collective-permute-start.15) | collective-permute-done | bytes 114720 | tf_op jit(solution)/shard_map/ppermute | solution.py:28
  167.6 2.3 %collective-permute-done.16 = bf16[2,112,256]{2,1,0:T(8,128)(2,1)S(1)} collective-permute-done((bf16[2,112,256]{2,1,0:T(8,128)(2,1)S(1)}, bf16[2,112,256]{2,1,0:T(8,128)(2,1)S(1)}, u32[]{:S(2)}, u32[]{:S(2)}) %collective-permute-start.16) | collective-permute-done | bytes 114720 | tf_op jit(solution)/shard_map/ppermute | solution.py:28
  169.9 1.0 fusion.1
  170.9 0.9 collective-permute-start.28
  171.8 4.4 %shard_map.80 = (bf16[1536,384]{1,0:T(8,128)(2,1)}, bf16[384,1536]{1,0:T(8,128)(2,1)}) custom-call(s32[5]{0:T(128)} %stack.37.me.refs_0_, bf16[3072,384]{1,0:T(8,128)(2,1)} %get-tuple-element.34.refs_0_, bf16[768,384]{1,0:T(8,128)(2,1)} %copy-done, bf16[2304,384]{1,0:T(8,128)(2,1)} %collective-permute-done.29.refs_2_), custom_call_target="tpu_custom_call" | custom-call | tf_op jit(solution)/shard_map/pallas_call | solution.py:274
  176.3 0.6 slice_bitcast_fusion.4
  (56 shorter events, 0.5 us)
Async XLA Ops:
  7.2 70.7 %all-gather.2.cloned.1.call-start = ((), (), s32[]{:S(2)}) async-start(), calls=%async_computation.1 | async-start | bytes 4128768 | tf_op jit(solution)/shard_map/all_gather | solution.py:324
  8.1 4.7 %collective-permute-start = (bf16[192,256]{1,0:T(8,128)(2,1)S(1)}, bf16[192,256]{1,0:T(8,128)(2,1)S(1)}, u32[]{:S(2)}, u32[]{:S(2)}) collective-permute-start(bf16[192,256]{1,0:T(8,128)(2,1)S(1)} %get-tuple-element.49), channel_id=1, source_target_pairs={{0,32},{32,0},{1,33},{33,1},{2,34},{34,2},{3,35},{35,3},{4,36},{36... | collective-permute-start | bytes 294920 | tf_op jit(solution)/shard_map/ppermute | solution.py:28
  12.8 6.8 %collective-permute-start.14 = (bf16[2,112,256]{2,1,0:T(8,128)(2,1)S(1)}, bf16[2,112,256]{2,1,0:T(8,128)(2,1)S(1)}, u32[]{:S(2)}, u32[]{:S(2)}) collective-permute-start(bf16[2,112,256]{2,1,0:T(8,128)(2,1)S(1)} %pad_maximum_fusion.2), channel_id=1, source_target_pairs={{0,24},{8,0},{16,8},{24,16},{1,25},{9,1},{17,9},{25,17},{2,26},{10... | collective-permute-start | bytes 344072 | tf_op jit(solution)/shard_map/ppermute | solution.py:28
  15.7 6.4 %collective-permute-start.13 = (bf16[2,112,256]{2,1,0:T(8,128)(2,1)S(1)}, bf16[2,112,256]{2,1,0:T(8,128)(2,1)S(1)}, u32[]{:S(2)}, u32[]{:S(2)}) collective-permute-start(bf16[2,112,256]{2,1,0:T(8,128)(2,1)S(1)} %pad_maximum_fusion.2), channel_id=1, source_target_pairs={{0,16},{8,24},{16,0},{24,8},{1,17},{9,25},{17,1},{25,9},{2,18},{10... | collective-permute-start | bytes 344072 | tf_op jit(solution)/shard_map/ppermute | solution.py:28
  16.5 6.7 %collective-permute-start.12 = (bf16[2,112,256]{2,1,0:T(8,128)(2,1)S(1)}, bf16[2,112,256]{2,1,0:T(8,128)(2,1)S(1)}, u32[]{:S(2)}, u32[]{:S(2)}) collective-permute-start(bf16[2,112,256]{2,1,0:T(8,128)(2,1)S(1)} %pad_maximum_fusion.2), channel_id=1, source_target_pairs={{0,8},{8,16},{16,24},{24,0},{1,9},{9,17},{17,25},{25,1},{2,10},{10... | collective-permute-start | bytes 344072 | tf_op jit(solution)/shard_map/ppermute | solution.py:28
  24.1 135.2 %reduce-scatter.2.cloned.1.call-start = ((), (), s32[]{:S(2)}) async-start(), calls=%async_computation.2 | async-start | bytes 4128768 | tf_op jit(solution)/shard_map/reduce_scatter | solution.py:417
  24.1 8.4 %collective-permute-start.1 = (bf16[2,80,256]{2,1,0:T(8,128)(2,1)S(1)}, bf16[2,80,256]{2,1,0:T(8,128)(2,1)S(1)}, u32[]{:S(2)}, u32[]{:S(2)}) collective-permute-start(bf16[2,80,256]{2,1,0:T(8,128)(2,1)S(1)} %slice.68), channel_id=1, source_target_pairs={{0,1},{1,2},{2,3},{3,4},{4,5},{5,6},{6,7},{7,0},{8,9},{9,10},{10,1... | collective-permute-start | bytes 245768 | tf_op jit(solution)/shard_map/ppermute | solution.py:28
  26.1 6.4 %collective-permute-start.2 = (bf16[2,80,256]{2,1,0:T(8,128)(2,1)S(1)}, bf16[2,80,256]{2,1,0:T(8,128)(2,1)S(1)}, u32[]{:S(2)}, u32[]{:S(2)}) collective-permute-start(bf16[2,80,256]{2,1,0:T(8,128)(2,1)S(1)} %slice.68), channel_id=1, source_target_pairs={{0,7},{1,0},{2,1},{3,2},{4,3},{5,4},{6,5},{7,6},{8,15},{9,8},{10,9... | collective-permute-start | bytes 245768 | tf_op jit(solution)/shard_map/ppermute | solution.py:28
  32.5 6.4 %collective-permute-start.3 = (bf16[2,80,256]{2,1,0:T(8,128)(2,1)S(1)}, bf16[2,80,256]{2,1,0:T(8,128)(2,1)S(1)}, u32[]{:S(2)}, u32[]{:S(2)}) collective-permute-start(bf16[2,80,256]{2,1,0:T(8,128)(2,1)S(1)} %collective-permute-done.1), channel_id=1, source_target_pairs={{0,1},{1,2},{2,3},{3,4},{4,5},{5,6},{6,7},{7,0},{8,9},{9,10},{10,1... | collective-permute-start | bytes 245768 | tf_op jit(solution)/shard_map/ppermute | solution.py:28
  32.5 7.5 %collective-permute-start.4 = (bf16[2,80,256]{2,1,0:T(8,128)(2,1)S(1)}, bf16[2,80,256]{2,1,0:T(8,128)(2,1)S(1)}, u32[]{:S(2)}, u32[]{:S(2)}) collective-permute-start(bf16[2,80,256]{2,1,0:T(8,128)(2,1)S(1)} %collective-permute-done.2), channel_id=1, source_target_pairs={{0,7},{1,0},{2,1},{3,2},{4,3},{5,4},{6,5},{7,6},{8,15},{9,8},{10,9... | collective-permute-start | bytes 245768 | tf_op jit(solution)/shard_map/ppermute | solution.py:28
  38.9 7.4 %collective-permute-start.5 = (bf16[2,80,256]{2,1,0:T(8,128)(2,1)S(1)}, bf16[2,80,256]{2,1,0:T(8,128)(2,1)S(1)}, u32[]{:S(2)}, u32[]{:S(2)}) collective-permute-start(bf16[2,80,256]{2,1,0:T(8,128)(2,1)S(1)} %collective-permute-done.3), channel_id=1, source_target_pairs={{0,1},{1,2},{2,3},{3,4},{4,5},{5,6},{6,7},{7,0},{8,9},{9,10},{10,1... | collective-permute-start | bytes 245768 | tf_op jit(solution)/shard_map/ppermute | solution.py:28
  40.0 7.5 %collective-permute-start.6 = (bf16[2,80,256]{2,1,0:T(8,128)(2,1)S(1)}, bf16[2,80,256]{2,1,0:T(8,128)(2,1)S(1)}, u32[]{:S(2)}, u32[]{:S(2)}) collective-permute-start(bf16[2,80,256]{2,1,0:T(8,128)(2,1)S(1)} %collective-permute-done.4), channel_id=1, source_target_pairs={{0,7},{1,0},{2,1},{3,2},{4,3},{5,4},{6,5},{7,6},{8,15},{9,8},{10,9... | collective-permute-start | bytes 245768 | tf_op jit(solution)/shard_map/ppermute | solution.py:28
  46.4 5.8 %collective-permute-start.7 = (bf16[2,32,256]{2,1,0:T(8,128)(2,1)S(1)}, bf16[2,32,256]{2,1,0:T(8,128)(2,1)S(1)}, u32[]{:S(2)}, u32[]{:S(2)}) collective-permute-start(bf16[2,32,256]{2,1,0:T(8,128)(2,1)S(1)} %slice.69), channel_id=1, source_target_pairs={{0,1},{1,2},{2,3},{3,4},{4,5},{5,6},{6,7},{7,0},{8,9},{9,10},{10,1... | collective-permute-start | bytes 98312 | tf_op jit(solution)/shard_map/ppermute | solution.py:28
  47.5 6.3 %collective-permute-start.8 = (bf16[2,48,256]{2,1,0:T(8,128)(2,1)S(1)}, bf16[2,48,256]{2,1,0:T(8,128)(2,1)S(1)}, u32[]{:S(2)}, u32[]{:S(2)}) collective-permute-start(bf16[2,48,256]{2,1,0:T(8,128)(2,1)S(1)} %slice.70), channel_id=1, source_target_pairs={{0,7},{1,0},{2,1},{3,2},{4,3},{5,4},{6,5},{7,6},{8,15},{9,8},{10,9... | collective-permute-start | bytes 147464 | tf_op jit(solution)/shard_map/ppermute | solution.py:28
  53.9 5.3 %copy-start.3 = (bf16[2,8,80,256]{3,2,1,0:T(8,128)(2,1)}, bf16[2,8,80,256]{3,2,1,0:T(8,128)(2,1)S(1)}, u32[]{:S(2)}) copy-start(bf16[2,8,80,256]{3,2,1,0:T(8,128)(2,1)S(1)} %fusion.8.p0) | copy-start | bytes 1966084
  53.9 15.4 %collective-permute-start.11 = (bf16[2,8,80,256]{3,2,1,0:T(8,128)(2,1)S(1)}, bf16[2,8,80,256]{3,2,1,0:T(8,128)(2,1)S(1)}, u32[]{:S(2)}, u32[]{:S(2)}) collective-permute-start(bf16[2,8,80,256]{3,2,1,0:T(8,128)(2,1)S(1)} %fusion.8.p0), channel_id=1, source_target_pairs={{0,24},{8,0},{16,8},{24,16},{1,25},{9,1},{17,9},{25,17},{2,26},{10... | collective-permute-start | bytes 1966088 | tf_op jit(solution)/shard_map/ppermute | solution.py:28
  54.0 17.0 %collective-permute-start.10 = (bf16[2,8,80,256]{3,2,1,0:T(8,128)(2,1)S(1)}, bf16[2,8,80,256]{3,2,1,0:T(8,128)(2,1)S(1)}, u32[]{:S(2)}, u32[]{:S(2)}) collective-permute-start(bf16[2,8,80,256]{3,2,1,0:T(8,128)(2,1)S(1)} %fusion.8.p0), channel_id=1, source_target_pairs={{0,16},{8,24},{16,0},{24,8},{1,17},{9,25},{17,1},{25,9},{2,18},{10... | collective-permute-start | bytes 1966088 | tf_op jit(solution)/shard_map/ppermute | solution.py:28
  54.1 23.8 %collective-permute-start.9 = (bf16[2,8,80,256]{3,2,1,0:T(8,128)(2,1)S(1)}, bf16[2,8,80,256]{3,2,1,0:T(8,128)(2,1)S(1)}, u32[]{:S(2)}, u32[]{:S(2)}) collective-permute-start(bf16[2,8,80,256]{3,2,1,0:T(8,128)(2,1)S(1)} %fusion.8.p0), channel_id=1, source_target_pairs={{0,8},{8,16},{16,24},{24,0},{1,9},{9,17},{17,25},{25,1},{2,10},{10... | collective-permute-start | bytes 1966088 | tf_op jit(solution)/shard_map/ppermute | solution.py:28
  69.3 8.6 %copy-start.5 = (bf16[2,8,80,256]{3,2,1,0:T(8,128)(2,1)}, bf16[2,8,80,256]{3,2,1,0:T(8,128)(2,1)S(1)}, u32[]{:S(2)}) copy-start(bf16[2,8,80,256]{3,2,1,0:T(8,128)(2,1)S(1)} %collective-permute-done.11.p3) | copy-start | bytes 1966084
  71.0 6.9 %copy-start.6 = (bf16[2,8,80,256]{3,2,1,0:T(8,128)(2,1)}, bf16[2,8,80,256]{3,2,1,0:T(8,128)(2,1)S(1)}, u32[]{:S(2)}) copy-start(bf16[2,8,80,256]{3,2,1,0:T(8,128)(2,1)S(1)} %collective-permute-done.10.p2) | copy-start | bytes 1966084
  77.9 0.8 copy-start.7
  96.8 12.7 %copy-start.4 = (bf16[2,8,80,256]{3,2,1,0:T(8,128)(2,1)S(1)}, bf16[2,8,80,256]{3,2,1,0:T(8,128)(2,1)}, u32[]{:S(2)}) copy-start(bf16[2,8,80,256]{3,2,1,0:T(8,128)(2,1)} %get-tuple-element.26) | copy-start | bytes 1966084
  106.2 5.0 %collective-permute-start.21 = (bf16[3072,384]{1,0:T(8,128)(2,1)}, bf16[3072,384]{1,0:T(8,128)(2,1)}, u32[]{:S(2)}, u32[]{:S(2)}) collective-permute-start(bf16[3072,384]{1,0:T(8,128)(2,1)} %get-tuple-element.31), channel_id=1, source_target_pairs={{0,64},{64,0},{1,65},{65,1},{2,66},{66,2},{3,67},{67,3},{4,68},{68... | collective-permute-start | bytes 7077896 | tf_op jit(solution)/shard_map/ppermute | solution.py:28
  106.3 9.1 %collective-permute-start.22 = (bf16[3072,384]{1,0:T(8,128)(2,1)}, bf16[3072,384]{1,0:T(8,128)(2,1)}, u32[]{:S(2)}, u32[]{:S(2)}) collective-permute-start(bf16[3072,384]{1,0:T(8,128)(2,1)} %get-tuple-element.33), channel_id=1, source_target_pairs={{0,64},{64,0},{1,65},{65,1},{2,66},{66,2},{3,67},{67,3},{4,68},{68... | collective-permute-start | bytes 7077896 | tf_op jit(solution)/shard_map/ppermute | solution.py:28
  106.8 32.2 %collective-permute-start.18 = (bf16[2,8,80,256]{3,2,1,0:T(8,128)(2,1)}, bf16[2,8,80,256]{3,2,1,0:T(8,128)(2,1)S(1)}, u32[]{:S(2)}, u32[]{:S(2)}) collective-permute-start(bf16[2,8,80,256]{3,2,1,0:T(8,128)(2,1)} %get-tuple-element.24), channel_id=1, source_target_pairs={{0,8},{8,16},{16,24},{24,0},{1,9},{9,17},{17,25},{25,1},{2,10},{10... | collective-permute-start | bytes 1966088 | tf_op jit(solution)/shard_map/ppermute | solution.py:28
  106.8 32.2 %collective-permute-start.19 = (bf16[2,8,80,256]{3,2,1,0:T(8,128)(2,1)}, bf16[2,8,80,256]{3,2,1,0:T(8,128)(2,1)S(1)}, u32[]{:S(2)}, u32[]{:S(2)}) collective-permute-start(bf16[2,8,80,256]{3,2,1,0:T(8,128)(2,1)} %get-tuple-element.25), channel_id=1, source_target_pairs={{0,16},{8,24},{16,0},{24,8},{1,17},{9,25},{17,1},{25,9},{2,18},{10... | collective-permute-start | bytes 1966088 | tf_op jit(solution)/shard_map/ppermute | solution.py:28
  109.6 30.1 %collective-permute-start.20 = (bf16[2,8,80,256]{3,2,1,0:T(8,128)(2,1)S(1)}, bf16[2,8,80,256]{3,2,1,0:T(8,128)(2,1)S(1)}, u32[]{:S(2)}, u32[]{:S(2)}) collective-permute-start(bf16[2,8,80,256]{3,2,1,0:T(8,128)(2,1)S(1)} %copy-done.4), channel_id=1, source_target_pairs={{0,24},{8,0},{16,8},{24,16},{1,25},{9,1},{17,9},{25,17},{2,26},{10... | collective-permute-start | bytes 1966088 | tf_op jit(solution)/shard_map/ppermute | solution.py:28
  113.9 25.7 %collective-permute-start.23 = (bf16[768,384]{1,0:T(8,128)(2,1)}, bf16[768,384]{1,0:T(8,128)(2,1)S(1)}, u32[]{:S(2)}, u32[]{:S(2)}) collective-permute-start(bf16[768,384]{1,0:T(8,128)(2,1)} %shard_map.78), channel_id=1, source_target_pairs={{0,128},{128,0},{1,129},{129,1},{2,130},{130,2},{3,131},{131,3},{4... | collective-permute-start | bytes 1769480 | tf_op jit(solution)/shard_map/ppermute | solution.py:28
  115.4 24.2 %copy-start.1 = (s32[5]{0:T(128)S(1)}, s32[5]{0:T(128)}, u32[]{:S(2)}) copy-start(s32[5]{0:T(128)} %stack.37.me.refs_0_) | copy-start | bytes 64
  121.8 50.0 %collective-permute-start.29 = (bf16[2304,384]{1,0:T(8,128)(2,1)}, bf16[2304,384]{1,0:T(8,128)(2,1)}, u32[]{:S(2)}, u32[]{:S(2)}) collective-permute-start(bf16[2304,384]{1,0:T(8,128)(2,1)} %get-tuple-element.37), channel_id=1, source_target_pairs={{0,128},{128,0},{1,129},{129,1},{2,130},{130,2},{3,131},{131,3},{4... | collective-permute-start | bytes 5308424 | tf_op jit(solution)/shard_map/ppermute | solution.py:28
  139.6 11.5 %copy-start = (bf16[768,384]{1,0:T(8,128)(2,1)}, bf16[768,384]{1,0:T(8,128)(2,1)S(1)}, u32[]{:S(2)}) copy-start(bf16[768,384]{1,0:T(8,128)(2,1)S(1)} %collective-permute-done.23.refs_6_.refs_1_) | copy-start | bytes 1769476
  139.6 1.3 copy-start.2
  142.2 8.8 %collective-permute-start.24 = (bf16[4,2,80,256]{3,2,1,0:T(8,128)(2,1)S(1)}, bf16[4,2,80,256]{3,2,1,0:T(8,128)(2,1)S(1)}, u32[]{:S(2)}, u32[]{:S(2)}) collective-permute-start(bf16[4,2,80,256]{3,2,1,0:T(8,128)(2,1)S(1)} %get-tuple-element.36), channel_id=1, source_target_pairs={{0,1},{1,0},{2,3},{3,2},{4,5},{5,4},{6,7},{7,6},{8,9},{9,8},{10,11... | collective-permute-start | bytes 983048 | tf_op jit(solution)/shard_map/ppermute | solution.py:412
  151.1 10.7 %collective-permute-start.25 = (bf16[2,80,256]{2,1,0:T(8,128)(2,1)S(1)}, bf16[2,80,256]{2,1,0:T(8,128)(2,1)S(1)}, u32[]{:S(2)}, u32[]{:S(2)}) collective-permute-start(bf16[2,80,256]{2,1,0:T(8,128)(2,1)S(1)} %get-tuple-element.45), channel_id=1, source_target_pairs={{0,2},{1,3},{2,4},{3,5},{4,6},{5,7},{6,0},{7,1},{8,10},{9,11},{10,... | collective-permute-start | bytes 245768 | tf_op jit(solution)/shard_map/ppermute | solution.py:28
  154.9 8.7 %collective-permute-start.27 = (bf16[2,80,256]{2,1,0:T(8,128)(2,1)S(1)}, bf16[2,80,256]{2,1,0:T(8,128)(2,1)S(1)}, u32[]{:S(2)}, u32[]{:S(2)}) collective-permute-start(bf16[2,80,256]{2,1,0:T(8,128)(2,1)S(1)} %get-tuple-element.46), channel_id=1, source_target_pairs={{0,6},{1,7},{2,0},{3,1},{4,2},{5,3},{6,4},{7,5},{8,14},{9,15},{10,... | collective-permute-start | bytes 245768 | tf_op jit(solution)/shard_map/ppermute | solution.py:28
  155.3 10.1 %collective-permute-start.26 = (bf16[2,80,256]{2,1,0:T(8,128)(2,1)S(1)}, bf16[2,80,256]{2,1,0:T(8,128)(2,1)S(1)}, u32[]{:S(2)}, u32[]{:S(2)}) collective-permute-start(bf16[2,80,256]{2,1,0:T(8,128)(2,1)S(1)} %get-tuple-element.47), channel_id=1, source_target_pairs={{0,4},{1,5},{2,6},{3,7},{4,0},{5,1},{6,2},{7,3},{8,12},{9,13},{10,... | collective-permute-start | bytes 245768 | tf_op jit(solution)/shard_map/ppermute | solution.py:28
  160.3 7.3 %collective-permute-start.15 = (bf16[2,112,256]{2,1,0:T(8,128)(2,1)S(1)}, bf16[2,112,256]{2,1,0:T(8,128)(2,1)S(1)}, u32[]{:S(2)}, u32[]{:S(2)}) collective-permute-start(bf16[2,112,256]{2,1,0:T(8,128)(2,1)S(1)} %get-tuple-element.42), channel_id=1, source_target_pairs={{0,8},{8,16},{16,24},{24,0},{1,9},{9,17},{17,25},{25,1},{2,10},{10... | collective-permute-start | bytes 344072 | tf_op jit(solution)/shard_map/ppermute | solution.py:28
  161.9 5.7 %collective-permute-start.17 = (bf16[2,112,256]{2,1,0:T(8,128)(2,1)S(1)}, bf16[2,112,256]{2,1,0:T(8,128)(2,1)S(1)}, u32[]{:S(2)}, u32[]{:S(2)}) collective-permute-start(bf16[2,112,256]{2,1,0:T(8,128)(2,1)S(1)} %get-tuple-element.43), channel_id=1, source_target_pairs={{0,24},{8,0},{16,8},{24,16},{1,25},{9,1},{17,9},{25,17},{2,26},{10... | collective-permute-start | bytes 344072 | tf_op jit(solution)/shard_map/ppermute | solution.py:28
  163.6 6.3 %collective-permute-start.16 = (bf16[2,112,256]{2,1,0:T(8,128)(2,1)S(1)}, bf16[2,112,256]{2,1,0:T(8,128)(2,1)S(1)}, u32[]{:S(2)}, u32[]{:S(2)}) collective-permute-start(bf16[2,112,256]{2,1,0:T(8,128)(2,1)S(1)} %get-tuple-element.44), channel_id=1, source_target_pairs={{0,16},{8,24},{16,0},{24,8},{1,17},{9,25},{17,1},{25,9},{2,18},{10... | collective-permute-start | bytes 344072 | tf_op jit(solution)/shard_map/ppermute | solution.py:28
  170.9 5.3 %collective-permute-start.28 = (bf16[192,256]{1,0:T(8,128)(2,1)S(1)}, bf16[192,256]{1,0:T(8,128)(2,1)S(1)}, u32[]{:S(2)}, u32[]{:S(2)}) collective-permute-start(bf16[192,256]{1,0:T(8,128)(2,1)S(1)} %fusion.7), channel_id=1, source_target_pairs={{0,32},{32,0},{1,33},{33,1},{2,34},{34,2},{3,35},{35,3},{4,36},{36... | collective-permute-start | bytes 294920 | tf_op jit(solution)/shard_map/ppermute | solution.py:28
Sparse Core Ops, SparseCore 0:
  24.2 51.9 all-gather.1
  97.0 48.8 reduce-scatter.1
